TPU v7x, 32 devices: a whole 2x2x4 slice. The times are simulated.
32 devices in a mesh: gx: 8 (over z, core), gy: 4 (over y, x).
Axes of the slice: x: 2, y: 2, z: 4, core: 2. Of those that a mesh axis runs over, the one named last changes fastest.
Arguments:
- tokens: bfloat16 [256, 16384], P('gy', 'gx'), may hold values from -6 to 6
- gate_weight: bfloat16 [16384, 26624], P('gx', 'gy'), may hold values from -0.046875 to 0.046875
- up_weight: bfloat16 [16384, 26624], P('gx', 'gy'), may hold values from -0.046875 to 0.046875
- down_weight: bfloat16 [26624, 16384], P('gy', 'gx'), may hold values from -0.0390625 to 0.0390625
Outputs:
- mixed: float32 [256, 16384], P('gy', 'gx')
All inputs are finite; a program needn't handle non-finite values.
Results may differ from a plain program's by a relative error of at most 0.0029.
Values may be sent and summed in bfloat16 or wider, within the bound.
No kernel may reach another device: no remote copies, remote signals or barrier semaphores. Data moves between devices by JAX's collectives and lax.ppermute only.
A program may use at most 192 MiB of HBM per device.

v0:
```python
import jax
import jax.numpy as jnp
from jax import lax
from jax.sharding import PartitionSpec as P


def local(tokens, gate_weight, up_weight, down_weight):
    all_rows = lax.all_gather(tokens, "gy", axis=0, tiled=True)
    width = gate_weight.shape[1]
    rows = all_rows
    gate_part = jnp.dot(rows, gate_weight, preferred_element_type=jnp.float32)
    up_part = jnp.dot(rows, up_weight, preferred_element_type=jnp.float32)
    shares = lax.psum_scatter(
        jnp.concatenate([gate_part, up_part], axis=1), "gx", scatter_dimension=0, tiled=True
    )
    hidden_share = (jax.nn.silu(shares[:, :width]) * shares[:, width:]).astype(jnp.bfloat16)
    hidden = lax.all_gather(hidden_share, "gx", axis=0, tiled=True)
    rows = hidden
    return lax.psum_scatter(
        jnp.dot(rows, down_weight, preferred_element_type=jnp.float32),
        "gy",
        scatter_dimension=0,
        tiled=True,
    )


def solution(mesh):
    placed = (P("gy", "gx"), P("gx", "gy"), P("gx", "gy"), P("gy", "gx"))
    return jax.shard_map(
        local, mesh=mesh, in_specs=placed, out_specs=P("gy", "gx"), check_vma=False
    )
```

profile of v0, /device:TPU:17, one launch (start us, length us, event | category | flops | bytes accessed | tf_op | source)
XLA Modules:
  0.0 306.9 jit_solution(7523826354375201170)
XLA Ops:
  6.5 0.0 all-gather.3.cloned.1.call-start
  6.5 0.7 all-gather.3.cloned.1.call-update
  7.3 0.0 reduce-scatter.3.cloned.1.call-start
  7.3 29.6 %all-gather.3.cloned.1.call-done = bf16[256,2048]{1,0:T(8,128)(2,1)} async-done(((bf16[64,2048]{1,0:T(8,128)(2,1)}), bf16[256,2048]{1,0:T(8,128)(2,1)}) %all-gather.3.cloned.1.call-update) | async-done | bytes 1048592 | tf_op jit(solution)/shard_map/all_gather | solution.py:8
  36.9 0.0 copy-start
  36.9 16.4 %fusion.2 = f32[256,6656]{1,0:T(8,128)S(1)} fusion(bf16[256,2048]{1,0:T(8,128)(2,1)} %all-gather.3.cloned.1.call-done, bf16[2048,6656]{1,0:T(8,128)(2,1)} %param.6), kind=kOutput, calls=%fused_computation.4 | convolution fusion | flops 6979321856 | bytes 35127296 | tf_op jit(solution)/shard_map/dot_general | solution.py:12
  53.3 0.0 copy-done
  53.3 12.5 %fusion.1 = f32[256,6656]{1,0:T(8,128)S(1)} fusion(bf16[256,2048]{1,0:T(8,128)(2,1)S(1)} %copy-done, bf16[2048,6656]{1,0:T(8,128)(2,1)} %param.5), kind=kOutput, calls=%fused_computation.3 | convolution fusion | flops 6979321856 | bytes 35127296 | tf_op jit(solution)/shard_map/dot_general | solution.py:11
  65.8 5.3 %pad_maximum_fusion = f32[256,13312]{1,0:T(8,128)} fusion(f32[256,6656]{1,0:T(8,128)S(1)} %fusion.2, f32[256,6656]{1,0:T(8,128)S(1)} %fusion.1), kind=kLoop, calls=%fused_computation | loop fusion | flops 3407872 | bytes 27262976 | tf_op jit(solution)/shard_map/concatenate | solution.py:14
  71.0 0.0 reduce-scatter.3.cloned.1.call-update
  71.1 0.0 all-gather.5.cloned.1.call-start
  71.1 137.6 %reduce-scatter.3.cloned.1.call-done = f32[32,13312]{1,0:T(8,128)} async-done(((f32[256,13312]{1,0:T(8,128)}), f32[32,13312]{1,0:T(8,128)}) %reduce-scatter.3.cloned.1.call-update) | async-done | bytes 1703952 | tf_op jit(solution)/shard_map/reduce_scatter | solution.py:13
  208.7 2.4 fusion
  211.1 0.0 all-gather.5.cloned.1.call-update
  211.1 0.0 reduce-scatter.5.cloned.1.call-start
  211.2 39.8 %all-gather.5.cloned.1.call-done = bf16[256,6656]{1,0:T(8,128)(2,1)} async-done(((bf16[32,6656]{1,0:T(8,128)(2,1)}), bf16[256,6656]{1,0:T(8,128)(2,1)}) %all-gather.5.cloned.1.call-update) | async-done | bytes 3407888 | tf_op jit(solution)/shard_map/all_gather | solution.py:17
  251.0 14.4 %fusion.3 = f32[256,2048]{1,0:T(8,128)} fusion(bf16[256,6656]{1,0:T(8,128)(2,1)} %all-gather.5.cloned.1.call-done, bf16[6656,2048]{1,0:T(8,128)(2,1)} %param.7), kind=kOutput, calls=%fused_computation.5 | convolution fusion | flops 6979321856 | bytes 32768000 | tf_op jit(solution)/shard_map/dot_general | solution.py:20
  265.4 0.0 reduce-scatter.5.cloned.1.call-update
  265.4 34.9 %reduce-scatter.5.cloned.1.call-done = f32[64,2048]{1,0:T(8,128)} async-done(((f32[256,2048]{1,0:T(8,128)}), f32[64,2048]{1,0:T(8,128)}) %reduce-scatter.5.cloned.1.call-update) | async-done | bytes 524304 | tf_op jit(solution)/shard_map/reduce_scatter | solution.py:19
Async XLA Ops:
  6.5 30.4 %all-gather.3.cloned.1.call-start = ((), (), s32[]{:S(2)}) async-start(), calls=%async_computation.2 | async-start | bytes 1310720 | tf_op jit(solution)/shard_map/all_gather | solution.py:8
  7.3 201.5 %reduce-scatter.3.cloned.1.call-start = ((), (), s32[]{:S(2)}) async-start(), calls=%async_computation.3 | async-start | bytes 15335424 | tf_op jit(solution)/shard_map/reduce_scatter | solution.py:13
  36.9 16.4 %copy-start = (bf16[256,2048]{1,0:T(8,128)(2,1)S(1)}, bf16[256,2048]{1,0:T(8,128)(2,1)}, u32[]{:S(2)}) copy-start(bf16[256,2048]{1,0:T(8,128)(2,1)} %all-gather.3.cloned.1.call-done) | copy-start | bytes 3145732
  71.1 179.9 %all-gather.5.cloned.1.call-start = ((), (), s32[]{:S(2)}) async-start(), calls=%async_computation.4 | async-start | bytes 3833856 | tf_op jit(solution)/shard_map/all_gather | solution.py:17
  211.1 89.2 %reduce-scatter.5.cloned.1.call-start = ((), (), s32[]{:S(2)}) async-start(), calls=%async_computation.5 | async-start | bytes 2621440 | tf_op jit(solution)/shard_map/reduce_scatter | solution.py:19
Sparse Core Ops, SparseCore 0:
  9.2 27.6 all-gather.2
  71.2 137.4 reduce-scatter.2
  211.3 39.6 all-gather.4
  265.5 34.7 reduce-scatter.4
where the time goes:
time: 309 us; the launch traced here: 307 us
  waiting for transfers between devices  243 us (79%)
  matrix products  43.2 us (14%)
  between operations  13.2 us (4%)
  other arithmetic  7.66 us (2%)
    reduce_scatter x1, waiting for transfers between devices, local(): lax.psum_scatter(jnp.concatenate([gate_part, up_part], axis=1), 'gx', sca...  138 us
    all_gather x1, waiting for transfers between devices, local(): hidden = lax.all_gather(hidden_share, 'gx', axis=0, tiled=True)  39.8 us
    reduce_scatter x1, waiting for transfers between devices, local(): lax.psum_scatter(jnp.dot(rows, down_weight, preferred_element_type=jnp.fl...  34.9 us
    all_gather x1, waiting for transfers between devices, local(): all_rows = lax.all_gather(tokens, 'gy', axis=0, tiled=True)  29.6 us
    dot_general x1, matrix products, local(): up_part = jnp.dot(rows, up_weight, preferred_element_type=jnp.float32)  16.4 us
    dot_general x1, matrix products, local(): jnp.dot(rows, down_weight, preferred_element_type=jnp.float32)  14.4 us
    dot_general x1, matrix products, local(): gate_part = jnp.dot(rows, gate_weight, preferred_element_type=jnp.float32)  12.5 us
  transfers between devices with their start and end apart: 4, of which 4 were waited for; matrix products, arithmetic and copies ran while one was open for 0% of the time, Pallas kernels for 0%

commit v1 on v0

v1 whole, which is shorter than its diff:
```python
import functools
import math

import jax
import jax.numpy as jnp
from jax import lax
from jax.experimental import pallas as pl
from jax.experimental.pallas import tpu as pltpu
from jax.sharding import PartitionSpec as P

CORES = 2
TOKEN_MAX = 6.0
WEIGHT_MAX = 0.046875
VMEM = 40 * 1024 * 1024
PIECES = 2
SIZES = [3, 3, 3, 2, 2]
GAPS = [0, 1, 1, 2]


def encode(v, scale):
    root = lax.rsqrt(jnp.maximum(jnp.abs(v), 1e-37))
    return (v * root * scale).astype(jnp.float16)


def decode(q, scale):
    u = q.astype(jnp.float32)
    return u * jnp.abs(u) * (1.0 / (scale * scale))


def first(rows, gate_weight, up_weight, start, width, tile):
    count, depth = rows.shape
    half = count // 2
    steps = [(k, i) for i in range(width // tile) for k in (0, 1)]
    slots = 3
    piece = depth // PIECES

    def kernel(rows_ref, gate_ref, up_ref, theirs_ref, mine_ref, held, sems):
        def load(n):
            k, i = steps[n]
            ref = (gate_ref, up_ref)[k]
            slot = n % slots
            return [
                pltpu.make_async_copy(
                    ref.at[pl.ds(p * piece, piece), pl.ds(start + i * tile, tile)],
                    held.at[slot, pl.ds(p * piece, piece)],
                    sems.at[slot, p],
                )
                for p in range(PIECES)
            ]

        for n in range(min(slots - 1, len(steps))):
            for copy in load(n):
                copy.start()
        for n, (k, i) in enumerate(steps):
            if n + slots - 1 < len(steps):
                for copy in load(n + slots - 1):
                    copy.start()
            for copy in load(n):
                copy.wait()
            part = jnp.dot(rows_ref[...], held[n % slots], preferred_element_type=jnp.float32)
            theirs_ref[k, :, i * tile : (i + 1) * tile] = part[:half]
            mine_ref[k, :, i * tile : (i + 1) * tile] = part[half:]

    hbm = pl.BlockSpec(memory_space=pltpu.HBM)
    vmem = pl.BlockSpec(memory_space=pltpu.VMEM)
    shape = pltpu.VMEM((2, half, width), jnp.float32)
    return pl.pallas_call(
        kernel,
        in_specs=[vmem, hbm, hbm],
        out_specs=[vmem, vmem],
        out_shape=[shape, shape],
        scratch_shapes=[
            pltpu.VMEM((slots, depth, tile), jnp.bfloat16),
            pltpu.SemaphoreType.DMA((slots, PIECES)),
        ],
        compiler_params=pltpu.CompilerParams(vmem_limit_bytes=VMEM),
        cost_estimate=pl.CostEstimate(
            flops=4 * count * depth * width,
            bytes_accessed=4 * depth * width + 8 * count * width,
            transcendentals=0,
        ),
    )(rows, gate_weight, up_weight)


def second(total, parts, down_weight, start, width, tile):
    half = parts[0].shape[0]
    depth = down_weight.shape[1]
    carried = total is not None
    slots = 3
    steps = depth // tile
    piece = width // PIECES

    def kernel(*refs):
        weight_ref = refs[2]
        out_ref, rows, held, sems = refs[-4:]

        def load(n):
            return [
                pltpu.make_async_copy(
                    weight_ref.at[pl.ds(start + p * piece, piece), pl.ds(n * tile, tile)],
                    held.at[n % slots, pl.ds(p * piece, piece)],
                    sems.at[n % slots, p],
                )
                for p in range(PIECES)
            ]

        for n in range(min(slots - 1, steps)):
            for copy in load(n):
                copy.start()
        rows[:half] = refs[0][...]
        rows[half:] = refs[1][...]
        for n in range(steps):
            if n + slots - 1 < steps:
                for copy in load(n + slots - 1):
                    copy.start()
            for copy in load(n):
                copy.wait()
            part = jnp.dot(rows[...], held[n % slots], preferred_element_type=jnp.float32)
            at = slice(n * tile, (n + 1) * tile)
            if carried:
                part = part + refs[3][:, at]
            out_ref[:, at] = part

    hbm = pl.BlockSpec(memory_space=pltpu.HBM)
    vmem = pl.BlockSpec(memory_space=pltpu.VMEM)
    return pl.pallas_call(
        kernel,
        in_specs=[vmem, vmem, hbm] + ([vmem] if carried else []),
        out_specs=vmem,
        out_shape=jax.ShapeDtypeStruct((2 * half, depth), jnp.float32),
        scratch_shapes=[
            pltpu.VMEM((2 * half, width), jnp.bfloat16),
            pltpu.VMEM((slots, width, tile), jnp.bfloat16),
            pltpu.SemaphoreType.DMA((slots, PIECES)),
        ],
        compiler_params=pltpu.CompilerParams(vmem_limit_bytes=VMEM),
        cost_estimate=pl.CostEstimate(
            flops=4 * half * depth * width,
            bytes_accessed=2 * depth * width + 16 * half * depth,
            transcendentals=0,
        ),
    )(*parts, down_weight, *([total] if carried else []))


def unit_of(width):
    for unit in (512, 256, 128):
        if width % unit == 0:
            return unit
    return width


def plan(count):
    if count == sum(SIZES):
        return SIZES, GAPS
    return [1] * count, [1] * (count - 1)


def queue(steps, gaps):
    waiting, order = [], []

    def take():
        chunk, step = waiting.pop(0)
        order.append((chunk, step))
        if step + 1 < steps:
            waiting.append((chunk, step + 1))

    for chunk in range(len(gaps) + 1):
        for _ in range(gaps[chunk - 1] if chunk else 0):
            if waiting:
                take()
        order.append((chunk, 0))
        waiting.append((chunk, 1))
    while waiting:
        take()
    return order


def local(tokens, gate_weight, up_weight, down_weight, *, n_gx, n_gy):
    chips = n_gx // CORES
    own, depth = tokens.shape
    width = gate_weight.shape[1]
    x = lax.axis_index("gx")
    y = lax.axis_index("gy")
    z, core = x // CORES, x % CORES
    half = own * n_gy // CORES
    per = n_gy // CORES
    away = jnp.where(core == 0, z, chips - 1 - z)

    limit = TOKEN_MAX * WEIGHT_MAX * depth * n_gx
    scale = 2.0 ** math.floor(math.log2(60000.0 / math.sqrt(limit)))

    def swap(v):
        return lax.ppermute(v, "gx", [(i, i ^ 1) for i in range(n_gx)])

    def towards(v, step):
        return lax.ppermute(
            v,
            "gx",
            [
                ((chips - step) * CORES, (chips - step - 1) * CORES),
                ((step - 1) * CORES + 1, step * CORES + 1),
            ],
        )

    def back(v, step):
        return lax.ppermute(
            v,
            "gx",
            [
                ((step - 1) * CORES, step * CORES),
                ((chips - step) * CORES + 1, (chips - step - 1) * CORES + 1),
            ],
        )

    def across(v, shift):
        return lax.ppermute(v, "gy", [(i, i ^ shift) for i in range(n_gy)])

    blocks = jnp.stack([tokens] + [across(tokens, s) for s in range(1, n_gy)])
    rows = jnp.concatenate(
        [
            lax.dynamic_index_in_dim(blocks, (side * per + b) ^ y, 0, False)
            for side in (1 - core, core)
            for b in range(per)
        ]
    )

    unit = unit_of(width)
    tile = unit
    down_tile = min(depth, 512)
    counts, gaps = plan(width // unit)
    sizes = [n * unit for n in counts]
    starts = [sum(sizes[:c]) for c in range(len(sizes))]

    state = {}
    token = [rows]

    def tied(*values):
        return lax.optimization_barrier(values + (token[0],))[:-1]

    def matmul_in(c):
        (lhs,) = tied(rows)
        theirs, mine = first(lhs, gate_weight, up_weight, starts[c], sizes[c], tile)
        state["mine", c], state["moved", c] = mine, swap(theirs)
        token[0] = mine

    def leave(c):
        mine, got = tied(state["mine", c], state["moved", c])
        held = mine + got
        sent = encode(held, scale)
        state["held", c], state["moved", c] = held, towards(sent, 1)
        token[0] = sent

    def pass_sum(step):
        def run(c):
            held, got = tied(state["held", c], state["moved", c])
            sent = encode(held + decode(got, scale), scale)
            state["moved", c] = towards(sent, step + 1)
            token[0] = sent

        return run

    def finish(c):
        held, got = tied(state["held", c], state["moved", c])
        value = held + decode(got, scale)
        hidden = (jax.nn.silu(value[0]) * value[1]).astype(jnp.bfloat16)
        state["stage", c], state["moved", c] = [hidden], back(hidden, 1)
        token[0] = hidden

    def pass_hidden(step):
        def run(c):
            (got,) = tied(state["moved", c])
            state["stage", c].append(got)
            state["moved", c] = back(got, step + 1)
            token[0] = got

        return run

    def gather(c):
        (got,) = tied(state["moved", c])
        rows_here = got
        for step, stage in enumerate(state["stage", c]):
            rows_here = jnp.where(away == step, stage, rows_here)
        state["parts", c], state["moved", c] = rows_here, swap(rows_here)
        token[0] = rows_here

    def matmul_out(c):
        parts = tied(state["parts", c], state["moved", c])
        token[0] = state["total"] = second(
            state.get("total"), parts, down_weight, starts[c], sizes[c], down_tile
        )

    steps = [matmul_in, leave]
    steps += [pass_sum(step) for step in range(1, chips - 1)]
    steps += [finish]
    steps += [pass_hidden(step) for step in range(1, chips - 1)]
    steps += [gather, matmul_out]
    for chunk, step in queue(len(steps), gaps):
        steps[step](chunk)
    total = state["total"]

    def block_for(j):
        at = ((j // per) ^ core) * half + (j % per) * own
        return lax.dynamic_slice_in_dim(total, at, own, 0)

    result = block_for(y)
    for shift in range(1, n_gy):
        result = result + across(block_for(y ^ shift).astype(jnp.bfloat16), shift).astype(jnp.float32)
    return result


def solution(mesh):
    n_gx, n_gy = mesh.shape["gx"], mesh.shape["gy"]
    placed = (P("gy", "gx"), P("gx", "gy"), P("gx", "gy"), P("gy", "gx"))
    return jax.shard_map(
        functools.partial(local, n_gx=n_gx, n_gy=n_gy),
        mesh=mesh,
        in_specs=placed,
        out_specs=P("gy", "gx"),
        check_vma=False,
    )
```

time: 309 us -> 167 us (0.54)
  waiting for transfers between devices: 243 us -> 39.5 us
  starting transfers between devices: 0.12 us -> 59.5 us
  Pallas kernels: 0 us -> 47.3 us
  matrix products: 43.2 us -> 0 us
  between operations: 13.2 us -> 0.9 us
  other arithmetic: 7.66 us -> 18.6 us
    reduce_scatter x2 -> x0, waiting for transfers between devices: 173 us -> none  [the longest x1 138 us: local(): lax.psum_scatter(jnp.concatenate([gate_part, up_part], axis=1), 'gx', sca...]
    all_gather x2 -> x0, waiting for transfers between devices: 69.4 us -> none  [the longest x1 39.8 us: local(): hidden = lax.all_gather(hidden_share, 'gx', axis=0, tiled=True)]
    ppermute x0 -> x46, starting transfers between devices: none -> 59.5 us  [the longest x15 25.4 us: towards(): lax.ppermute(v, 'gx', [((chips - step) * CORES, (chips - step - 1) * CORE...]
    pallas_call x0 -> x10, Pallas kernels: none -> 47.3 us  [the longest x5 29.2 us: first(): pl.pallas_call(kernel, in_specs=[vmem, hbm, hbm], out_specs=[vmem, vmem],...]
    dot_general x3 -> x0, matrix products: 43.2 us -> none  [the longest x1 16.4 us: local(): up_part = jnp.dot(rows, up_weight, preferred_element_type=jnp.float32)]
    ppermute x0 -> x46, waiting for transfers between devices: none -> 39.5 us  [the longest x6 22.9 us: across(): return lax.ppermute(v, 'gy', [(i, i ^ shift) for i in range(n_gy)])]
    convert_element_type x1 -> x20, other arithmetic: 2.4 us -> 12.6 us  [the longest x15 11.6 us: encode(): return (v * root * scale).astype(jnp.float16)]
    concatenate x1, other arithmetic: 5.26 us -> 0.1 us  [local(): jnp.concatenate([lax.dynamic_index_in_dim(blocks, side * per + b ^ y, 0,...]
  transfers between devices with their start and end apart: 4 -> 46, of which waited for: 4 -> 13; matrix products, arithmetic and copies ran while one was open for 0% -> 9% of each run, Pallas kernels for 0% -> 23%
where the time goes in v1:
time: 167 us; the launch traced here: 166 us
  starting transfers between devices  59.5 us (36%)
  Pallas kernels  47.3 us (28%)
  waiting for transfers between devices  39.5 us (24%)
  other arithmetic  18.6 us (11%)
    pallas_call x5, Pallas kernels, first(): pl.pallas_call(kernel, in_specs=[vmem, hbm, hbm], out_specs=[vmem, vmem],...  29.2 us
    ppermute x15, starting transfers between devices, towards(): lax.ppermute(v, 'gx', [((chips - step) * CORES, (chips - step - 1) * CORE...  25.4 us
    ppermute x6, waiting for transfers between devices, across(): return lax.ppermute(v, 'gy', [(i, i ^ shift) for i in range(n_gy)])  22.9 us
    ppermute x15, starting transfers between devices, back(): lax.ppermute(v, 'gx', [((step - 1) * CORES, step * CORES), ((chips - step...  19.9 us
    pallas_call x5, Pallas kernels, second(): pl.pallas_call(kernel, in_specs=[vmem, vmem, hbm] + ([vmem] if carried el...  18.1 us
    ppermute x15, waiting for transfers between devices, towards(): lax.ppermute(v, 'gx', [((chips - step) * CORES, (chips - step - 1) * CORE...  13.8 us
    convert_element_type x15, other arithmetic, encode(): return (v * root * scale).astype(jnp.float16)  11.6 us
    ppermute x10, starting transfers between devices, swap(): return lax.ppermute(v, 'gx', [(i, i ^ 1) for i in range(n_gx)])  8.84 us
  transfers between devices with their start and end apart: 46, of which 13 were waited for; matrix products, arithmetic and copies ran while one was open for 9% of the time, Pallas kernels for 23%

profile of v1, /device:TPU:17, one launch (start us, length us, event | category | flops | bytes accessed | tf_op | source)
XLA Modules:
  0.0 166.0 jit_solution(6180693946937769368)
XLA Ops:
  0.0 1.2 collective-permute-start
  1.2 1.2 collective-permute-start.1
  2.6 4.7 %collective-permute-done = bf16[64,2048]{1,0:T(8,128)(2,1)S(1)} collective-permute-done((bf16[64,2048]{1,0:T(8,128)(2,1)}, bf16[64,2048]{1,0:T(8,128)(2,1)S(1)}, u32[]{:S(2)}, u32[]{:S(2)}) %collective-permute-start) | collective-permute-done | bytes 262176 | tf_op jit(solution)/shard_map/ppermute | solution.py:216
  8.3 5.7 %collective-permute-done.2 = bf16[64,2048]{1,0:T(8,128)(2,1)S(1)} collective-permute-done((bf16[64,2048]{1,0:T(8,128)(2,1)}, bf16[64,2048]{1,0:T(8,128)(2,1)S(1)}, u32[]{:S(2)}, u32[]{:S(2)}) %collective-permute-start.2) | collective-permute-done | bytes 262176 | tf_op jit(solution)/shard_map/ppermute | solution.py:216
  15.3 6.0 %shard_map.46 = (f32[2,128,1536]{2,1,0:T(8,128)S(1)}, f32[2,128,1536]{2,1,0:T(8,128)S(1)}) custom-call(bf16[256,2048]{1,0:T(8,128)(2,1)S(1)} %pad_maximum_fusion.1.rows_ref, bf16[2048,6656]{1,0:T(8,128)(2,1)} %gate_ref.9, bf16[2048,6656]{1,0:T(8,128)(2,1)} %up_ref.9), custom_call_target="tpu_custom_call" | custom-call | flops 3221225472 | bytes 15728640 | tf_op jit(solution)/shard_map/pallas_call | solution.py:67
  21.3 1.8 %collective-permute-start.3 = (f32[2,128,1536]{2,1,0:T(8,128)S(1)}, f32[2,128,1536]{2,1,0:T(8,128)S(1)}, u32[]{:S(2)}, u32[]{:S(2)}) collective-permute-start(f32[2,128,1536]{2,1,0:T(8,128)S(1)} %get-tuple-element.87), channel_id=1, source_target_pairs={{0,4},{4,0},{8,12},{12,8},{16,20},{20,16},{24,28},{28,24},{1,5},{5... | collective-permute-start | bytes 4718600 | tf_op jit(solution)/shard_map/ppermute | solution.py:193
  23.1 7.1 %shard_map.47 = (f32[2,128,1536]{2,1,0:T(8,128)}, f32[2,128,1536]{2,1,0:T(8,128)S(1)}) custom-call(bf16[256,2048]{1,0:T(8,128)(2,1)S(1)} %pad_maximum_fusion.1.rows_ref, bf16[2048,6656]{1,0:T(8,128)(2,1)} %gate_ref.9, bf16[2048,6656]{1,0:T(8,128)(2,1)} %up_ref.9), custom_call_target="tpu_custom_call" | custom-call | flops 3221225472 | bytes 15728640 | tf_op jit(solution)/shard_map/pallas_call | solution.py:67
  30.3 1.6 multiply_convert_fusion.8
  31.9 7.1 %shard_map.48 = (f32[2,128,1536]{2,1,0:T(8,128)}, f32[2,128,1536]{2,1,0:T(8,128)S(1)}) custom-call(bf16[256,2048]{1,0:T(8,128)(2,1)S(1)} %pad_maximum_fusion.1.rows_ref, bf16[2048,6656]{1,0:T(8,128)(2,1)} %gate_ref.9, bf16[2048,6656]{1,0:T(8,128)(2,1)} %up_ref.9), custom_call_target="tpu_custom_call" | custom-call | flops 3221225472 | bytes 15728640 | tf_op jit(solution)/shard_map/pallas_call | solution.py:67
  40.3 2.3 %multiply_convert_fusion.7 = (f16[2,128,1536]{2,1,0:T(8,128)(2,1)S(1)}, f32[2,128,1536]{2,1,0:T(8,128)S(1)}) fusion(f32[2,128,1536]{2,1,0:T(8,128)} %copy-done, f32[2,128,1536]{2,1,0:T(8,128)} %collective-permute-done.6), kind=kLoop, calls=%fused_computation.40 | loop fusion | flops 2359296 | bytes 5505024 | tf_op jit(solution)/shard_map/convert_element_type | solution.py:22
  43.4 4.5 %shard_map.49 = (f32[2,128,1024]{2,1,0:T(8,128)S(1)}, f32[2,128,1024]{2,1,0:T(8,128)S(1)}) custom-call(bf16[256,2048]{1,0:T(8,128)(2,1)S(1)} %pad_maximum_fusion.1.rows_ref, bf16[2048,6656]{1,0:T(8,128)(2,1)} %gate_ref.9, bf16[2048,6656]{1,0:T(8,128)(2,1)} %up_ref.9), custom_call_target="tpu_custom_call" | custom-call | flops 2147483648 | bytes 10485760 | tf_op jit(solution)/shard_map/pallas_call | solution.py:67
  48.0 1.3 collective-permute-start.10
  49.9 1.3 collective-permute-start.9
  51.2 1.8 %multiply_convert_fusion.5 = (f16[2,128,1536]{2,1,0:T(8,128)(2,1)S(1)}, f32[2,128,1536]{2,1,0:T(8,128)S(1)}) fusion(f32[2,128,1536]{2,1,0:T(8,128)S(1)} %get-tuple-element.102, f32[2,128,1536]{2,1,0:T(8,128)} %collective-permute-done.4), kind=kLoop, calls=%fused_computation.38 | loop fusion | flops 2359296 | bytes 5505024 | tf_op jit(solution)/shard_map/convert_element_type | solution.py:22
  53.9 4.5 %shard_map.50 = (f32[2,128,1024]{2,1,0:T(8,128)S(1)}, f32[2,128,1024]{2,1,0:T(8,128)S(1)}) custom-call(bf16[256,2048]{1,0:T(8,128)(2,1)S(1)} %pad_maximum_fusion.1.rows_ref, bf16[2048,6656]{1,0:T(8,128)(2,1)} %gate_ref.9, bf16[2048,6656]{1,0:T(8,128)(2,1)} %up_ref.9), custom_call_target="tpu_custom_call" | custom-call | flops 2147483648 | bytes 10485760 | tf_op jit(solution)/shard_map/pallas_call | solution.py:67
  59.0 1.3 collective-permute-start.16
  61.4 2.6 %collective-permute-done.9 = f16[2,128,1536]{2,1,0:T(8,128)(2,1)S(1)} collective-permute-done((f16[2,128,1536]{2,1,0:T(8,128)(2,1)S(1)}, f16[2,128,1536]{2,1,0:T(8,128)(2,1)S(1)}, u32[]{:S(2)}, u32[]{:S(2)}) %collective-permute-start.9) | collective-permute-done | bytes 786464 | tf_op jit(solution)/shard_map/ppermute | solution.py:196
  64.0 3.0 %collective-permute-start.7 = (f32[2,128,1024]{2,1,0:T(8,128)S(1)}, f32[2,128,1024]{2,1,0:T(8,128)S(1)}, u32[]{:S(2)}, u32[]{:S(2)}) collective-permute-start(f32[2,128,1024]{2,1,0:T(8,128)S(1)} %get-tuple-element.106), channel_id=1, source_target_pairs={{0,4},{4,0},{8,12},{12,8},{16,20},{20,16},{24,28},{28,24},{1,5},{5... | collective-permute-start | bytes 3145736 | tf_op jit(solution)/shard_map/ppermute | solution.py:193
  67.6 4.3 %collective-permute-start.14 = (f16[2,128,1536]{2,1,0:T(8,128)(2,1)S(1)}, f16[2,128,1536]{2,1,0:T(8,128)(2,1)S(1)}, u32[]{:S(2)}, u32[]{:S(2)}) collective-permute-start(f16[2,128,1536]{2,1,0:T(8,128)(2,1)S(1)} %multiply_convert_fusion.3), channel_id=1, source_target_pairs={{8,0},{20,28},{9,1},{21,29},{10,2},{22,30},{11,3},{23,31}} | collective-permute-start | bytes 2359304 | tf_op jit(solution)/shard_map/ppermute | solution.py:196
  72.5 1.3 collective-permute-start.13
  75.5 1.3 collective-permute-start.21
  77.2 1.3 collective-permute-start.20
  78.5 2.3 %collective-permute-done.14 = f16[2,128,1536]{2,1,0:T(8,128)(2,1)S(1)} collective-permute-done((f16[2,128,1536]{2,1,0:T(8,128)(2,1)S(1)}, f16[2,128,1536]{2,1,0:T(8,128)(2,1)S(1)}, u32[]{:S(2)}, u32[]{:S(2)}) %collective-permute-start.14) | collective-permute-done | bytes 786464 | tf_op jit(solution)/shard_map/ppermute | solution.py:196
  81.3 1.3 collective-permute-start.19
  82.6 2.7 %collective-permute-done.13 = f16[2,128,1536]{2,1,0:T(8,128)(2,1)S(1)} collective-permute-done((f16[2,128,1536]{2,1,0:T(8,128)(2,1)S(1)}, f16[2,128,1536]{2,1,0:T(8,128)(2,1)S(1)}, u32[]{:S(2)}, u32[]{:S(2)}) %collective-permute-start.13) | collective-permute-done | bytes 786464 | tf_op jit(solution)/shard_map/ppermute | solution.py:196
  85.9 1.4 collective-permute-start.18
  87.7 1.3 collective-permute-start.17
  89.8 1.3 collective-permute-start.26
  91.5 4.0 %collective-permute-start.25 = (f16[2,128,1024]{2,1,0:T(8,128)(2,1)S(1)}, f16[2,128,1024]{2,1,0:T(8,128)(2,1)S(1)}, u32[]{:S(2)}, u32[]{:S(2)}) collective-permute-start(f16[2,128,1024]{2,1,0:T(8,128)(2,1)S(1)} %multiply_convert_fusion.10), channel_id=1, source_target_pairs={{8,0},{20,28},{9,1},{21,29},{10,2},{22,30},{11,3},{23,31}} | collective-permute-start | bytes 1572872 | tf_op jit(solution)/shard_map/ppermute | solution.py:196
  95.5 1.3 collective-permute-start.24
  98.2 1.3 collective-permute-start.23
  99.9 4.0 %collective-permute-start.22 = (f16[2,128,1024]{2,1,0:T(8,128)(2,1)S(1)}, f16[2,128,1024]{2,1,0:T(8,128)(2,1)S(1)}, u32[]{:S(2)}, u32[]{:S(2)}) collective-permute-start(f16[2,128,1024]{2,1,0:T(8,128)(2,1)S(1)} %multiply_convert_fusion.9), channel_id=1, source_target_pairs={{8,0},{20,28},{9,1},{21,29},{10,2},{22,30},{11,3},{23,31}} | collective-permute-start | bytes 1572872 | tf_op jit(solution)/shard_map/ppermute | solution.py:196
  104.0 1.3 collective-permute-start.31
  105.7 1.3 collective-permute-start.30
  107.7 1.3 collective-permute-start.28
  109.0 5.2 %collective-permute-done.22 = f16[2,128,1024]{2,1,0:T(8,128)(2,1)S(1)} collective-permute-done((f16[2,128,1024]{2,1,0:T(8,128)(2,1)S(1)}, f16[2,128,1024]{2,1,0:T(8,128)(2,1)S(1)}, u32[]{:S(2)}, u32[]{:S(2)}) %collective-permute-start.22) | collective-permute-done | bytes 524320 | tf_op jit(solution)/shard_map/ppermute | solution.py:196
  114.6 1.3 collective-permute-start.27
  116.9 1.3 collective-permute-start.35
  119.4 2.8 %collective-permute-done.27 = bf16[128,1024]{1,0:T(8,128)(2,1)S(1)} collective-permute-done((bf16[128,1024]{1,0:T(8,128)(2,1)S(1)}, bf16[128,1024]{1,0:T(8,128)(2,1)S(1)}, u32[]{:S(2)}, u32[]{:S(2)}) %collective-permute-start.27) | collective-permute-done | bytes 262176 | tf_op jit(solution)/shard_map/ppermute | solution.py:206
  122.2 4.5 %collective-permute-start.32 = (bf16[128,1024]{1,0:T(8,128)(2,1)S(1)}, bf16[128,1024]{1,0:T(8,128)(2,1)S(1)}, u32[]{:S(2)}, u32[]{:S(2)}) collective-permute-start(bf16[128,1024]{1,0:T(8,128)(2,1)S(1)} %collective-permute-done.27), channel_id=1, source_target_pairs={{8,16},{20,12},{9,17},{21,13},{10,18},{22,14},{11,19},{23,15}} | collective-permute-start | bytes 786440 | tf_op jit(solution)/shard_map/ppermute | solution.py:206
  127.9 3.9 %shard_map.51.refs_3_ = f32[256,2048]{1,0:T(8,128)S(1)} custom-call(bf16[128,1536]{1,0:T(8,128)(2,1)S(1)} %select_select_fusion.2.refs_0_, bf16[128,1536]{1,0:T(8,128)(2,1)S(1)} %collective-permute-done.34.refs_1_, bf16[6656,2048]{1,0:T(8,128)(2,1)} %refs_2_.9), custom_call_target="tpu_custom_call" | custom-call | flops 1610612736 | bytes 10485760 | tf_op jit(solution)/shard_map/pallas_call | solution.py:126
  134.0 3.9 %shard_map.52.refs_3_ = f32[256,2048]{1,0:T(8,128)S(1)} custom-call(bf16[128,1536]{1,0:T(8,128)(2,1)S(1)} %select_select_fusion.1.refs_0_, bf16[128,1536]{1,0:T(8,128)(2,1)S(1)} %collective-permute-done.40.refs_1_, bf16[6656,2048]{1,0:T(8,128)(2,1)} %refs_2_.9, f32[256,2048]{1,0:T(8,128)S(1)} %shard_map.51.refs_3_), custom_call_target="tpu_custom_call" | custom-call | flops 1610612736 | bytes 10485760 | tf_op jit(solution)/shard_map/pallas_call | solution.py:126
  138.9 3.9 %shard_map.53.refs_3_ = f32[256,2048]{1,0:T(8,128)S(1)} custom-call(bf16[128,1536]{1,0:T(8,128)(2,1)S(1)} %select_select_fusion.refs_0_, bf16[128,1536]{1,0:T(8,128)(2,1)S(1)} %collective-permute-done.38.refs_1_, bf16[6656,2048]{1,0:T(8,128)(2,1)} %refs_2_.9, f32[256,2048]{1,0:T(8,128)S(1)} %shard_map.52.refs_3_), custom_call_target="tpu_custom_call" | custom-call | flops 1610612736 | bytes 10485760 | tf_op jit(solution)/shard_map/pallas_call | solution.py:126
  143.3 3.2 %shard_map.54.refs_3_ = f32[256,2048]{1,0:T(8,128)S(1)} custom-call(bf16[128,1024]{1,0:T(8,128)(2,1)S(1)} %select_select_fusion.4.refs_0_, bf16[128,1024]{1,0:T(8,128)(2,1)S(1)} %collective-permute-done.42.refs_1_, bf16[6656,2048]{1,0:T(8,128)(2,1)} %refs_2_.9, f32[256,2048]{1,0:T(8,128)S(1)} %shard_map.53.refs_3_), custom_call_target="tpu_custom_call" | custom-call | flops 1073741824 | bytes 8388608 | tf_op jit(solution)/shard_map/pallas_call | solution.py:126
  146.5 3.2 %shard_map.55 = f32[256,2048]{1,0:T(8,128)S(1)} custom-call(bf16[128,1024]{1,0:T(8,128)(2,1)S(1)} %select_select_fusion.3.refs_0_, bf16[128,1024]{1,0:T(8,128)(2,1)S(1)} %collective-permute-done.41.refs_1_, bf16[6656,2048]{1,0:T(8,128)(2,1)} %refs_2_.9, f32[256,2048]{1,0:T(8,128)S(1)} %shard_map.54.refs_3_), custom_call_target="tpu_custom_call" | custom-call | flops 1073741824 | bytes 8388608 | tf_op jit(solution)/shard_map/pallas_call | solution.py:126
  152.6 4.9 %collective-permute-done.43 = bf16[64,2048]{1,0:T(8,128)(2,1)S(1)} collective-permute-done((bf16[64,2048]{1,0:T(8,128)(2,1)S(1)}, bf16[64,2048]{1,0:T(8,128)(2,1)S(1)}, u32[]{:S(2)}, u32[]{:S(2)}) %collective-permute-start.43) | collective-permute-done | bytes 262176 | tf_op jit(solution)/shard_map/ppermute | solution.py:216
  158.1 6.0 %collective-permute-done.45 = bf16[64,2048]{1,0:T(8,128)(2,1)} collective-permute-done((bf16[64,2048]{1,0:T(8,128)(2,1)S(1)}, bf16[64,2048]{1,0:T(8,128)(2,1)}, u32[]{:S(2)}, u32[]{:S(2)}) %collective-permute-start.45) | collective-permute-done | bytes 262176 | tf_op jit(solution)/shard_map/ppermute | solution.py:216
  164.1 1.9 %convert_add_fusion = f32[64,2048]{1,0:T(8,128)} fusion(bf16[64,2048]{1,0:T(8,128)(2,1)} %collective-permute-done.45, bf16[64,2048]{1,0:T(8,128)(2,1)S(1)} %collective-permute-done.44, bf16[64,2048]{1,0:T(8,128)(2,1)S(1)} %collective-permute-done.43, f32[256,2048]{1,0:T(8,128)S(1)} %shard_map.55, s32[]{:T(128)S(6)} %select_n.173), kind=kLoop, calls=%fused_computation.82 | loop fusion | flops 786432 | bytes 1835012 | tf_op jit(solution)/shard_map/add | solution.py:307
  (93 shorter events, 26.9 us)
Async XLA Ops:
  0.0 7.4 %collective-permute-start = (bf16[64,2048]{1,0:T(8,128)(2,1)}, bf16[64,2048]{1,0:T(8,128)(2,1)S(1)}, u32[]{:S(2)}, u32[]{:S(2)}) collective-permute-start(bf16[64,2048]{1,0:T(8,128)(2,1)} %param.4), channel_id=1, source_target_pairs={{0,1},{1,0},{2,3},{3,2},{4,5},{5,4},{6,7},{7,6},{8,9},{9,8},{10,11... | collective-permute-start | bytes 786440 | tf_op jit(solution)/shard_map/ppermute | solution.py:216
  1.2 7.1 %collective-permute-start.1 = (bf16[64,2048]{1,0:T(8,128)(2,1)}, bf16[64,2048]{1,0:T(8,128)(2,1)S(1)}, u32[]{:S(2)}, u32[]{:S(2)}) collective-permute-start(bf16[64,2048]{1,0:T(8,128)(2,1)} %param.4), channel_id=1, source_target_pairs={{0,2},{1,3},{2,0},{3,1},{4,6},{5,7},{6,4},{7,5},{8,10},{9,11},{10,... | collective-permute-start | bytes 786440 | tf_op jit(solution)/shard_map/ppermute | solution.py:216
  2.5 11.6 %collective-permute-start.2 = (bf16[64,2048]{1,0:T(8,128)(2,1)}, bf16[64,2048]{1,0:T(8,128)(2,1)S(1)}, u32[]{:S(2)}, u32[]{:S(2)}) collective-permute-start(bf16[64,2048]{1,0:T(8,128)(2,1)} %param.4), channel_id=1, source_target_pairs={{0,3},{1,2},{2,1},{3,0},{4,7},{5,6},{6,5},{7,4},{8,11},{9,10},{10,... | collective-permute-start | bytes 786440 | tf_op jit(solution)/shard_map/ppermute | solution.py:216
  21.3 9.0 %collective-permute-start.3 = (f32[2,128,1536]{2,1,0:T(8,128)S(1)}, f32[2,128,1536]{2,1,0:T(8,128)S(1)}, u32[]{:S(2)}, u32[]{:S(2)}) collective-permute-start(f32[2,128,1536]{2,1,0:T(8,128)S(1)} %get-tuple-element.87), channel_id=1, source_target_pairs={{0,4},{4,0},{8,12},{12,8},{16,20},{20,16},{24,28},{28,24},{1,5},{5... | collective-permute-start | bytes 4718600 | tf_op jit(solution)/shard_map/ppermute | solution.py:193
  30.2 1.7 %copy-start = (f32[2,128,1536]{2,1,0:T(8,128)}, f32[2,128,1536]{2,1,0:T(8,128)S(1)}, u32[]{:S(2)}) copy-start(f32[2,128,1536]{2,1,0:T(8,128)S(1)} %get-tuple-element.96) | copy-start | bytes 4718596
  30.2 10.1 %collective-permute-start.6 = (f32[2,128,1536]{2,1,0:T(8,128)}, f32[2,128,1536]{2,1,0:T(8,128)}, u32[]{:S(2)}, u32[]{:S(2)}) collective-permute-start(f32[2,128,1536]{2,1,0:T(8,128)} %get-tuple-element.95), channel_id=1, source_target_pairs={{0,4},{4,0},{8,12},{12,8},{16,20},{20,16},{24,28},{28,24},{1,5},{5... | collective-permute-start | bytes 4718600 | tf_op jit(solution)/shard_map/ppermute | solution.py:193
  39.0 12.1 %collective-permute-start.4 = (f32[2,128,1536]{2,1,0:T(8,128)}, f32[2,128,1536]{2,1,0:T(8,128)}, u32[]{:S(2)}, u32[]{:S(2)}) collective-permute-start(f32[2,128,1536]{2,1,0:T(8,128)} %get-tuple-element.94), channel_id=1, source_target_pairs={{0,4},{4,0},{8,12},{12,8},{16,20},{20,16},{24,28},{28,24},{1,5},{5... | collective-permute-start | bytes 4718600 | tf_op jit(solution)/shard_map/ppermute | solution.py:193
  39.6 9.7 %collective-permute-start.5 = (f16[2,128,1536]{2,1,0:T(8,128)(2,1)S(1)}, f16[2,128,1536]{2,1,0:T(8,128)(2,1)S(1)}, u32[]{:S(2)}, u32[]{:S(2)}) collective-permute-start(f16[2,128,1536]{2,1,0:T(8,128)(2,1)S(1)} %get-tuple-element.173), channel_id=1, source_target_pairs={{24,16},{4,12},{25,17},{5,13},{26,18},{6,14},{27,19},{7,15}} | collective-permute-start | bytes 2359304 | tf_op jit(solution)/shard_map/ppermute | solution.py:196
  42.6 6.7 %copy-start.1 = (f32[2,128,1536]{2,1,0:T(8,128)S(1)}, f32[2,128,1536]{2,1,0:T(8,128)}, u32[]{:S(2)}) copy-start(f32[2,128,1536]{2,1,0:T(8,128)} %get-tuple-element.122) | copy-start | bytes 4718596
  42.6 15.8 %collective-permute-start.11 = (f16[2,128,1536]{2,1,0:T(8,128)(2,1)S(1)}, f16[2,128,1536]{2,1,0:T(8,128)(2,1)S(1)}, u32[]{:S(2)}, u32[]{:S(2)}) collective-permute-start(f16[2,128,1536]{2,1,0:T(8,128)(2,1)S(1)} %get-tuple-element.171), channel_id=1, source_target_pairs={{24,16},{4,12},{25,17},{5,13},{26,18},{6,14},{27,19},{7,15}} | collective-permute-start | bytes 2359304 | tf_op jit(solution)/shard_map/ppermute | solution.py:196
  48.0 12.4 %collective-permute-start.10 = (f32[2,128,1024]{2,1,0:T(8,128)S(1)}, f32[2,128,1024]{2,1,0:T(8,128)S(1)}, u32[]{:S(2)}, u32[]{:S(2)}) collective-permute-start(f32[2,128,1024]{2,1,0:T(8,128)S(1)} %get-tuple-element.107), channel_id=1, source_target_pairs={{0,4},{4,0},{8,12},{12,8},{16,20},{20,16},{24,28},{28,24},{1,5},{5... | collective-permute-start | bytes 3145736 | tf_op jit(solution)/shard_map/ppermute | solution.py:193
  49.9 14.1 %collective-permute-start.9 = (f16[2,128,1536]{2,1,0:T(8,128)(2,1)S(1)}, f16[2,128,1536]{2,1,0:T(8,128)(2,1)S(1)}, u32[]{:S(2)}, u32[]{:S(2)}) collective-permute-start(f16[2,128,1536]{2,1,0:T(8,128)(2,1)S(1)} %multiply_convert_fusion.6), channel_id=1, source_target_pairs={{16,8},{12,20},{17,9},{13,21},{18,10},{14,22},{19,11},{15,23}} | collective-permute-start | bytes 2359304 | tf_op jit(solution)/shard_map/ppermute | solution.py:196
  53.0 18.9 %collective-permute-start.8 = (f16[2,128,1536]{2,1,0:T(8,128)(2,1)S(1)}, f16[2,128,1536]{2,1,0:T(8,128)(2,1)S(1)}, u32[]{:S(2)}, u32[]{:S(2)}) collective-permute-start(f16[2,128,1536]{2,1,0:T(8,128)(2,1)S(1)} %get-tuple-element.169), channel_id=1, source_target_pairs={{24,16},{4,12},{25,17},{5,13},{26,18},{6,14},{27,19},{7,15}} | collective-permute-start | bytes 2359304 | tf_op jit(solution)/shard_map/ppermute | solution.py:196
  59.0 15.8 %collective-permute-start.16 = (f16[2,128,1536]{2,1,0:T(8,128)(2,1)S(1)}, f16[2,128,1536]{2,1,0:T(8,128)(2,1)S(1)}, u32[]{:S(2)}, u32[]{:S(2)}) collective-permute-start(f16[2,128,1536]{2,1,0:T(8,128)(2,1)S(1)} %multiply_convert_fusion.4), channel_id=1, source_target_pairs={{16,8},{12,20},{17,9},{13,21},{18,10},{14,22},{19,11},{15,23}} | collective-permute-start | bytes 2359304 | tf_op jit(solution)/shard_map/ppermute | solution.py:196
  60.7 16.1 %collective-permute-start.15 = (f16[2,128,1024]{2,1,0:T(8,128)(2,1)S(1)}, f16[2,128,1024]{2,1,0:T(8,128)(2,1)S(1)}, u32[]{:S(2)}, u32[]{:S(2)}) collective-permute-start(f16[2,128,1024]{2,1,0:T(8,128)(2,1)S(1)} %get-tuple-element.167), channel_id=1, source_target_pairs={{24,16},{4,12},{25,17},{5,13},{26,18},{6,14},{27,19},{7,15}} | collective-permute-start | bytes 1572872 | tf_op jit(solution)/shard_map/ppermute | solution.py:196
  64.0 9.9 %collective-permute-start.7 = (f32[2,128,1024]{2,1,0:T(8,128)S(1)}, f32[2,128,1024]{2,1,0:T(8,128)S(1)}, u32[]{:S(2)}, u32[]{:S(2)}) collective-permute-start(f32[2,128,1024]{2,1,0:T(8,128)S(1)} %get-tuple-element.106), channel_id=1, source_target_pairs={{0,4},{4,0},{8,12},{12,8},{16,20},{20,16},{24,28},{28,24},{1,5},{5... | collective-permute-start | bytes 3145736 | tf_op jit(solution)/shard_map/ppermute | solution.py:193
  67.6 13.2 %collective-permute-start.14 = (f16[2,128,1536]{2,1,0:T(8,128)(2,1)S(1)}, f16[2,128,1536]{2,1,0:T(8,128)(2,1)S(1)}, u32[]{:S(2)}, u32[]{:S(2)}) collective-permute-start(f16[2,128,1536]{2,1,0:T(8,128)(2,1)S(1)} %multiply_convert_fusion.3), channel_id=1, source_target_pairs={{8,0},{20,28},{9,1},{21,29},{10,2},{22,30},{11,3},{23,31}} | collective-permute-start | bytes 2359304 | tf_op jit(solution)/shard_map/ppermute | solution.py:196
  72.5 12.7 %collective-permute-start.13 = (f16[2,128,1536]{2,1,0:T(8,128)(2,1)S(1)}, f16[2,128,1536]{2,1,0:T(8,128)(2,1)S(1)}, u32[]{:S(2)}, u32[]{:S(2)}) collective-permute-start(f16[2,128,1536]{2,1,0:T(8,128)(2,1)S(1)} %multiply_convert_fusion.2), channel_id=1, source_target_pairs={{16,8},{12,20},{17,9},{13,21},{18,10},{14,22},{19,11},{15,23}} | collective-permute-start | bytes 2359304 | tf_op jit(solution)/shard_map/ppermute | solution.py:196
  74.2 13.1 %collective-permute-start.12 = (f16[2,128,1024]{2,1,0:T(8,128)(2,1)S(1)}, f16[2,128,1024]{2,1,0:T(8,128)(2,1)S(1)}, u32[]{:S(2)}, u32[]{:S(2)}) collective-permute-start(f16[2,128,1024]{2,1,0:T(8,128)(2,1)S(1)} %get-tuple-element.165), channel_id=1, source_target_pairs={{24,16},{4,12},{25,17},{5,13},{26,18},{6,14},{27,19},{7,15}} | collective-permute-start | bytes 1572872 | tf_op jit(solution)/shard_map/ppermute | solution.py:196
  75.5 13.8 %collective-permute-start.21 = (f16[2,128,1536]{2,1,0:T(8,128)(2,1)S(1)}, f16[2,128,1536]{2,1,0:T(8,128)(2,1)S(1)}, u32[]{:S(2)}, u32[]{:S(2)}) collective-permute-start(f16[2,128,1536]{2,1,0:T(8,128)(2,1)S(1)} %multiply_convert_fusion.1), channel_id=1, source_target_pairs={{8,0},{20,28},{9,1},{21,29},{10,2},{22,30},{11,3},{23,31}} | collective-permute-start | bytes 2359304 | tf_op jit(solution)/shard_map/ppermute | solution.py:196
  77.2 13.8 %collective-permute-start.20 = (f16[2,128,1024]{2,1,0:T(8,128)(2,1)S(1)}, f16[2,128,1024]{2,1,0:T(8,128)(2,1)S(1)}, u32[]{:S(2)}, u32[]{:S(2)}) collective-permute-start(f16[2,128,1024]{2,1,0:T(8,128)(2,1)S(1)} %multiply_convert_fusion.12), channel_id=1, source_target_pairs={{16,8},{12,20},{17,9},{13,21},{18,10},{14,22},{19,11},{15,23}} | collective-permute-start | bytes 1572872 | tf_op jit(solution)/shard_map/ppermute | solution.py:196
  81.3 14.2 %collective-permute-start.19 = (bf16[128,1536]{1,0:T(8,128)(2,1)S(1)}, bf16[128,1536]{1,0:T(8,128)(2,1)S(1)}, u32[]{:S(2)}, u32[]{:S(2)}) collective-permute-start(bf16[128,1536]{1,0:T(8,128)(2,1)S(1)} %fusion.35), channel_id=1, source_target_pairs={{0,8},{28,20},{1,9},{29,21},{2,10},{30,22},{3,11},{31,23}} | collective-permute-start | bytes 1179656 | tf_op jit(solution)/shard_map/ppermute | solution.py:206
  85.9 11.8 %collective-permute-start.18 = (f16[2,128,1536]{2,1,0:T(8,128)(2,1)S(1)}, f16[2,128,1536]{2,1,0:T(8,128)(2,1)S(1)}, u32[]{:S(2)}, u32[]{:S(2)}) collective-permute-start(f16[2,128,1536]{2,1,0:T(8,128)(2,1)S(1)} %multiply_convert_fusion), channel_id=1, source_target_pairs={{8,0},{20,28},{9,1},{21,29},{10,2},{22,30},{11,3},{23,31}} | collective-permute-start | bytes 2359304 | tf_op jit(solution)/shard_map/ppermute | solution.py:196
  87.7 11.8 %collective-permute-start.17 = (f16[2,128,1024]{2,1,0:T(8,128)(2,1)S(1)}, f16[2,128,1024]{2,1,0:T(8,128)(2,1)S(1)}, u32[]{:S(2)}, u32[]{:S(2)}) collective-permute-start(f16[2,128,1024]{2,1,0:T(8,128)(2,1)S(1)} %multiply_convert_fusion.11), channel_id=1, source_target_pairs={{16,8},{12,20},{17,9},{13,21},{18,10},{14,22},{19,11},{15,23}} | collective-permute-start | bytes 1572872 | tf_op jit(solution)/shard_map/ppermute | solution.py:196
  89.8 14.2 %collective-permute-start.26 = (bf16[128,1536]{1,0:T(8,128)(2,1)S(1)}, bf16[128,1536]{1,0:T(8,128)(2,1)S(1)}, u32[]{:S(2)}, u32[]{:S(2)}) collective-permute-start(bf16[128,1536]{1,0:T(8,128)(2,1)S(1)} %fusion.33), channel_id=1, source_target_pairs={{0,8},{28,20},{1,9},{29,21},{2,10},{30,22},{3,11},{31,23}} | collective-permute-start | bytes 1179656 | tf_op jit(solution)/shard_map/ppermute | solution.py:206
  91.5 13.8 %collective-permute-start.25 = (f16[2,128,1024]{2,1,0:T(8,128)(2,1)S(1)}, f16[2,128,1024]{2,1,0:T(8,128)(2,1)S(1)}, u32[]{:S(2)}, u32[]{:S(2)}) collective-permute-start(f16[2,128,1024]{2,1,0:T(8,128)(2,1)S(1)} %multiply_convert_fusion.10), channel_id=1, source_target_pairs={{8,0},{20,28},{9,1},{21,29},{10,2},{22,30},{11,3},{23,31}} | collective-permute-start | bytes 1572872 | tf_op jit(solution)/shard_map/ppermute | solution.py:196
  95.5 11.5 %collective-permute-start.24 = (bf16[128,1536]{1,0:T(8,128)(2,1)S(1)}, bf16[128,1536]{1,0:T(8,128)(2,1)S(1)}, u32[]{:S(2)}, u32[]{:S(2)}) collective-permute-start(bf16[128,1536]{1,0:T(8,128)(2,1)S(1)} %collective-permute-done.19), channel_id=1, source_target_pairs={{8,16},{20,12},{9,17},{21,13},{10,18},{22,14},{11,19},{23,15}} | collective-permute-start | bytes 1179656 | tf_op jit(solution)/shard_map/ppermute | solution.py:206
  98.2 9.5 %collective-permute-start.23 = (bf16[128,1536]{1,0:T(8,128)(2,1)S(1)}, bf16[128,1536]{1,0:T(8,128)(2,1)S(1)}, u32[]{:S(2)}, u32[]{:S(2)}) collective-permute-start(bf16[128,1536]{1,0:T(8,128)(2,1)S(1)} %fusion.31), channel_id=1, source_target_pairs={{0,8},{28,20},{1,9},{29,21},{2,10},{30,22},{3,11},{31,23}} | collective-permute-start | bytes 1179656 | tf_op jit(solution)/shard_map/ppermute | solution.py:206
  99.9 14.3 %collective-permute-start.22 = (f16[2,128,1024]{2,1,0:T(8,128)(2,1)S(1)}, f16[2,128,1024]{2,1,0:T(8,128)(2,1)S(1)}, u32[]{:S(2)}, u32[]{:S(2)}) collective-permute-start(f16[2,128,1024]{2,1,0:T(8,128)(2,1)S(1)} %multiply_convert_fusion.9), channel_id=1, source_target_pairs={{8,0},{20,28},{9,1},{21,29},{10,2},{22,30},{11,3},{23,31}} | collective-permute-start | bytes 1572872 | tf_op jit(solution)/shard_map/ppermute | solution.py:196
  104.0 12.0 %collective-permute-start.31 = (bf16[128,1536]{1,0:T(8,128)(2,1)S(1)}, bf16[128,1536]{1,0:T(8,128)(2,1)S(1)}, u32[]{:S(2)}, u32[]{:S(2)}) collective-permute-start(bf16[128,1536]{1,0:T(8,128)(2,1)S(1)} %collective-permute-done.26), channel_id=1, source_target_pairs={{8,16},{20,12},{9,17},{21,13},{10,18},{22,14},{11,19},{23,15}} | collective-permute-start | bytes 1179656 | tf_op jit(solution)/shard_map/ppermute | solution.py:206
  105.7 11.2 %collective-permute-start.30 = (bf16[128,1024]{1,0:T(8,128)(2,1)S(1)}, bf16[128,1024]{1,0:T(8,128)(2,1)S(1)}, u32[]{:S(2)}, u32[]{:S(2)}) collective-permute-start(bf16[128,1024]{1,0:T(8,128)(2,1)S(1)} %fusion.39), channel_id=1, source_target_pairs={{0,8},{28,20},{1,9},{29,21},{2,10},{30,22},{3,11},{31,23}} | collective-permute-start | bytes 786440 | tf_op jit(solution)/shard_map/ppermute | solution.py:206
  107.0 11.2 %collective-permute-start.29 = (bf16[128,1536]{1,0:T(8,128)(2,1)S(1)}, bf16[128,1536]{1,0:T(8,128)(2,1)S(1)}, u32[]{:S(2)}, u32[]{:S(2)}) collective-permute-start(bf16[128,1536]{1,0:T(8,128)(2,1)S(1)} %collective-permute-done.24), channel_id=1, source_target_pairs={{16,24},{12,4},{17,25},{13,5},{18,26},{14,6},{19,27},{15,7}} | collective-permute-start | bytes 1179656 | tf_op jit(solution)/shard_map/ppermute | solution.py:206
  107.7 10.9 %collective-permute-start.28 = (bf16[128,1536]{1,0:T(8,128)(2,1)S(1)}, bf16[128,1536]{1,0:T(8,128)(2,1)S(1)}, u32[]{:S(2)}, u32[]{:S(2)}) collective-permute-start(bf16[128,1536]{1,0:T(8,128)(2,1)S(1)} %collective-permute-done.23), channel_id=1, source_target_pairs={{8,16},{20,12},{9,17},{21,13},{10,18},{22,14},{11,19},{23,15}} | collective-permute-start | bytes 1179656 | tf_op jit(solution)/shard_map/ppermute | solution.py:206
  114.6 7.5 %collective-permute-start.27 = (bf16[128,1024]{1,0:T(8,128)(2,1)S(1)}, bf16[128,1024]{1,0:T(8,128)(2,1)S(1)}, u32[]{:S(2)}, u32[]{:S(2)}) collective-permute-start(bf16[128,1024]{1,0:T(8,128)(2,1)S(1)} %fusion.37), channel_id=1, source_target_pairs={{0,8},{28,20},{1,9},{29,21},{2,10},{30,22},{3,11},{31,23}} | collective-permute-start | bytes 786440 | tf_op jit(solution)/shard_map/ppermute | solution.py:206
  116.0 10.8 %collective-permute-start.36 = (bf16[128,1536]{1,0:T(8,128)(2,1)S(1)}, bf16[128,1536]{1,0:T(8,128)(2,1)S(1)}, u32[]{:S(2)}, u32[]{:S(2)}) collective-permute-start(bf16[128,1536]{1,0:T(8,128)(2,1)S(1)} %collective-permute-done.31), channel_id=1, source_target_pairs={{16,24},{12,4},{17,25},{13,5},{18,26},{14,6},{19,27},{15,7}} | collective-permute-start | bytes 1179656 | tf_op jit(solution)/shard_map/ppermute | solution.py:206
  116.9 10.3 %collective-permute-start.35 = (bf16[128,1024]{1,0:T(8,128)(2,1)S(1)}, bf16[128,1024]{1,0:T(8,128)(2,1)S(1)}, u32[]{:S(2)}, u32[]{:S(2)}) collective-permute-start(bf16[128,1024]{1,0:T(8,128)(2,1)S(1)} %collective-permute-done.30), channel_id=1, source_target_pairs={{8,16},{20,12},{9,17},{21,13},{10,18},{22,14},{11,19},{23,15}} | collective-permute-start | bytes 786440 | tf_op jit(solution)/shard_map/ppermute | solution.py:206
  118.6 9.3 %collective-permute-start.34 = (bf16[128,1536]{1,0:T(8,128)(2,1)S(1)}, bf16[128,1536]{1,0:T(8,128)(2,1)S(1)}, u32[]{:S(2)}, u32[]{:S(2)}) collective-permute-start(bf16[128,1536]{1,0:T(8,128)(2,1)S(1)} %select_select_fusion.2.refs_0_), channel_id=1, source_target_pairs={{0,4},{4,0},{8,12},{12,8},{16,20},{20,16},{24,28},{28,24},{1,5},{5... | collective-permute-start | bytes 1179656 | tf_op jit(solution)/shard_map/ppermute | solution.py:193
  118.7 13.1 %collective-permute-start.33 = (bf16[128,1536]{1,0:T(8,128)(2,1)S(1)}, bf16[128,1536]{1,0:T(8,128)(2,1)S(1)}, u32[]{:S(2)}, u32[]{:S(2)}) collective-permute-start(bf16[128,1536]{1,0:T(8,128)(2,1)S(1)} %collective-permute-done.28), channel_id=1, source_target_pairs={{16,24},{12,4},{17,25},{13,5},{18,26},{14,6},{19,27},{15,7}} | collective-permute-start | bytes 1179656 | tf_op jit(solution)/shard_map/ppermute | solution.py:206
  122.2 11.2 %collective-permute-start.32 = (bf16[128,1024]{1,0:T(8,128)(2,1)S(1)}, bf16[128,1024]{1,0:T(8,128)(2,1)S(1)}, u32[]{:S(2)}, u32[]{:S(2)}) collective-permute-start(bf16[128,1024]{1,0:T(8,128)(2,1)S(1)} %collective-permute-done.27), channel_id=1, source_target_pairs={{8,16},{20,12},{9,17},{21,13},{10,18},{22,14},{11,19},{23,15}} | collective-permute-start | bytes 786440 | tf_op jit(solution)/shard_map/ppermute | solution.py:206
  127.1 6.9 %collective-permute-start.40 = (bf16[128,1536]{1,0:T(8,128)(2,1)S(1)}, bf16[128,1536]{1,0:T(8,128)(2,1)S(1)}, u32[]{:S(2)}, u32[]{:S(2)}) collective-permute-start(bf16[128,1536]{1,0:T(8,128)(2,1)S(1)} %select_select_fusion.1.refs_0_), channel_id=1, source_target_pairs={{0,4},{4,0},{8,12},{12,8},{16,20},{20,16},{24,28},{28,24},{1,5},{5... | collective-permute-start | bytes 1179656 | tf_op jit(solution)/shard_map/ppermute | solution.py:193
  127.2 10.7 %collective-permute-start.39 = (bf16[128,1024]{1,0:T(8,128)(2,1)S(1)}, bf16[128,1024]{1,0:T(8,128)(2,1)S(1)}, u32[]{:S(2)}, u32[]{:S(2)}) collective-permute-start(bf16[128,1024]{1,0:T(8,128)(2,1)S(1)} %collective-permute-done.35), channel_id=1, source_target_pairs={{16,24},{12,4},{17,25},{13,5},{18,26},{14,6},{19,27},{15,7}} | collective-permute-start | bytes 786440 | tf_op jit(solution)/shard_map/ppermute | solution.py:206
  132.2 6.8 %collective-permute-start.38 = (bf16[128,1536]{1,0:T(8,128)(2,1)S(1)}, bf16[128,1536]{1,0:T(8,128)(2,1)S(1)}, u32[]{:S(2)}, u32[]{:S(2)}) collective-permute-start(bf16[128,1536]{1,0:T(8,128)(2,1)S(1)} %select_select_fusion.refs_0_), channel_id=1, source_target_pairs={{0,4},{4,0},{8,12},{12,8},{16,20},{20,16},{24,28},{28,24},{1,5},{5... | collective-permute-start | bytes 1179656 | tf_op jit(solution)/shard_map/ppermute | solution.py:193
  133.3 9.5 %collective-permute-start.37 = (bf16[128,1024]{1,0:T(8,128)(2,1)S(1)}, bf16[128,1024]{1,0:T(8,128)(2,1)S(1)}, u32[]{:S(2)}, u32[]{:S(2)}) collective-permute-start(bf16[128,1024]{1,0:T(8,128)(2,1)S(1)} %collective-permute-done.32), channel_id=1, source_target_pairs={{16,24},{12,4},{17,25},{13,5},{18,26},{14,6},{19,27},{15,7}} | collective-permute-start | bytes 786440 | tf_op jit(solution)/shard_map/ppermute | solution.py:206
  138.2 5.1 %collective-permute-start.42 = (bf16[128,1024]{1,0:T(8,128)(2,1)S(1)}, bf16[128,1024]{1,0:T(8,128)(2,1)S(1)}, u32[]{:S(2)}, u32[]{:S(2)}) collective-permute-start(bf16[128,1024]{1,0:T(8,128)(2,1)S(1)} %select_select_fusion.4.refs_0_), channel_id=1, source_target_pairs={{0,4},{4,0},{8,12},{12,8},{16,20},{20,16},{24,28},{28,24},{1,5},{5... | collective-permute-start | bytes 786440 | tf_op jit(solution)/shard_map/ppermute | solution.py:193
  143.1 3.4 %collective-permute-start.41 = (bf16[128,1024]{1,0:T(8,128)(2,1)S(1)}, bf16[128,1024]{1,0:T(8,128)(2,1)S(1)}, u32[]{:S(2)}, u32[]{:S(2)}) collective-permute-start(bf16[128,1024]{1,0:T(8,128)(2,1)S(1)} %select_select_fusion.3.refs_0_), channel_id=1, source_target_pairs={{0,4},{4,0},{8,12},{12,8},{16,20},{20,16},{24,28},{28,24},{1,5},{5... | collective-permute-start | bytes 786440 | tf_op jit(solution)/shard_map/ppermute | solution.py:193
  149.9 7.6 %collective-permute-start.43 = (bf16[64,2048]{1,0:T(8,128)(2,1)S(1)}, bf16[64,2048]{1,0:T(8,128)(2,1)S(1)}, u32[]{:S(2)}, u32[]{:S(2)}) collective-permute-start(bf16[64,2048]{1,0:T(8,128)(2,1)S(1)} %get-tuple-element.175), channel_id=1, source_target_pairs={{0,1},{1,0},{2,3},{3,2},{4,5},{5,4},{6,7},{7,6},{8,9},{9,8},{10,11... | collective-permute-start | bytes 786440 | tf_op jit(solution)/shard_map/ppermute | solution.py:216
  150.9 7.2 %collective-permute-start.44 = (bf16[64,2048]{1,0:T(8,128)(2,1)S(1)}, bf16[64,2048]{1,0:T(8,128)(2,1)S(1)}, u32[]{:S(2)}, u32[]{:S(2)}) collective-permute-start(bf16[64,2048]{1,0:T(8,128)(2,1)S(1)} %get-tuple-element.177), channel_id=1, source_target_pairs={{0,2},{1,3},{2,0},{3,1},{4,6},{5,7},{6,4},{7,5},{8,10},{9,11},{10,... | collective-permute-start | bytes 786440 | tf_op jit(solution)/shard_map/ppermute | solution.py:216
  151.4 12.7 %collective-permute-start.45 = (bf16[64,2048]{1,0:T(8,128)(2,1)S(1)}, bf16[64,2048]{1,0:T(8,128)(2,1)}, u32[]{:S(2)}, u32[]{:S(2)}) collective-permute-start(bf16[64,2048]{1,0:T(8,128)(2,1)S(1)} %get-tuple-element.176), channel_id=1, source_target_pairs={{0,3},{1,2},{2,1},{3,0},{4,7},{5,6},{6,5},{7,4},{8,11},{9,10},{10,... | collective-permute-start | bytes 786440 | tf_op jit(solution)/shard_map/ppermute | solution.py:216

commit v2 on v1

--- a/solution.py
+++ b/solution.py
@@ -11,9 +11,9 @@
 CORES = 2
 TOKEN_MAX = 6.0
 WEIGHT_MAX = 0.046875
-VMEM = 40 * 1024 * 1024
+VMEM = 20 * 1024 * 1024
 PIECES = 2
-SIZES = [3, 3, 3, 2, 2]
+SIZES = [3, 3, 2, 3, 2]
 GAPS = [0, 1, 1, 2]
 
 
@@ -179,6 +179,10 @@
     chips = n_gx // CORES
     own, depth = tokens.shape
     width = gate_weight.shape[1]
+    gate_weight, up_weight, down_weight = (
+        pltpu.with_memory_space_constraint(w, pltpu.HBM)
+        for w in (gate_weight, up_weight, down_weight)
+    )
     x = lax.axis_index("gx")
     y = lax.axis_index("gy")
     z, core = x // CORES, x % CORES
@@ -192,10 +196,13 @@
     def swap(v):
         return lax.ppermute(v, "gx", [(i, i ^ 1) for i in range(n_gx)])
 
+    def hop(v, pairs):
+        idle = set(range(n_gx)) - {i for pair in pairs for i in pair}
+        return lax.ppermute(v, "gx", pairs + [(i, i) for i in sorted(idle)])
+
     def towards(v, step):
-        return lax.ppermute(
+        return hop(
             v,
-            "gx",
             [
                 ((chips - step) * CORES, (chips - step - 1) * CORES),
                 ((step - 1) * CORES + 1, step * CORES + 1),
@@ -203,9 +210,8 @@
         )
 
     def back(v, step):
-        return lax.ppermute(
+        return hop(
             v,
-            "gx",
             [
                 ((step - 1) * CORES, step * CORES),
                 ((chips - step) * CORES + 1, (chips - step - 1) * CORES + 1),

time: 167 us -> 166 us (level)
  starting transfers between devices: 59.5 us -> 63.8 us
  waiting for transfers between devices: 39.5 us -> 36.2 us
    ppermute x30, starting transfers between devices: 45.3 us -> 50.9 us  [hop(): return lax.ppermute(v, 'gx', pairs + [(i, i) for i in sorted(idle)])]
    ppermute x30, waiting for transfers between devices: 16.6 us -> 11.7 us  [hop(): return lax.ppermute(v, 'gx', pairs + [(i, i) for i in sorted(idle)])]
  transfers between devices with their start and end apart: 46 -> 46, of which waited for: 13 -> 9; matrix products, arithmetic and copies ran while one was open for 9% -> 9% of each run, Pallas kernels for 23% -> 22%
where the time goes in v2:
time: 166 us
  starting transfers between devices  63.8 us (38%)
  Pallas kernels  47.3 us (28%)
  waiting for transfers between devices  36.2 us (22%)
  other arithmetic  17.2 us (10%)
    ppermute x30, starting transfers between devices, hop(): return lax.ppermute(v, 'gx', pairs + [(i, i) for i in sorted(idle)])  50.9 us
    pallas_call x5, Pallas kernels, first(): pl.pallas_call(kernel, in_specs=[vmem, hbm, hbm], out_specs=[vmem, vmem],...  29.2 us
    ppermute x6, waiting for transfers between devices, across(): return lax.ppermute(v, 'gy', [(i, i ^ shift) for i in range(n_gy)])  24.5 us
    pallas_call x5, Pallas kernels, second(): pl.pallas_call(kernel, in_specs=[vmem, vmem, hbm] + ([vmem] if carried el...  18.1 us
    ppermute x30, waiting for transfers between devices, hop(): return lax.ppermute(v, 'gx', pairs + [(i, i) for i in sorted(idle)])  11.7 us
    convert_element_type x15, other arithmetic, encode(): return (v * root * scale).astype(jnp.float16)  10.3 us
    ppermute x10, starting transfers between devices, swap(): return lax.ppermute(v, 'gx', [(i, i ^ 1) for i in range(n_gx)])  7.49 us
    ppermute x6, starting transfers between devices, across(): return lax.ppermute(v, 'gy', [(i, i ^ shift) for i in range(n_gy)])  5.36 us
  transfers between devices with their start and end apart: 46, of which 9 were waited for; matrix products, arithmetic and copies ran while one was open for 9% of the time, Pallas kernels for 22%

profile of v2, /device:TPU:17, one launch (start us, length us, event | category | flops | bytes accessed | tf_op | source)
XLA Modules:
  0.0 165.6 jit_solution(14447941022035981021)
XLA Ops:
  0.0 2.2 %collective-permute-start.2 = (bf16[64,2048]{1,0:T(8,128)(2,1)}, bf16[64,2048]{1,0:T(8,128)(2,1)S(1)}, u32[]{:S(2)}, u32[]{:S(2)}) collective-permute-start(bf16[64,2048]{1,0:T(8,128)(2,1)} %param.4), channel_id=1, source_target_pairs={{0,3},{1,2},{2,1},{3,0},{4,7},{5,6},{6,5},{7,4},{8,11},{9,10},{10,... | collective-permute-start | bytes 786440 | tf_op jit(solution)/shard_map/ppermute | solution.py:222
  2.7 5.7 %collective-permute-done.2 = bf16[64,2048]{1,0:T(8,128)(2,1)S(1)} collective-permute-done((bf16[64,2048]{1,0:T(8,128)(2,1)}, bf16[64,2048]{1,0:T(8,128)(2,1)S(1)}, u32[]{:S(2)}, u32[]{:S(2)}) %collective-permute-start.2) | collective-permute-done | bytes 262176 | tf_op jit(solution)/shard_map/ppermute | solution.py:222
  8.3 6.6 %collective-permute-done.1 = bf16[64,2048]{1,0:T(8,128)(2,1)S(1)} collective-permute-done((bf16[64,2048]{1,0:T(8,128)(2,1)}, bf16[64,2048]{1,0:T(8,128)(2,1)S(1)}, u32[]{:S(2)}, u32[]{:S(2)}) %collective-permute-start.1) | collective-permute-done | bytes 262176 | tf_op jit(solution)/shard_map/ppermute | solution.py:222
  15.0 1.1 pad_maximum_fusion
  16.3 7.1 %shard_map.46 = (f32[2,128,1536]{2,1,0:T(8,128)}, f32[2,128,1536]{2,1,0:T(8,128)S(1)}) custom-call(bf16[256,2048]{1,0:T(8,128)(2,1)S(1)} %pad_maximum_fusion.1.rows_ref, bf16[2048,6656]{1,0:T(8,128)(2,1)} %gate_ref.9, bf16[2048,6656]{1,0:T(8,128)(2,1)} %up_ref.9), custom_call_target="tpu_custom_call" | custom-call | flops 3221225472 | bytes 15728640 | tf_op jit(solution)/shard_map/pallas_call | solution.py:67
  24.0 7.1 %shard_map.47 = (f32[2,128,1536]{2,1,0:T(8,128)}, f32[2,128,1536]{2,1,0:T(8,128)S(1)}) custom-call(bf16[256,2048]{1,0:T(8,128)(2,1)S(1)} %pad_maximum_fusion.1.rows_ref, bf16[2048,6656]{1,0:T(8,128)(2,1)} %gate_ref.9, bf16[2048,6656]{1,0:T(8,128)(2,1)} %up_ref.9), custom_call_target="tpu_custom_call" | custom-call | flops 3221225472 | bytes 15728640 | tf_op jit(solution)/shard_map/pallas_call | solution.py:67
  31.7 2.3 %multiply_convert_fusion.8 = (f16[2,128,1536]{2,1,0:T(8,128)(2,1)S(1)}, f32[2,128,1536]{2,1,0:T(8,128)S(1)}) fusion(f32[2,128,1536]{2,1,0:T(8,128)} %copy-done, f32[2,128,1536]{2,1,0:T(8,128)} %collective-permute-done.3), kind=kLoop, calls=%fused_computation.41 | loop fusion | flops 2359296 | bytes 5505024 | tf_op jit(solution)/shard_map/convert_element_type | solution.py:22
  34.8 4.5 %shard_map.48 = (f32[2,128,1024]{2,1,0:T(8,128)S(1)}, f32[2,128,1024]{2,1,0:T(8,128)S(1)}) custom-call(bf16[256,2048]{1,0:T(8,128)(2,1)S(1)} %pad_maximum_fusion.1.rows_ref, bf16[2048,6656]{1,0:T(8,128)(2,1)} %gate_ref.9, bf16[2048,6656]{1,0:T(8,128)(2,1)} %up_ref.9), custom_call_target="tpu_custom_call" | custom-call | flops 2147483648 | bytes 10485760 | tf_op jit(solution)/shard_map/pallas_call | solution.py:67
  40.0 1.8 %multiply_convert_fusion.7 = (f16[2,128,1536]{2,1,0:T(8,128)(2,1)S(1)}, f32[2,128,1536]{2,1,0:T(8,128)S(1)}) fusion(f32[2,128,1536]{2,1,0:T(8,128)S(1)} %get-tuple-element.96, f32[2,128,1536]{2,1,0:T(8,128)} %collective-permute-done.6), kind=kLoop, calls=%fused_computation.40 | loop fusion | flops 2359296 | bytes 5505024 | tf_op jit(solution)/shard_map/convert_element_type | solution.py:22
  42.5 6.0 %shard_map.49 = (f32[2,128,1536]{2,1,0:T(8,128)S(1)}, f32[2,128,1536]{2,1,0:T(8,128)S(1)}) custom-call(bf16[256,2048]{1,0:T(8,128)(2,1)S(1)} %pad_maximum_fusion.1.rows_ref, bf16[2048,6656]{1,0:T(8,128)(2,1)} %gate_ref.9, bf16[2048,6656]{1,0:T(8,128)(2,1)} %up_ref.9), custom_call_target="tpu_custom_call" | custom-call | flops 3221225472 | bytes 15728640 | tf_op jit(solution)/shard_map/pallas_call | solution.py:67
  49.8 1.3 collective-permute-start.9
  51.4 0.9 collective-permute-start.8
  52.3 4.5 %shard_map.50 = (f32[2,128,1024]{2,1,0:T(8,128)S(1)}, f32[2,128,1024]{2,1,0:T(8,128)S(1)}) custom-call(bf16[256,2048]{1,0:T(8,128)(2,1)S(1)} %pad_maximum_fusion.1.rows_ref, bf16[2048,6656]{1,0:T(8,128)(2,1)} %gate_ref.9, bf16[2048,6656]{1,0:T(8,128)(2,1)} %up_ref.9), custom_call_target="tpu_custom_call" | custom-call | flops 2147483648 | bytes 10485760 | tf_op jit(solution)/shard_map/pallas_call | solution.py:67
  56.9 2.2 %collective-permute-start.7 = (f32[2,128,1024]{2,1,0:T(8,128)S(1)}, f32[2,128,1024]{2,1,0:T(8,128)S(1)}, u32[]{:S(2)}, u32[]{:S(2)}) collective-permute-start(f32[2,128,1024]{2,1,0:T(8,128)S(1)} %get-tuple-element.106), channel_id=1, source_target_pairs={{0,4},{4,0},{8,12},{12,8},{16,20},{20,16},{24,28},{28,24},{1,5},{5... | collective-permute-start | bytes 3145736 | tf_op jit(solution)/shard_map/ppermute | solution.py:197
  59.7 1.3 collective-permute-start.16
  63.4 3.1 %collective-permute-start.14 = (f16[2,128,1536]{2,1,0:T(8,128)(2,1)S(1)}, f16[2,128,1536]{2,1,0:T(8,128)(2,1)S(1)}, u32[]{:S(2)}, u32[]{:S(2)}) collective-permute-start(f16[2,128,1536]{2,1,0:T(8,128)(2,1)S(1)} %multiply_convert_fusion.3), channel_id=1, source_target_pairs={{8,0},{20,28},{4,4},{12,12},{16,16},{24,24},{9,1},{21,29},{5,5},{1... | collective-permute-start | bytes 2359304 | tf_op jit(solution)/shard_map/ppermute | solution.py:201
  66.9 1.3 collective-permute-start.13
  69.2 3.5 %collective-permute-done.16 = f16[2,128,1536]{2,1,0:T(8,128)(2,1)S(1)} collective-permute-done((f16[2,128,1536]{2,1,0:T(8,128)(2,1)S(1)}, f16[2,128,1536]{2,1,0:T(8,128)(2,1)S(1)}, u32[]{:S(2)}, u32[]{:S(2)}) %collective-permute-start.16) | collective-permute-done | bytes 786464 | tf_op jit(solution)/shard_map/ppermute | solution.py:201
  73.3 1.3 collective-permute-start.21
  75.3 1.3 collective-permute-start.20
  77.1 1.3 collective-permute-start.19
  78.8 4.0 %collective-permute-start.18 = (f16[2,128,1024]{2,1,0:T(8,128)(2,1)S(1)}, f16[2,128,1024]{2,1,0:T(8,128)(2,1)S(1)}, u32[]{:S(2)}, u32[]{:S(2)}) collective-permute-start(f16[2,128,1024]{2,1,0:T(8,128)(2,1)S(1)} %multiply_convert_fusion.11), channel_id=1, source_target_pairs={{8,0},{20,28},{4,4},{12,12},{16,16},{24,24},{9,1},{21,29},{5,5},{1... | collective-permute-start | bytes 1572872 | tf_op jit(solution)/shard_map/ppermute | solution.py:201
  83.3 1.3 collective-permute-start.17
  85.1 1.3 collective-permute-start.26
  86.4 1.6 collective-permute-done.20
  88.6 2.4 %collective-permute-start.25 = (f16[2,128,1536]{2,1,0:T(8,128)(2,1)S(1)}, f16[2,128,1536]{2,1,0:T(8,128)(2,1)S(1)}, u32[]{:S(2)}, u32[]{:S(2)}) collective-permute-start(f16[2,128,1536]{2,1,0:T(8,128)(2,1)S(1)} %multiply_convert_fusion), channel_id=1, source_target_pairs={{8,0},{20,28},{4,4},{12,12},{16,16},{24,24},{9,1},{21,29},{5,5},{1... | collective-permute-start | bytes 2359304 | tf_op jit(solution)/shard_map/ppermute | solution.py:201
  91.1 1.3 collective-permute-start.24
  92.8 1.3 collective-permute-start.23
  94.5 4.0 %collective-permute-start.22 = (f16[2,128,1024]{2,1,0:T(8,128)(2,1)S(1)}, f16[2,128,1024]{2,1,0:T(8,128)(2,1)S(1)}, u32[]{:S(2)}, u32[]{:S(2)}) collective-permute-start(f16[2,128,1024]{2,1,0:T(8,128)(2,1)S(1)} %multiply_convert_fusion.9), channel_id=1, source_target_pairs={{8,0},{20,28},{4,4},{12,12},{16,16},{24,24},{9,1},{21,29},{5,5},{1... | collective-permute-start | bytes 1572872 | tf_op jit(solution)/shard_map/ppermute | solution.py:201
  98.6 1.3 collective-permute-start.31
  100.5 1.3 collective-permute-start.30
  102.5 1.3 collective-permute-start.28
  103.8 3.8 %collective-permute-done.22 = f16[2,128,1024]{2,1,0:T(8,128)(2,1)S(1)} collective-permute-done((f16[2,128,1024]{2,1,0:T(8,128)(2,1)S(1)}, f16[2,128,1024]{2,1,0:T(8,128)(2,1)S(1)}, u32[]{:S(2)}, u32[]{:S(2)}) %collective-permute-start.22) | collective-permute-done | bytes 524320 | tf_op jit(solution)/shard_map/ppermute | solution.py:201
  108.0 1.5 collective-permute-start.27
  110.2 1.3 collective-permute-start.35
  113.2 2.0 %collective-permute-done.27 = bf16[128,1024]{1,0:T(8,128)(2,1)S(1)} collective-permute-done((bf16[128,1024]{1,0:T(8,128)(2,1)S(1)}, bf16[128,1024]{1,0:T(8,128)(2,1)S(1)}, u32[]{:S(2)}, u32[]{:S(2)}) %collective-permute-start.27) | collective-permute-done | bytes 262176 | tf_op jit(solution)/shard_map/ppermute | solution.py:201
  115.2 10.5 %collective-permute-start.32 = (bf16[128,1024]{1,0:T(8,128)(2,1)S(1)}, bf16[128,1024]{1,0:T(8,128)(2,1)S(1)}, u32[]{:S(2)}, u32[]{:S(2)}) collective-permute-start(bf16[128,1024]{1,0:T(8,128)(2,1)S(1)} %collective-permute-done.27), channel_id=1, source_target_pairs={{8,16},{20,12},{0,0},{4,4},{24,24},{28,28},{9,17},{21,13},{1,1},{5... | collective-permute-start | bytes 786440 | tf_op jit(solution)/shard_map/ppermute | solution.py:201
  126.9 3.9 %shard_map.51.refs_3_ = f32[256,2048]{1,0:T(8,128)S(1)} custom-call(bf16[128,1536]{1,0:T(8,128)(2,1)S(1)} %select_select_fusion.2.refs_0_, bf16[128,1536]{1,0:T(8,128)(2,1)S(1)} %collective-permute-done.34.refs_1_, bf16[6656,2048]{1,0:T(8,128)(2,1)} %refs_2_.9), custom_call_target="tpu_custom_call" | custom-call | flops 1610612736 | bytes 10485760 | tf_op jit(solution)/shard_map/pallas_call | solution.py:126
  131.0 1.2 collective-permute-start.38
  132.9 3.9 %shard_map.52.refs_3_ = f32[256,2048]{1,0:T(8,128)S(1)} custom-call(bf16[128,1536]{1,0:T(8,128)(2,1)S(1)} %select_select_fusion.1.refs_0_, bf16[128,1536]{1,0:T(8,128)(2,1)S(1)} %collective-permute-done.40.refs_1_, bf16[6656,2048]{1,0:T(8,128)(2,1)} %refs_2_.9, f32[256,2048]{1,0:T(8,128)S(1)} %shard_map.51.refs_3_), custom_call_target="tpu_custom_call" | custom-call | flops 1610612736 | bytes 10485760 | tf_op jit(solution)/shard_map/pallas_call | solution.py:126
  137.9 3.2 %shard_map.53.refs_3_ = f32[256,2048]{1,0:T(8,128)S(1)} custom-call(bf16[128,1024]{1,0:T(8,128)(2,1)S(1)} %select_select_fusion.4.refs_0_, bf16[128,1024]{1,0:T(8,128)(2,1)S(1)} %collective-permute-done.38.refs_1_, bf16[6656,2048]{1,0:T(8,128)(2,1)} %refs_2_.9, f32[256,2048]{1,0:T(8,128)S(1)} %shard_map.52.refs_3_), custom_call_target="tpu_custom_call" | custom-call | flops 1073741824 | bytes 8388608 | tf_op jit(solution)/shard_map/pallas_call | solution.py:126
  141.6 3.9 %shard_map.54.refs_3_ = f32[256,2048]{1,0:T(8,128)S(1)} custom-call(bf16[128,1536]{1,0:T(8,128)(2,1)S(1)} %select_select_fusion.refs_0_, bf16[128,1536]{1,0:T(8,128)(2,1)S(1)} %collective-permute-done.42.refs_1_, bf16[6656,2048]{1,0:T(8,128)(2,1)} %refs_2_.9, f32[256,2048]{1,0:T(8,128)S(1)} %shard_map.53.refs_3_), custom_call_target="tpu_custom_call" | custom-call | flops 1610612736 | bytes 10485760 | tf_op jit(solution)/shard_map/pallas_call | solution.py:126
  145.5 3.2 %shard_map.55 = f32[256,2048]{1,0:T(8,128)S(1)} custom-call(bf16[128,1024]{1,0:T(8,128)(2,1)S(1)} %select_select_fusion.3.refs_0_, bf16[128,1024]{1,0:T(8,128)(2,1)S(1)} %collective-permute-done.41.refs_1_, bf16[6656,2048]{1,0:T(8,128)(2,1)} %refs_2_.9, f32[256,2048]{1,0:T(8,128)S(1)} %shard_map.54.refs_3_), custom_call_target="tpu_custom_call" | custom-call | flops 1073741824 | bytes 8388608 | tf_op jit(solution)/shard_map/pallas_call | solution.py:126
  148.8 1.4 collective-permute-start.45
  150.3 1.0 collective-permute-start.44
  151.6 5.8 %collective-permute-done.45 = bf16[64,2048]{1,0:T(8,128)(2,1)S(1)} collective-permute-done((bf16[64,2048]{1,0:T(8,128)(2,1)S(1)}, bf16[64,2048]{1,0:T(8,128)(2,1)S(1)}, u32[]{:S(2)}, u32[]{:S(2)}) %collective-permute-start.45) | collective-permute-done | bytes 262176 | tf_op jit(solution)/shard_map/ppermute | solution.py:222
  157.4 6.4 %collective-permute-done.44 = bf16[64,2048]{1,0:T(8,128)(2,1)S(1)} collective-permute-done((bf16[64,2048]{1,0:T(8,128)(2,1)S(1)}, bf16[64,2048]{1,0:T(8,128)(2,1)S(1)}, u32[]{:S(2)}, u32[]{:S(2)}) %collective-permute-start.44) | collective-permute-done | bytes 262176 | tf_op jit(solution)/shard_map/ppermute | solution.py:222
  163.8 1.9 %convert_add_fusion = f32[64,2048]{1,0:T(8,128)} fusion(bf16[64,2048]{1,0:T(8,128)(2,1)S(1)} %collective-permute-done.45, bf16[64,2048]{1,0:T(8,128)(2,1)S(1)} %collective-permute-done.44, bf16[64,2048]{1,0:T(8,128)(2,1)} %collective-permute-done.43, f32[256,2048]{1,0:T(8,128)S(1)} %shard_map.55, s32[]{:T(128)S(6)} %select_n.173), kind=kLoop, calls=%fused_computation.82 | loop fusion | flops 786432 | bytes 1835012 | tf_op jit(solution)/shard_map/add | solution.py:313
  (91 shorter events, 22.2 us)
Async XLA Ops:
  0.0 8.3 %collective-permute-start.2 = (bf16[64,2048]{1,0:T(8,128)(2,1)}, bf16[64,2048]{1,0:T(8,128)(2,1)S(1)}, u32[]{:S(2)}, u32[]{:S(2)}) collective-permute-start(bf16[64,2048]{1,0:T(8,128)(2,1)} %param.4), channel_id=1, source_target_pairs={{0,3},{1,2},{2,1},{3,0},{4,7},{5,6},{6,5},{7,4},{8,11},{9,10},{10,... | collective-permute-start | bytes 786440 | tf_op jit(solution)/shard_map/ppermute | solution.py:222
  2.2 12.8 %collective-permute-start.1 = (bf16[64,2048]{1,0:T(8,128)(2,1)}, bf16[64,2048]{1,0:T(8,128)(2,1)S(1)}, u32[]{:S(2)}, u32[]{:S(2)}) collective-permute-start(bf16[64,2048]{1,0:T(8,128)(2,1)} %param.4), channel_id=1, source_target_pairs={{0,2},{1,3},{2,0},{3,1},{4,6},{5,7},{6,4},{7,5},{8,10},{9,11},{10,... | collective-permute-start | bytes 786440 | tf_op jit(solution)/shard_map/ppermute | solution.py:222
  2.4 12.6 %collective-permute-start = (bf16[64,2048]{1,0:T(8,128)(2,1)}, bf16[64,2048]{1,0:T(8,128)(2,1)S(1)}, u32[]{:S(2)}, u32[]{:S(2)}) collective-permute-start(bf16[64,2048]{1,0:T(8,128)(2,1)} %param.4), channel_id=1, source_target_pairs={{0,1},{1,0},{2,3},{3,2},{4,5},{5,4},{6,7},{7,6},{8,9},{9,8},{10,11... | collective-permute-start | bytes 786440 | tf_op jit(solution)/shard_map/ppermute | solution.py:222
  23.4 7.8 %copy-start = (f32[2,128,1536]{2,1,0:T(8,128)}, f32[2,128,1536]{2,1,0:T(8,128)S(1)}, u32[]{:S(2)}) copy-start(f32[2,128,1536]{2,1,0:T(8,128)S(1)} %get-tuple-element.90) | copy-start | bytes 4718596
  23.4 8.3 %collective-permute-start.3 = (f32[2,128,1536]{2,1,0:T(8,128)}, f32[2,128,1536]{2,1,0:T(8,128)}, u32[]{:S(2)}, u32[]{:S(2)}) collective-permute-start(f32[2,128,1536]{2,1,0:T(8,128)} %get-tuple-element.87), channel_id=1, source_target_pairs={{0,4},{4,0},{8,12},{12,8},{16,20},{20,16},{24,28},{28,24},{1,5},{5... | collective-permute-start | bytes 4718600 | tf_op jit(solution)/shard_map/ppermute | solution.py:197
  31.2 8.8 %collective-permute-start.6 = (f32[2,128,1536]{2,1,0:T(8,128)}, f32[2,128,1536]{2,1,0:T(8,128)}, u32[]{:S(2)}, u32[]{:S(2)}) collective-permute-start(f32[2,128,1536]{2,1,0:T(8,128)} %get-tuple-element.95), channel_id=1, source_target_pairs={{0,4},{4,0},{8,12},{12,8},{16,20},{20,16},{24,28},{28,24},{1,5},{5... | collective-permute-start | bytes 4718600 | tf_op jit(solution)/shard_map/ppermute | solution.py:197
  34.0 15.1 %collective-permute-start.5 = (f16[2,128,1536]{2,1,0:T(8,128)(2,1)S(1)}, f16[2,128,1536]{2,1,0:T(8,128)(2,1)S(1)}, u32[]{:S(2)}, u32[]{:S(2)}) collective-permute-start(f16[2,128,1536]{2,1,0:T(8,128)(2,1)S(1)} %get-tuple-element.173), channel_id=1, source_target_pairs={{24,16},{4,12},{0,0},{8,8},{20,20},{28,28},{25,17},{5,13},{1,1},{9... | collective-permute-start | bytes 2359304 | tf_op jit(solution)/shard_map/ppermute | solution.py:201
  39.3 11.8 %collective-permute-start.4 = (f32[2,128,1024]{2,1,0:T(8,128)S(1)}, f32[2,128,1024]{2,1,0:T(8,128)S(1)}, u32[]{:S(2)}, u32[]{:S(2)}) collective-permute-start(f32[2,128,1024]{2,1,0:T(8,128)S(1)} %get-tuple-element.94), channel_id=1, source_target_pairs={{0,4},{4,0},{8,12},{12,8},{16,20},{20,16},{24,28},{28,24},{1,5},{5... | collective-permute-start | bytes 3145736 | tf_op jit(solution)/shard_map/ppermute | solution.py:197
  41.8 17.3 %collective-permute-start.11 = (f16[2,128,1536]{2,1,0:T(8,128)(2,1)S(1)}, f16[2,128,1536]{2,1,0:T(8,128)(2,1)S(1)}, u32[]{:S(2)}, u32[]{:S(2)}) collective-permute-start(f16[2,128,1536]{2,1,0:T(8,128)(2,1)S(1)} %get-tuple-element.171), channel_id=1, source_target_pairs={{24,16},{4,12},{0,0},{8,8},{20,20},{28,28},{25,17},{5,13},{1,1},{9... | collective-permute-start | bytes 2359304 | tf_op jit(solution)/shard_map/ppermute | solution.py:201
  48.5 12.5 %collective-permute-start.10 = (f32[2,128,1536]{2,1,0:T(8,128)S(1)}, f32[2,128,1536]{2,1,0:T(8,128)S(1)}, u32[]{:S(2)}, u32[]{:S(2)}) collective-permute-start(f32[2,128,1536]{2,1,0:T(8,128)S(1)} %get-tuple-element.107), channel_id=1, source_target_pairs={{0,4},{4,0},{8,12},{12,8},{16,20},{20,16},{24,28},{28,24},{1,5},{5... | collective-permute-start | bytes 4718600 | tf_op jit(solution)/shard_map/ppermute | solution.py:197
  49.8 13.0 %collective-permute-start.9 = (f16[2,128,1536]{2,1,0:T(8,128)(2,1)S(1)}, f16[2,128,1536]{2,1,0:T(8,128)(2,1)S(1)}, u32[]{:S(2)}, u32[]{:S(2)}) collective-permute-start(f16[2,128,1536]{2,1,0:T(8,128)(2,1)S(1)} %multiply_convert_fusion.6), channel_id=1, source_target_pairs={{16,8},{12,20},{0,0},{4,4},{24,24},{28,28},{17,9},{13,21},{1,1},{5... | collective-permute-start | bytes 2359304 | tf_op jit(solution)/shard_map/ppermute | solution.py:201
  51.4 15.1 %collective-permute-start.8 = (f16[2,128,1024]{2,1,0:T(8,128)(2,1)S(1)}, f16[2,128,1024]{2,1,0:T(8,128)(2,1)S(1)}, u32[]{:S(2)}, u32[]{:S(2)}) collective-permute-start(f16[2,128,1024]{2,1,0:T(8,128)(2,1)S(1)} %get-tuple-element.169), channel_id=1, source_target_pairs={{24,16},{4,12},{0,0},{8,8},{20,20},{28,28},{25,17},{5,13},{1,1},{9... | collective-permute-start | bytes 1572872 | tf_op jit(solution)/shard_map/ppermute | solution.py:201
  56.9 11.4 %collective-permute-start.7 = (f32[2,128,1024]{2,1,0:T(8,128)S(1)}, f32[2,128,1024]{2,1,0:T(8,128)S(1)}, u32[]{:S(2)}, u32[]{:S(2)}) collective-permute-start(f32[2,128,1024]{2,1,0:T(8,128)S(1)} %get-tuple-element.106), channel_id=1, source_target_pairs={{0,4},{4,0},{8,12},{12,8},{16,20},{20,16},{24,28},{28,24},{1,5},{5... | collective-permute-start | bytes 3145736 | tf_op jit(solution)/shard_map/ppermute | solution.py:197
  59.7 13.0 %collective-permute-start.16 = (f16[2,128,1536]{2,1,0:T(8,128)(2,1)S(1)}, f16[2,128,1536]{2,1,0:T(8,128)(2,1)S(1)}, u32[]{:S(2)}, u32[]{:S(2)}) collective-permute-start(f16[2,128,1536]{2,1,0:T(8,128)(2,1)S(1)} %multiply_convert_fusion.5), channel_id=1, source_target_pairs={{16,8},{12,20},{0,0},{4,4},{24,24},{28,28},{17,9},{13,21},{1,1},{5... | collective-permute-start | bytes 2359304 | tf_op jit(solution)/shard_map/ppermute | solution.py:201
  61.4 13.2 %collective-permute-start.15 = (f16[2,128,1536]{2,1,0:T(8,128)(2,1)S(1)}, f16[2,128,1536]{2,1,0:T(8,128)(2,1)S(1)}, u32[]{:S(2)}, u32[]{:S(2)}) collective-permute-start(f16[2,128,1536]{2,1,0:T(8,128)(2,1)S(1)} %get-tuple-element.167), channel_id=1, source_target_pairs={{24,16},{4,12},{0,0},{8,8},{20,20},{28,28},{25,17},{5,13},{1,1},{9... | collective-permute-start | bytes 2359304 | tf_op jit(solution)/shard_map/ppermute | solution.py:201
  63.4 13.2 %collective-permute-start.14 = (f16[2,128,1536]{2,1,0:T(8,128)(2,1)S(1)}, f16[2,128,1536]{2,1,0:T(8,128)(2,1)S(1)}, u32[]{:S(2)}, u32[]{:S(2)}) collective-permute-start(f16[2,128,1536]{2,1,0:T(8,128)(2,1)S(1)} %multiply_convert_fusion.3), channel_id=1, source_target_pairs={{8,0},{20,28},{4,4},{12,12},{16,16},{24,24},{9,1},{21,29},{5,5},{1... | collective-permute-start | bytes 2359304 | tf_op jit(solution)/shard_map/ppermute | solution.py:201
  66.9 11.4 %collective-permute-start.13 = (f16[2,128,1024]{2,1,0:T(8,128)(2,1)S(1)}, f16[2,128,1024]{2,1,0:T(8,128)(2,1)S(1)}, u32[]{:S(2)}, u32[]{:S(2)}) collective-permute-start(f16[2,128,1024]{2,1,0:T(8,128)(2,1)S(1)} %multiply_convert_fusion.13), channel_id=1, source_target_pairs={{16,8},{12,20},{0,0},{4,4},{24,24},{28,28},{17,9},{13,21},{1,1},{5... | collective-permute-start | bytes 1572872 | tf_op jit(solution)/shard_map/ppermute | solution.py:201
  68.5 14.3 %collective-permute-start.12 = (f16[2,128,1024]{2,1,0:T(8,128)(2,1)S(1)}, f16[2,128,1024]{2,1,0:T(8,128)(2,1)S(1)}, u32[]{:S(2)}, u32[]{:S(2)}) collective-permute-start(f16[2,128,1024]{2,1,0:T(8,128)(2,1)S(1)} %get-tuple-element.165), channel_id=1, source_target_pairs={{24,16},{4,12},{0,0},{8,8},{20,20},{28,28},{25,17},{5,13},{1,1},{9... | collective-permute-start | bytes 1572872 | tf_op jit(solution)/shard_map/ppermute | solution.py:201
  73.3 11.3 %collective-permute-start.21 = (f16[2,128,1536]{2,1,0:T(8,128)(2,1)S(1)}, f16[2,128,1536]{2,1,0:T(8,128)(2,1)S(1)}, u32[]{:S(2)}, u32[]{:S(2)}) collective-permute-start(f16[2,128,1536]{2,1,0:T(8,128)(2,1)S(1)} %multiply_convert_fusion.2), channel_id=1, source_target_pairs={{8,0},{20,28},{4,4},{12,12},{16,16},{24,24},{9,1},{21,29},{5,5},{1... | collective-permute-start | bytes 2359304 | tf_op jit(solution)/shard_map/ppermute | solution.py:201
  75.3 12.7 %collective-permute-start.20 = (f16[2,128,1536]{2,1,0:T(8,128)(2,1)S(1)}, f16[2,128,1536]{2,1,0:T(8,128)(2,1)S(1)}, u32[]{:S(2)}, u32[]{:S(2)}) collective-permute-start(f16[2,128,1536]{2,1,0:T(8,128)(2,1)S(1)} %multiply_convert_fusion.1), channel_id=1, source_target_pairs={{16,8},{12,20},{0,0},{4,4},{24,24},{28,28},{17,9},{13,21},{1,1},{5... | collective-permute-start | bytes 2359304 | tf_op jit(solution)/shard_map/ppermute | solution.py:201
  77.1 14.0 %collective-permute-start.19 = (bf16[128,1536]{1,0:T(8,128)(2,1)S(1)}, bf16[128,1536]{1,0:T(8,128)(2,1)S(1)}, u32[]{:S(2)}, u32[]{:S(2)}) collective-permute-start(bf16[128,1536]{1,0:T(8,128)(2,1)S(1)} %fusion.35), channel_id=1, source_target_pairs={{0,8},{28,20},{4,4},{12,12},{16,16},{24,24},{1,9},{29,21},{5,5},{1... | collective-permute-start | bytes 1179656 | tf_op jit(solution)/shard_map/ppermute | solution.py:201
  78.8 13.6 %collective-permute-start.18 = (f16[2,128,1024]{2,1,0:T(8,128)(2,1)S(1)}, f16[2,128,1024]{2,1,0:T(8,128)(2,1)S(1)}, u32[]{:S(2)}, u32[]{:S(2)}) collective-permute-start(f16[2,128,1024]{2,1,0:T(8,128)(2,1)S(1)} %multiply_convert_fusion.11), channel_id=1, source_target_pairs={{8,0},{20,28},{4,4},{12,12},{16,16},{24,24},{9,1},{21,29},{5,5},{1... | collective-permute-start | bytes 1572872 | tf_op jit(solution)/shard_map/ppermute | solution.py:201
  83.3 10.8 %collective-permute-start.17 = (f16[2,128,1024]{2,1,0:T(8,128)(2,1)S(1)}, f16[2,128,1024]{2,1,0:T(8,128)(2,1)S(1)}, u32[]{:S(2)}, u32[]{:S(2)}) collective-permute-start(f16[2,128,1024]{2,1,0:T(8,128)(2,1)S(1)} %multiply_convert_fusion.10), channel_id=1, source_target_pairs={{16,8},{12,20},{0,0},{4,4},{24,24},{28,28},{17,9},{13,21},{1,1},{5... | collective-permute-start | bytes 1572872 | tf_op jit(solution)/shard_map/ppermute | solution.py:201
  85.1 13.5 %collective-permute-start.26 = (bf16[128,1536]{1,0:T(8,128)(2,1)S(1)}, bf16[128,1536]{1,0:T(8,128)(2,1)S(1)}, u32[]{:S(2)}, u32[]{:S(2)}) collective-permute-start(bf16[128,1536]{1,0:T(8,128)(2,1)S(1)} %fusion.33), channel_id=1, source_target_pairs={{0,8},{28,20},{4,4},{12,12},{16,16},{24,24},{1,9},{29,21},{5,5},{1... | collective-permute-start | bytes 1179656 | tf_op jit(solution)/shard_map/ppermute | solution.py:201
  88.6 11.3 %collective-permute-start.25 = (f16[2,128,1536]{2,1,0:T(8,128)(2,1)S(1)}, f16[2,128,1536]{2,1,0:T(8,128)(2,1)S(1)}, u32[]{:S(2)}, u32[]{:S(2)}) collective-permute-start(f16[2,128,1536]{2,1,0:T(8,128)(2,1)S(1)} %multiply_convert_fusion), channel_id=1, source_target_pairs={{8,0},{20,28},{4,4},{12,12},{16,16},{24,24},{9,1},{21,29},{5,5},{1... | collective-permute-start | bytes 2359304 | tf_op jit(solution)/shard_map/ppermute | solution.py:201
  91.1 10.7 %collective-permute-start.24 = (bf16[128,1536]{1,0:T(8,128)(2,1)S(1)}, bf16[128,1536]{1,0:T(8,128)(2,1)S(1)}, u32[]{:S(2)}, u32[]{:S(2)}) collective-permute-start(bf16[128,1536]{1,0:T(8,128)(2,1)S(1)} %collective-permute-done.19), channel_id=1, source_target_pairs={{8,16},{20,12},{0,0},{4,4},{24,24},{28,28},{9,17},{21,13},{1,1},{5... | collective-permute-start | bytes 1179656 | tf_op jit(solution)/shard_map/ppermute | solution.py:201
  92.8 9.7 %collective-permute-start.23 = (bf16[128,1024]{1,0:T(8,128)(2,1)S(1)}, bf16[128,1024]{1,0:T(8,128)(2,1)S(1)}, u32[]{:S(2)}, u32[]{:S(2)}) collective-permute-start(bf16[128,1024]{1,0:T(8,128)(2,1)S(1)} %fusion.39), channel_id=1, source_target_pairs={{0,8},{28,20},{4,4},{12,12},{16,16},{24,24},{1,9},{29,21},{5,5},{1... | collective-permute-start | bytes 786440 | tf_op jit(solution)/shard_map/ppermute | solution.py:201
  94.5 13.1 %collective-permute-start.22 = (f16[2,128,1024]{2,1,0:T(8,128)(2,1)S(1)}, f16[2,128,1024]{2,1,0:T(8,128)(2,1)S(1)}, u32[]{:S(2)}, u32[]{:S(2)}) collective-permute-start(f16[2,128,1024]{2,1,0:T(8,128)(2,1)S(1)} %multiply_convert_fusion.9), channel_id=1, source_target_pairs={{8,0},{20,28},{4,4},{12,12},{16,16},{24,24},{9,1},{21,29},{5,5},{1... | collective-permute-start | bytes 1572872 | tf_op jit(solution)/shard_map/ppermute | solution.py:201
  98.6 11.0 %collective-permute-start.31 = (bf16[128,1536]{1,0:T(8,128)(2,1)S(1)}, bf16[128,1536]{1,0:T(8,128)(2,1)S(1)}, u32[]{:S(2)}, u32[]{:S(2)}) collective-permute-start(bf16[128,1536]{1,0:T(8,128)(2,1)S(1)} %collective-permute-done.26), channel_id=1, source_target_pairs={{8,16},{20,12},{0,0},{4,4},{24,24},{28,28},{9,17},{21,13},{1,1},{5... | collective-permute-start | bytes 1179656 | tf_op jit(solution)/shard_map/ppermute | solution.py:201
  100.5 9.8 %collective-permute-start.30 = (bf16[128,1536]{1,0:T(8,128)(2,1)S(1)}, bf16[128,1536]{1,0:T(8,128)(2,1)S(1)}, u32[]{:S(2)}, u32[]{:S(2)}) collective-permute-start(bf16[128,1536]{1,0:T(8,128)(2,1)S(1)} %fusion.31), channel_id=1, source_target_pairs={{0,8},{28,20},{4,4},{12,12},{16,16},{24,24},{1,9},{29,21},{5,5},{1... | collective-permute-start | bytes 1179656 | tf_op jit(solution)/shard_map/ppermute | solution.py:201
  101.8 9.8 %collective-permute-start.29 = (bf16[128,1536]{1,0:T(8,128)(2,1)S(1)}, bf16[128,1536]{1,0:T(8,128)(2,1)S(1)}, u32[]{:S(2)}, u32[]{:S(2)}) collective-permute-start(bf16[128,1536]{1,0:T(8,128)(2,1)S(1)} %collective-permute-done.24), channel_id=1, source_target_pairs={{16,24},{12,4},{0,0},{8,8},{20,20},{28,28},{17,25},{13,5},{1,1},{9... | collective-permute-start | bytes 1179656 | tf_op jit(solution)/shard_map/ppermute | solution.py:201
  102.5 10.1 %collective-permute-start.28 = (bf16[128,1024]{1,0:T(8,128)(2,1)S(1)}, bf16[128,1024]{1,0:T(8,128)(2,1)S(1)}, u32[]{:S(2)}, u32[]{:S(2)}) collective-permute-start(bf16[128,1024]{1,0:T(8,128)(2,1)S(1)} %collective-permute-done.23), channel_id=1, source_target_pairs={{8,16},{20,12},{0,0},{4,4},{24,24},{28,28},{9,17},{21,13},{1,1},{5... | collective-permute-start | bytes 786440 | tf_op jit(solution)/shard_map/ppermute | solution.py:201
  108.0 7.2 %collective-permute-start.27 = (bf16[128,1024]{1,0:T(8,128)(2,1)S(1)}, bf16[128,1024]{1,0:T(8,128)(2,1)S(1)}, u32[]{:S(2)}, u32[]{:S(2)}) collective-permute-start(bf16[128,1024]{1,0:T(8,128)(2,1)S(1)} %fusion.37), channel_id=1, source_target_pairs={{0,8},{28,20},{4,4},{12,12},{16,16},{24,24},{1,9},{29,21},{5,5},{1... | collective-permute-start | bytes 786440 | tf_op jit(solution)/shard_map/ppermute | solution.py:201
  109.5 16.2 %collective-permute-start.36 = (bf16[128,1536]{1,0:T(8,128)(2,1)S(1)}, bf16[128,1536]{1,0:T(8,128)(2,1)S(1)}, u32[]{:S(2)}, u32[]{:S(2)}) collective-permute-start(bf16[128,1536]{1,0:T(8,128)(2,1)S(1)} %collective-permute-done.31), channel_id=1, source_target_pairs={{16,24},{12,4},{0,0},{8,8},{20,20},{28,28},{17,25},{13,5},{1,1},{9... | collective-permute-start | bytes 1179656 | tf_op jit(solution)/shard_map/ppermute | solution.py:201
  110.2 15.9 %collective-permute-start.35 = (bf16[128,1536]{1,0:T(8,128)(2,1)S(1)}, bf16[128,1536]{1,0:T(8,128)(2,1)S(1)}, u32[]{:S(2)}, u32[]{:S(2)}) collective-permute-start(bf16[128,1536]{1,0:T(8,128)(2,1)S(1)} %collective-permute-done.30), channel_id=1, source_target_pairs={{8,16},{20,12},{0,0},{4,4},{24,24},{28,28},{9,17},{21,13},{1,1},{5... | collective-permute-start | bytes 1179656 | tf_op jit(solution)/shard_map/ppermute | solution.py:201
  111.9 14.9 %collective-permute-start.34 = (bf16[128,1536]{1,0:T(8,128)(2,1)S(1)}, bf16[128,1536]{1,0:T(8,128)(2,1)S(1)}, u32[]{:S(2)}, u32[]{:S(2)}) collective-permute-start(bf16[128,1536]{1,0:T(8,128)(2,1)S(1)} %select_select_fusion.2.refs_0_), channel_id=1, source_target_pairs={{0,4},{4,0},{8,12},{12,8},{16,20},{20,16},{24,28},{28,24},{1,5},{5... | collective-permute-start | bytes 1179656 | tf_op jit(solution)/shard_map/ppermute | solution.py:197
  112.6 18.2 %collective-permute-start.33 = (bf16[128,1024]{1,0:T(8,128)(2,1)S(1)}, bf16[128,1024]{1,0:T(8,128)(2,1)S(1)}, u32[]{:S(2)}, u32[]{:S(2)}) collective-permute-start(bf16[128,1024]{1,0:T(8,128)(2,1)S(1)} %collective-permute-done.28), channel_id=1, source_target_pairs={{16,24},{12,4},{0,0},{8,8},{20,20},{28,28},{17,25},{13,5},{1,1},{9... | collective-permute-start | bytes 786440 | tf_op jit(solution)/shard_map/ppermute | solution.py:201
  115.2 17.0 %collective-permute-start.32 = (bf16[128,1024]{1,0:T(8,128)(2,1)S(1)}, bf16[128,1024]{1,0:T(8,128)(2,1)S(1)}, u32[]{:S(2)}, u32[]{:S(2)}) collective-permute-start(bf16[128,1024]{1,0:T(8,128)(2,1)S(1)} %collective-permute-done.27), channel_id=1, source_target_pairs={{8,16},{20,12},{0,0},{4,4},{24,24},{28,28},{9,17},{21,13},{1,1},{5... | collective-permute-start | bytes 786440 | tf_op jit(solution)/shard_map/ppermute | solution.py:201
  126.1 6.8 %collective-permute-start.40 = (bf16[128,1536]{1,0:T(8,128)(2,1)S(1)}, bf16[128,1536]{1,0:T(8,128)(2,1)S(1)}, u32[]{:S(2)}, u32[]{:S(2)}) collective-permute-start(bf16[128,1536]{1,0:T(8,128)(2,1)S(1)} %select_select_fusion.1.refs_0_), channel_id=1, source_target_pairs={{0,4},{4,0},{8,12},{12,8},{16,20},{20,16},{24,28},{28,24},{1,5},{5... | collective-permute-start | bytes 1179656 | tf_op jit(solution)/shard_map/ppermute | solution.py:197
  126.2 10.6 %collective-permute-start.39 = (bf16[128,1536]{1,0:T(8,128)(2,1)S(1)}, bf16[128,1536]{1,0:T(8,128)(2,1)S(1)}, u32[]{:S(2)}, u32[]{:S(2)}) collective-permute-start(bf16[128,1536]{1,0:T(8,128)(2,1)S(1)} %collective-permute-done.35), channel_id=1, source_target_pairs={{16,24},{12,4},{0,0},{8,8},{20,20},{28,28},{17,25},{13,5},{1,1},{9... | collective-permute-start | bytes 1179656 | tf_op jit(solution)/shard_map/ppermute | solution.py:201
  131.0 6.8 %collective-permute-start.38 = (bf16[128,1024]{1,0:T(8,128)(2,1)S(1)}, bf16[128,1024]{1,0:T(8,128)(2,1)S(1)}, u32[]{:S(2)}, u32[]{:S(2)}) collective-permute-start(bf16[128,1024]{1,0:T(8,128)(2,1)S(1)} %select_select_fusion.4.refs_0_), channel_id=1, source_target_pairs={{0,4},{4,0},{8,12},{12,8},{16,20},{20,16},{24,28},{28,24},{1,5},{5... | collective-permute-start | bytes 786440 | tf_op jit(solution)/shard_map/ppermute | solution.py:197
  132.2 8.9 %collective-permute-start.37 = (bf16[128,1024]{1,0:T(8,128)(2,1)S(1)}, bf16[128,1024]{1,0:T(8,128)(2,1)S(1)}, u32[]{:S(2)}, u32[]{:S(2)}) collective-permute-start(bf16[128,1024]{1,0:T(8,128)(2,1)S(1)} %collective-permute-done.32), channel_id=1, source_target_pairs={{16,24},{12,4},{0,0},{8,8},{20,20},{28,28},{17,25},{13,5},{1,1},{9... | collective-permute-start | bytes 786440 | tf_op jit(solution)/shard_map/ppermute | solution.py:201
  137.2 4.4 %collective-permute-start.42 = (bf16[128,1536]{1,0:T(8,128)(2,1)S(1)}, bf16[128,1536]{1,0:T(8,128)(2,1)S(1)}, u32[]{:S(2)}, u32[]{:S(2)}) collective-permute-start(bf16[128,1536]{1,0:T(8,128)(2,1)S(1)} %select_select_fusion.refs_0_), channel_id=1, source_target_pairs={{0,4},{4,0},{8,12},{12,8},{16,20},{20,16},{24,28},{28,24},{1,5},{5... | collective-permute-start | bytes 1179656 | tf_op jit(solution)/shard_map/ppermute | solution.py:197
  141.4 4.1 %collective-permute-start.41 = (bf16[128,1024]{1,0:T(8,128)(2,1)S(1)}, bf16[128,1024]{1,0:T(8,128)(2,1)S(1)}, u32[]{:S(2)}, u32[]{:S(2)}) collective-permute-start(bf16[128,1024]{1,0:T(8,128)(2,1)S(1)} %select_select_fusion.3.refs_0_), channel_id=1, source_target_pairs={{0,4},{4,0},{8,12},{12,8},{16,20},{20,16},{24,28},{28,24},{1,5},{5... | collective-permute-start | bytes 786440 | tf_op jit(solution)/shard_map/ppermute | solution.py:197
  148.8 8.5 %collective-permute-start.45 = (bf16[64,2048]{1,0:T(8,128)(2,1)S(1)}, bf16[64,2048]{1,0:T(8,128)(2,1)S(1)}, u32[]{:S(2)}, u32[]{:S(2)}) collective-permute-start(bf16[64,2048]{1,0:T(8,128)(2,1)S(1)} %get-tuple-element.176), channel_id=1, source_target_pairs={{0,3},{1,2},{2,1},{3,0},{4,7},{5,6},{6,5},{7,4},{8,11},{9,10},{10,... | collective-permute-start | bytes 786440 | tf_op jit(solution)/shard_map/ppermute | solution.py:222
  150.3 13.5 %collective-permute-start.44 = (bf16[64,2048]{1,0:T(8,128)(2,1)S(1)}, bf16[64,2048]{1,0:T(8,128)(2,1)S(1)}, u32[]{:S(2)}, u32[]{:S(2)}) collective-permute-start(bf16[64,2048]{1,0:T(8,128)(2,1)S(1)} %get-tuple-element.177), channel_id=1, source_target_pairs={{0,2},{1,3},{2,0},{3,1},{4,6},{5,7},{6,4},{7,5},{8,10},{9,11},{10,... | collective-permute-start | bytes 786440 | tf_op jit(solution)/shard_map/ppermute | solution.py:222
  151.3 12.5 %collective-permute-start.43 = (bf16[64,2048]{1,0:T(8,128)(2,1)S(1)}, bf16[64,2048]{1,0:T(8,128)(2,1)}, u32[]{:S(2)}, u32[]{:S(2)}) collective-permute-start(bf16[64,2048]{1,0:T(8,128)(2,1)S(1)} %get-tuple-element.175), channel_id=1, source_target_pairs={{0,1},{1,0},{2,3},{3,2},{4,5},{5,4},{6,7},{7,6},{8,9},{9,8},{10,11... | collective-permute-start | bytes 786440 | tf_op jit(solution)/shard_map/ppermute | solution.py:222

commit v3 on v2

--- a/solution.py
+++ b/solution.py
@@ -11,7 +11,7 @@
 CORES = 2
 TOKEN_MAX = 6.0
 WEIGHT_MAX = 0.046875
-VMEM = 20 * 1024 * 1024
+VMEM = 14 * 1024 * 1024
 PIECES = 2
 SIZES = [3, 3, 2, 3, 2]
 GAPS = [0, 1, 1, 2]

time: 166 us -> 167 us (level)
  no operation moved by 1% of the time
where the time goes in v3:
time: 167 us; the launch traced here: 166 us
  starting transfers between devices  63.8 us (38%)
  Pallas kernels  47.3 us (28%)
  waiting for transfers between devices  36.2 us (22%)
  other arithmetic  17.3 us (10%)
    ppermute x30, starting transfers between devices, hop(): return lax.ppermute(v, 'gx', pairs + [(i, i) for i in sorted(idle)])  50.9 us
    pallas_call x5, Pallas kernels, first(): pl.pallas_call(kernel, in_specs=[vmem, hbm, hbm], out_specs=[vmem, vmem],...  29.2 us
    ppermute x6, waiting for transfers between devices, across(): return lax.ppermute(v, 'gy', [(i, i ^ shift) for i in range(n_gy)])  24.5 us
    pallas_call x5, Pallas kernels, second(): pl.pallas_call(kernel, in_specs=[vmem, vmem, hbm] + ([vmem] if carried el...  18.1 us
    ppermute x30, waiting for transfers between devices, hop(): return lax.ppermute(v, 'gx', pairs + [(i, i) for i in sorted(idle)])  11.7 us
    convert_element_type x15, other arithmetic, encode(): return (v * root * scale).astype(jnp.float16)  10.4 us
    ppermute x10, starting transfers between devices, swap(): return lax.ppermute(v, 'gx', [(i, i ^ 1) for i in range(n_gx)])  7.46 us
    ppermute x6, starting transfers between devices, across(): return lax.ppermute(v, 'gy', [(i, i ^ shift) for i in range(n_gy)])  5.36 us
  transfers between devices with their start and end apart: 46, of which 9 were waited for; matrix products, arithmetic and copies ran while one was open for 9% of the time, Pallas kernels for 22%

profile of v3, /device:TPU:17, one launch (start us, length us, event | category | flops | bytes accessed | tf_op | source)
XLA Modules:
  0.0 165.7 jit_solution(11658009923110969622)
XLA Ops:
  0.0 2.2 %collective-permute-start.2 = (bf16[64,2048]{1,0:T(8,128)(2,1)}, bf16[64,2048]{1,0:T(8,128)(2,1)S(1)}, u32[]{:S(2)}, u32[]{:S(2)}) collective-permute-start(bf16[64,2048]{1,0:T(8,128)(2,1)} %param.4), channel_id=1, source_target_pairs={{0,3},{1,2},{2,1},{3,0},{4,7},{5,6},{6,5},{7,4},{8,11},{9,10},{10,... | collective-permute-start | bytes 786440 | tf_op jit(solution)/shard_map/ppermute | solution.py:222
  2.7 5.7 %collective-permute-done.2 = bf16[64,2048]{1,0:T(8,128)(2,1)S(1)} collective-permute-done((bf16[64,2048]{1,0:T(8,128)(2,1)}, bf16[64,2048]{1,0:T(8,128)(2,1)S(1)}, u32[]{:S(2)}, u32[]{:S(2)}) %collective-permute-start.2) | collective-permute-done | bytes 262176 | tf_op jit(solution)/shard_map/ppermute | solution.py:222
  8.3 6.6 %collective-permute-done.1 = bf16[64,2048]{1,0:T(8,128)(2,1)S(1)} collective-permute-done((bf16[64,2048]{1,0:T(8,128)(2,1)}, bf16[64,2048]{1,0:T(8,128)(2,1)S(1)}, u32[]{:S(2)}, u32[]{:S(2)}) %collective-permute-start.1) | collective-permute-done | bytes 262176 | tf_op jit(solution)/shard_map/ppermute | solution.py:222
  15.0 1.1 pad_maximum_fusion
  16.3 7.1 %shard_map.46 = (f32[2,128,1536]{2,1,0:T(8,128)}, f32[2,128,1536]{2,1,0:T(8,128)S(1)}) custom-call(bf16[256,2048]{1,0:T(8,128)(2,1)S(1)} %pad_maximum_fusion.1.rows_ref, bf16[2048,6656]{1,0:T(8,128)(2,1)} %gate_ref.9, bf16[2048,6656]{1,0:T(8,128)(2,1)} %up_ref.9), custom_call_target="tpu_custom_call" | custom-call | flops 3221225472 | bytes 15728640 | tf_op jit(solution)/shard_map/pallas_call | solution.py:67
  24.0 7.1 %shard_map.47 = (f32[2,128,1536]{2,1,0:T(8,128)}, f32[2,128,1536]{2,1,0:T(8,128)S(1)}) custom-call(bf16[256,2048]{1,0:T(8,128)(2,1)S(1)} %pad_maximum_fusion.1.rows_ref, bf16[2048,6656]{1,0:T(8,128)(2,1)} %gate_ref.9, bf16[2048,6656]{1,0:T(8,128)(2,1)} %up_ref.9), custom_call_target="tpu_custom_call" | custom-call | flops 3221225472 | bytes 15728640 | tf_op jit(solution)/shard_map/pallas_call | solution.py:67
  31.7 2.3 %multiply_convert_fusion.8 = (f16[2,128,1536]{2,1,0:T(8,128)(2,1)S(1)}, f32[2,128,1536]{2,1,0:T(8,128)S(1)}) fusion(f32[2,128,1536]{2,1,0:T(8,128)} %copy-done, f32[2,128,1536]{2,1,0:T(8,128)} %collective-permute-done.3), kind=kLoop, calls=%fused_computation.41 | loop fusion | flops 2359296 | bytes 5505024 | tf_op jit(solution)/shard_map/convert_element_type | solution.py:22
  34.8 4.5 %shard_map.48 = (f32[2,128,1024]{2,1,0:T(8,128)S(1)}, f32[2,128,1024]{2,1,0:T(8,128)S(1)}) custom-call(bf16[256,2048]{1,0:T(8,128)(2,1)S(1)} %pad_maximum_fusion.1.rows_ref, bf16[2048,6656]{1,0:T(8,128)(2,1)} %gate_ref.9, bf16[2048,6656]{1,0:T(8,128)(2,1)} %up_ref.9), custom_call_target="tpu_custom_call" | custom-call | flops 2147483648 | bytes 10485760 | tf_op jit(solution)/shard_map/pallas_call | solution.py:67
  40.0 1.8 %multiply_convert_fusion.7 = (f16[2,128,1536]{2,1,0:T(8,128)(2,1)S(1)}, f32[2,128,1536]{2,1,0:T(8,128)S(1)}) fusion(f32[2,128,1536]{2,1,0:T(8,128)S(1)} %get-tuple-element.96, f32[2,128,1536]{2,1,0:T(8,128)} %collective-permute-done.6), kind=kLoop, calls=%fused_computation.40 | loop fusion | flops 2359296 | bytes 5505024 | tf_op jit(solution)/shard_map/convert_element_type | solution.py:22
  42.5 6.0 %shard_map.49 = (f32[2,128,1536]{2,1,0:T(8,128)S(1)}, f32[2,128,1536]{2,1,0:T(8,128)S(1)}) custom-call(bf16[256,2048]{1,0:T(8,128)(2,1)S(1)} %pad_maximum_fusion.1.rows_ref, bf16[2048,6656]{1,0:T(8,128)(2,1)} %gate_ref.9, bf16[2048,6656]{1,0:T(8,128)(2,1)} %up_ref.9), custom_call_target="tpu_custom_call" | custom-call | flops 3221225472 | bytes 15728640 | tf_op jit(solution)/shard_map/pallas_call | solution.py:67
  49.8 1.3 collective-permute-start.9
  51.4 0.9 collective-permute-start.8
  52.3 4.5 %shard_map.50 = (f32[2,128,1024]{2,1,0:T(8,128)S(1)}, f32[2,128,1024]{2,1,0:T(8,128)S(1)}) custom-call(bf16[256,2048]{1,0:T(8,128)(2,1)S(1)} %pad_maximum_fusion.1.rows_ref, bf16[2048,6656]{1,0:T(8,128)(2,1)} %gate_ref.9, bf16[2048,6656]{1,0:T(8,128)(2,1)} %up_ref.9), custom_call_target="tpu_custom_call" | custom-call | flops 2147483648 | bytes 10485760 | tf_op jit(solution)/shard_map/pallas_call | solution.py:67
  56.8 2.2 %collective-permute-start.7 = (f32[2,128,1024]{2,1,0:T(8,128)S(1)}, f32[2,128,1024]{2,1,0:T(8,128)S(1)}, u32[]{:S(2)}, u32[]{:S(2)}) collective-permute-start(f32[2,128,1024]{2,1,0:T(8,128)S(1)} %get-tuple-element.106), channel_id=1, source_target_pairs={{0,4},{4,0},{8,12},{12,8},{16,20},{20,16},{24,28},{28,24},{1,5},{5... | collective-permute-start | bytes 3145736 | tf_op jit(solution)/shard_map/ppermute | solution.py:197
  59.7 1.3 collective-permute-start.16
  63.4 3.1 %collective-permute-start.14 = (f16[2,128,1536]{2,1,0:T(8,128)(2,1)S(1)}, f16[2,128,1536]{2,1,0:T(8,128)(2,1)S(1)}, u32[]{:S(2)}, u32[]{:S(2)}) collective-permute-start(f16[2,128,1536]{2,1,0:T(8,128)(2,1)S(1)} %multiply_convert_fusion.3), channel_id=1, source_target_pairs={{8,0},{20,28},{4,4},{12,12},{16,16},{24,24},{9,1},{21,29},{5,5},{1... | collective-permute-start | bytes 2359304 | tf_op jit(solution)/shard_map/ppermute | solution.py:201
  66.9 1.3 collective-permute-start.13
  69.3 3.4 %collective-permute-done.16 = f16[2,128,1536]{2,1,0:T(8,128)(2,1)S(1)} collective-permute-done((f16[2,128,1536]{2,1,0:T(8,128)(2,1)S(1)}, f16[2,128,1536]{2,1,0:T(8,128)(2,1)S(1)}, u32[]{:S(2)}, u32[]{:S(2)}) %collective-permute-start.16) | collective-permute-done | bytes 786464 | tf_op jit(solution)/shard_map/ppermute | solution.py:201
  73.3 1.3 collective-permute-start.21
  75.3 1.3 collective-permute-start.20
  77.1 1.3 collective-permute-start.19
  78.8 4.0 %collective-permute-start.18 = (f16[2,128,1024]{2,1,0:T(8,128)(2,1)S(1)}, f16[2,128,1024]{2,1,0:T(8,128)(2,1)S(1)}, u32[]{:S(2)}, u32[]{:S(2)}) collective-permute-start(f16[2,128,1024]{2,1,0:T(8,128)(2,1)S(1)} %multiply_convert_fusion.11), channel_id=1, source_target_pairs={{8,0},{20,28},{4,4},{12,12},{16,16},{24,24},{9,1},{21,29},{5,5},{1... | collective-permute-start | bytes 1572872 | tf_op jit(solution)/shard_map/ppermute | solution.py:201
  83.3 1.3 collective-permute-start.17
  85.1 1.3 collective-permute-start.26
  86.4 1.6 collective-permute-done.20
  88.6 2.5 %collective-permute-start.25 = (f16[2,128,1536]{2,1,0:T(8,128)(2,1)S(1)}, f16[2,128,1536]{2,1,0:T(8,128)(2,1)S(1)}, u32[]{:S(2)}, u32[]{:S(2)}) collective-permute-start(f16[2,128,1536]{2,1,0:T(8,128)(2,1)S(1)} %multiply_convert_fusion), channel_id=1, source_target_pairs={{8,0},{20,28},{4,4},{12,12},{16,16},{24,24},{9,1},{21,29},{5,5},{1... | collective-permute-start | bytes 2359304 | tf_op jit(solution)/shard_map/ppermute | solution.py:201
  91.1 1.3 collective-permute-start.24
  92.8 1.3 collective-permute-start.23
  94.5 4.0 %collective-permute-start.22 = (f16[2,128,1024]{2,1,0:T(8,128)(2,1)S(1)}, f16[2,128,1024]{2,1,0:T(8,128)(2,1)S(1)}, u32[]{:S(2)}, u32[]{:S(2)}) collective-permute-start(f16[2,128,1024]{2,1,0:T(8,128)(2,1)S(1)} %multiply_convert_fusion.9), channel_id=1, source_target_pairs={{8,0},{20,28},{4,4},{12,12},{16,16},{24,24},{9,1},{21,29},{5,5},{1... | collective-permute-start | bytes 1572872 | tf_op jit(solution)/shard_map/ppermute | solution.py:201
  98.5 1.3 collective-permute-start.31
  100.5 1.3 collective-permute-start.30
  102.5 1.3 collective-permute-start.28
  103.8 3.8 %collective-permute-done.22 = f16[2,128,1024]{2,1,0:T(8,128)(2,1)S(1)} collective-permute-done((f16[2,128,1024]{2,1,0:T(8,128)(2,1)S(1)}, f16[2,128,1024]{2,1,0:T(8,128)(2,1)S(1)}, u32[]{:S(2)}, u32[]{:S(2)}) %collective-permute-start.22) | collective-permute-done | bytes 524320 | tf_op jit(solution)/shard_map/ppermute | solution.py:201
  108.0 1.5 collective-permute-start.27
  110.3 1.3 collective-permute-start.35
  113.2 2.0 %collective-permute-done.27 = bf16[128,1024]{1,0:T(8,128)(2,1)S(1)} collective-permute-done((bf16[128,1024]{1,0:T(8,128)(2,1)S(1)}, bf16[128,1024]{1,0:T(8,128)(2,1)S(1)}, u32[]{:S(2)}, u32[]{:S(2)}) %collective-permute-start.27) | collective-permute-done | bytes 262176 | tf_op jit(solution)/shard_map/ppermute | solution.py:201
  115.3 10.5 %collective-permute-start.32 = (bf16[128,1024]{1,0:T(8,128)(2,1)S(1)}, bf16[128,1024]{1,0:T(8,128)(2,1)S(1)}, u32[]{:S(2)}, u32[]{:S(2)}) collective-permute-start(bf16[128,1024]{1,0:T(8,128)(2,1)S(1)} %collective-permute-done.27), channel_id=1, source_target_pairs={{8,16},{20,12},{0,0},{4,4},{24,24},{28,28},{9,17},{21,13},{1,1},{5... | collective-permute-start | bytes 786440 | tf_op jit(solution)/shard_map/ppermute | solution.py:201
  126.9 3.9 %shard_map.51.refs_3_ = f32[256,2048]{1,0:T(8,128)S(1)} custom-call(bf16[128,1536]{1,0:T(8,128)(2,1)S(1)} %select_select_fusion.2.refs_0_, bf16[128,1536]{1,0:T(8,128)(2,1)S(1)} %collective-permute-done.34.refs_1_, bf16[6656,2048]{1,0:T(8,128)(2,1)} %refs_2_.9), custom_call_target="tpu_custom_call" | custom-call | flops 1610612736 | bytes 10485760 | tf_op jit(solution)/shard_map/pallas_call | solution.py:126
  131.1 1.2 collective-permute-start.38
  132.9 3.9 %shard_map.52.refs_3_ = f32[256,2048]{1,0:T(8,128)S(1)} custom-call(bf16[128,1536]{1,0:T(8,128)(2,1)S(1)} %select_select_fusion.1.refs_0_, bf16[128,1536]{1,0:T(8,128)(2,1)S(1)} %collective-permute-done.40.refs_1_, bf16[6656,2048]{1,0:T(8,128)(2,1)} %refs_2_.9, f32[256,2048]{1,0:T(8,128)S(1)} %shard_map.51.refs_3_), custom_call_target="tpu_custom_call" | custom-call | flops 1610612736 | bytes 10485760 | tf_op jit(solution)/shard_map/pallas_call | solution.py:126
  137.9 3.2 %shard_map.53.refs_3_ = f32[256,2048]{1,0:T(8,128)S(1)} custom-call(bf16[128,1024]{1,0:T(8,128)(2,1)S(1)} %select_select_fusion.4.refs_0_, bf16[128,1024]{1,0:T(8,128)(2,1)S(1)} %collective-permute-done.38.refs_1_, bf16[6656,2048]{1,0:T(8,128)(2,1)} %refs_2_.9, f32[256,2048]{1,0:T(8,128)S(1)} %shard_map.52.refs_3_), custom_call_target="tpu_custom_call" | custom-call | flops 1073741824 | bytes 8388608 | tf_op jit(solution)/shard_map/pallas_call | solution.py:126
  141.7 3.9 %shard_map.54.refs_3_ = f32[256,2048]{1,0:T(8,128)S(1)} custom-call(bf16[128,1536]{1,0:T(8,128)(2,1)S(1)} %select_select_fusion.refs_0_, bf16[128,1536]{1,0:T(8,128)(2,1)S(1)} %collective-permute-done.42.refs_1_, bf16[6656,2048]{1,0:T(8,128)(2,1)} %refs_2_.9, f32[256,2048]{1,0:T(8,128)S(1)} %shard_map.53.refs_3_), custom_call_target="tpu_custom_call" | custom-call | flops 1610612736 | bytes 10485760 | tf_op jit(solution)/shard_map/pallas_call | solution.py:126
  145.6 3.2 %shard_map.55 = f32[256,2048]{1,0:T(8,128)S(1)} custom-call(bf16[128,1024]{1,0:T(8,128)(2,1)S(1)} %select_select_fusion.3.refs_0_, bf16[128,1024]{1,0:T(8,128)(2,1)S(1)} %collective-permute-done.41.refs_1_, bf16[6656,2048]{1,0:T(8,128)(2,1)} %refs_2_.9, f32[256,2048]{1,0:T(8,128)S(1)} %shard_map.54.refs_3_), custom_call_target="tpu_custom_call" | custom-call | flops 1073741824 | bytes 8388608 | tf_op jit(solution)/shard_map/pallas_call | solution.py:126
  148.9 1.4 collective-permute-start.45
  150.3 1.0 collective-permute-start.44
  151.6 5.8 %collective-permute-done.45 = bf16[64,2048]{1,0:T(8,128)(2,1)S(1)} collective-permute-done((bf16[64,2048]{1,0:T(8,128)(2,1)S(1)}, bf16[64,2048]{1,0:T(8,128)(2,1)S(1)}, u32[]{:S(2)}, u32[]{:S(2)}) %collective-permute-start.45) | collective-permute-done | bytes 262176 | tf_op jit(solution)/shard_map/ppermute | solution.py:222
  157.4 6.4 %collective-permute-done.44 = bf16[64,2048]{1,0:T(8,128)(2,1)S(1)} collective-permute-done((bf16[64,2048]{1,0:T(8,128)(2,1)S(1)}, bf16[64,2048]{1,0:T(8,128)(2,1)S(1)}, u32[]{:S(2)}, u32[]{:S(2)}) %collective-permute-start.44) | collective-permute-done | bytes 262176 | tf_op jit(solution)/shard_map/ppermute | solution.py:222
  163.8 1.9 %convert_add_fusion = f32[64,2048]{1,0:T(8,128)} fusion(bf16[64,2048]{1,0:T(8,128)(2,1)S(1)} %collective-permute-done.45, bf16[64,2048]{1,0:T(8,128)(2,1)S(1)} %collective-permute-done.44, bf16[64,2048]{1,0:T(8,128)(2,1)} %collective-permute-done.43, f32[256,2048]{1,0:T(8,128)S(1)} %shard_map.55, s32[]{:T(128)S(6)} %select_n.173), kind=kLoop, calls=%fused_computation.82 | loop fusion | flops 786432 | bytes 1835012 | tf_op jit(solution)/shard_map/add | solution.py:313
  (91 shorter events, 22.3 us)
Async XLA Ops:
  0.0 8.3 %collective-permute-start.2 = (bf16[64,2048]{1,0:T(8,128)(2,1)}, bf16[64,2048]{1,0:T(8,128)(2,1)S(1)}, u32[]{:S(2)}, u32[]{:S(2)}) collective-permute-start(bf16[64,2048]{1,0:T(8,128)(2,1)} %param.4), channel_id=1, source_target_pairs={{0,3},{1,2},{2,1},{3,0},{4,7},{5,6},{6,5},{7,4},{8,11},{9,10},{10,... | collective-permute-start | bytes 786440 | tf_op jit(solution)/shard_map/ppermute | solution.py:222
  2.2 12.8 %collective-permute-start.1 = (bf16[64,2048]{1,0:T(8,128)(2,1)}, bf16[64,2048]{1,0:T(8,128)(2,1)S(1)}, u32[]{:S(2)}, u32[]{:S(2)}) collective-permute-start(bf16[64,2048]{1,0:T(8,128)(2,1)} %param.4), channel_id=1, source_target_pairs={{0,2},{1,3},{2,0},{3,1},{4,6},{5,7},{6,4},{7,5},{8,10},{9,11},{10,... | collective-permute-start | bytes 786440 | tf_op jit(solution)/shard_map/ppermute | solution.py:222
  2.4 12.6 %collective-permute-start = (bf16[64,2048]{1,0:T(8,128)(2,1)}, bf16[64,2048]{1,0:T(8,128)(2,1)S(1)}, u32[]{:S(2)}, u32[]{:S(2)}) collective-permute-start(bf16[64,2048]{1,0:T(8,128)(2,1)} %param.4), channel_id=1, source_target_pairs={{0,1},{1,0},{2,3},{3,2},{4,5},{5,4},{6,7},{7,6},{8,9},{9,8},{10,11... | collective-permute-start | bytes 786440 | tf_op jit(solution)/shard_map/ppermute | solution.py:222
  23.4 7.8 %copy-start = (f32[2,128,1536]{2,1,0:T(8,128)}, f32[2,128,1536]{2,1,0:T(8,128)S(1)}, u32[]{:S(2)}) copy-start(f32[2,128,1536]{2,1,0:T(8,128)S(1)} %get-tuple-element.90) | copy-start | bytes 4718596
  23.4 8.3 %collective-permute-start.3 = (f32[2,128,1536]{2,1,0:T(8,128)}, f32[2,128,1536]{2,1,0:T(8,128)}, u32[]{:S(2)}, u32[]{:S(2)}) collective-permute-start(f32[2,128,1536]{2,1,0:T(8,128)} %get-tuple-element.87), channel_id=1, source_target_pairs={{0,4},{4,0},{8,12},{12,8},{16,20},{20,16},{24,28},{28,24},{1,5},{5... | collective-permute-start | bytes 4718600 | tf_op jit(solution)/shard_map/ppermute | solution.py:197
  31.2 8.8 %collective-permute-start.6 = (f32[2,128,1536]{2,1,0:T(8,128)}, f32[2,128,1536]{2,1,0:T(8,128)}, u32[]{:S(2)}, u32[]{:S(2)}) collective-permute-start(f32[2,128,1536]{2,1,0:T(8,128)} %get-tuple-element.95), channel_id=1, source_target_pairs={{0,4},{4,0},{8,12},{12,8},{16,20},{20,16},{24,28},{28,24},{1,5},{5... | collective-permute-start | bytes 4718600 | tf_op jit(solution)/shard_map/ppermute | solution.py:197
  34.0 15.1 %collective-permute-start.5 = (f16[2,128,1536]{2,1,0:T(8,128)(2,1)S(1)}, f16[2,128,1536]{2,1,0:T(8,128)(2,1)S(1)}, u32[]{:S(2)}, u32[]{:S(2)}) collective-permute-start(f16[2,128,1536]{2,1,0:T(8,128)(2,1)S(1)} %get-tuple-element.173), channel_id=1, source_target_pairs={{24,16},{4,12},{0,0},{8,8},{20,20},{28,28},{25,17},{5,13},{1,1},{9... | collective-permute-start | bytes 2359304 | tf_op jit(solution)/shard_map/ppermute | solution.py:201
  39.3 11.8 %collective-permute-start.4 = (f32[2,128,1024]{2,1,0:T(8,128)S(1)}, f32[2,128,1024]{2,1,0:T(8,128)S(1)}, u32[]{:S(2)}, u32[]{:S(2)}) collective-permute-start(f32[2,128,1024]{2,1,0:T(8,128)S(1)} %get-tuple-element.94), channel_id=1, source_target_pairs={{0,4},{4,0},{8,12},{12,8},{16,20},{20,16},{24,28},{28,24},{1,5},{5... | collective-permute-start | bytes 3145736 | tf_op jit(solution)/shard_map/ppermute | solution.py:197
  41.8 17.3 %collective-permute-start.11 = (f16[2,128,1536]{2,1,0:T(8,128)(2,1)S(1)}, f16[2,128,1536]{2,1,0:T(8,128)(2,1)S(1)}, u32[]{:S(2)}, u32[]{:S(2)}) collective-permute-start(f16[2,128,1536]{2,1,0:T(8,128)(2,1)S(1)} %get-tuple-element.171), channel_id=1, source_target_pairs={{24,16},{4,12},{0,0},{8,8},{20,20},{28,28},{25,17},{5,13},{1,1},{9... | collective-permute-start | bytes 2359304 | tf_op jit(solution)/shard_map/ppermute | solution.py:201
  48.5 12.5 %collective-permute-start.10 = (f32[2,128,1536]{2,1,0:T(8,128)S(1)}, f32[2,128,1536]{2,1,0:T(8,128)S(1)}, u32[]{:S(2)}, u32[]{:S(2)}) collective-permute-start(f32[2,128,1536]{2,1,0:T(8,128)S(1)} %get-tuple-element.107), channel_id=1, source_target_pairs={{0,4},{4,0},{8,12},{12,8},{16,20},{20,16},{24,28},{28,24},{1,5},{5... | collective-permute-start | bytes 4718600 | tf_op jit(solution)/shard_map/ppermute | solution.py:197
  49.8 13.0 %collective-permute-start.9 = (f16[2,128,1536]{2,1,0:T(8,128)(2,1)S(1)}, f16[2,128,1536]{2,1,0:T(8,128)(2,1)S(1)}, u32[]{:S(2)}, u32[]{:S(2)}) collective-permute-start(f16[2,128,1536]{2,1,0:T(8,128)(2,1)S(1)} %multiply_convert_fusion.6), channel_id=1, source_target_pairs={{16,8},{12,20},{0,0},{4,4},{24,24},{28,28},{17,9},{13,21},{1,1},{5... | collective-permute-start | bytes 2359304 | tf_op jit(solution)/shard_map/ppermute | solution.py:201
  51.4 15.1 %collective-permute-start.8 = (f16[2,128,1024]{2,1,0:T(8,128)(2,1)S(1)}, f16[2,128,1024]{2,1,0:T(8,128)(2,1)S(1)}, u32[]{:S(2)}, u32[]{:S(2)}) collective-permute-start(f16[2,128,1024]{2,1,0:T(8,128)(2,1)S(1)} %get-tuple-element.169), channel_id=1, source_target_pairs={{24,16},{4,12},{0,0},{8,8},{20,20},{28,28},{25,17},{5,13},{1,1},{9... | collective-permute-start | bytes 1572872 | tf_op jit(solution)/shard_map/ppermute | solution.py:201
  56.8 11.4 %collective-permute-start.7 = (f32[2,128,1024]{2,1,0:T(8,128)S(1)}, f32[2,128,1024]{2,1,0:T(8,128)S(1)}, u32[]{:S(2)}, u32[]{:S(2)}) collective-permute-start(f32[2,128,1024]{2,1,0:T(8,128)S(1)} %get-tuple-element.106), channel_id=1, source_target_pairs={{0,4},{4,0},{8,12},{12,8},{16,20},{20,16},{24,28},{28,24},{1,5},{5... | collective-permute-start | bytes 3145736 | tf_op jit(solution)/shard_map/ppermute | solution.py:197
  59.7 13.0 %collective-permute-start.16 = (f16[2,128,1536]{2,1,0:T(8,128)(2,1)S(1)}, f16[2,128,1536]{2,1,0:T(8,128)(2,1)S(1)}, u32[]{:S(2)}, u32[]{:S(2)}) collective-permute-start(f16[2,128,1536]{2,1,0:T(8,128)(2,1)S(1)} %multiply_convert_fusion.5), channel_id=1, source_target_pairs={{16,8},{12,20},{0,0},{4,4},{24,24},{28,28},{17,9},{13,21},{1,1},{5... | collective-permute-start | bytes 2359304 | tf_op jit(solution)/shard_map/ppermute | solution.py:201
  61.4 13.2 %collective-permute-start.15 = (f16[2,128,1536]{2,1,0:T(8,128)(2,1)S(1)}, f16[2,128,1536]{2,1,0:T(8,128)(2,1)S(1)}, u32[]{:S(2)}, u32[]{:S(2)}) collective-permute-start(f16[2,128,1536]{2,1,0:T(8,128)(2,1)S(1)} %get-tuple-element.167), channel_id=1, source_target_pairs={{24,16},{4,12},{0,0},{8,8},{20,20},{28,28},{25,17},{5,13},{1,1},{9... | collective-permute-start | bytes 2359304 | tf_op jit(solution)/shard_map/ppermute | solution.py:201
  63.4 13.2 %collective-permute-start.14 = (f16[2,128,1536]{2,1,0:T(8,128)(2,1)S(1)}, f16[2,128,1536]{2,1,0:T(8,128)(2,1)S(1)}, u32[]{:S(2)}, u32[]{:S(2)}) collective-permute-start(f16[2,128,1536]{2,1,0:T(8,128)(2,1)S(1)} %multiply_convert_fusion.3), channel_id=1, source_target_pairs={{8,0},{20,28},{4,4},{12,12},{16,16},{24,24},{9,1},{21,29},{5,5},{1... | collective-permute-start | bytes 2359304 | tf_op jit(solution)/shard_map/ppermute | solution.py:201
  66.9 11.4 %collective-permute-start.13 = (f16[2,128,1024]{2,1,0:T(8,128)(2,1)S(1)}, f16[2,128,1024]{2,1,0:T(8,128)(2,1)S(1)}, u32[]{:S(2)}, u32[]{:S(2)}) collective-permute-start(f16[2,128,1024]{2,1,0:T(8,128)(2,1)S(1)} %multiply_convert_fusion.13), channel_id=1, source_target_pairs={{16,8},{12,20},{0,0},{4,4},{24,24},{28,28},{17,9},{13,21},{1,1},{5... | collective-permute-start | bytes 1572872 | tf_op jit(solution)/shard_map/ppermute | solution.py:201
  68.6 14.2 %collective-permute-start.12 = (f16[2,128,1024]{2,1,0:T(8,128)(2,1)S(1)}, f16[2,128,1024]{2,1,0:T(8,128)(2,1)S(1)}, u32[]{:S(2)}, u32[]{:S(2)}) collective-permute-start(f16[2,128,1024]{2,1,0:T(8,128)(2,1)S(1)} %get-tuple-element.165), channel_id=1, source_target_pairs={{24,16},{4,12},{0,0},{8,8},{20,20},{28,28},{25,17},{5,13},{1,1},{9... | collective-permute-start | bytes 1572872 | tf_op jit(solution)/shard_map/ppermute | solution.py:201
  73.3 11.3 %collective-permute-start.21 = (f16[2,128,1536]{2,1,0:T(8,128)(2,1)S(1)}, f16[2,128,1536]{2,1,0:T(8,128)(2,1)S(1)}, u32[]{:S(2)}, u32[]{:S(2)}) collective-permute-start(f16[2,128,1536]{2,1,0:T(8,128)(2,1)S(1)} %multiply_convert_fusion.2), channel_id=1, source_target_pairs={{8,0},{20,28},{4,4},{12,12},{16,16},{24,24},{9,1},{21,29},{5,5},{1... | collective-permute-start | bytes 2359304 | tf_op jit(solution)/shard_map/ppermute | solution.py:201
  75.3 12.7 %collective-permute-start.20 = (f16[2,128,1536]{2,1,0:T(8,128)(2,1)S(1)}, f16[2,128,1536]{2,1,0:T(8,128)(2,1)S(1)}, u32[]{:S(2)}, u32[]{:S(2)}) collective-permute-start(f16[2,128,1536]{2,1,0:T(8,128)(2,1)S(1)} %multiply_convert_fusion.1), channel_id=1, source_target_pairs={{16,8},{12,20},{0,0},{4,4},{24,24},{28,28},{17,9},{13,21},{1,1},{5... | collective-permute-start | bytes 2359304 | tf_op jit(solution)/shard_map/ppermute | solution.py:201
  77.1 14.0 %collective-permute-start.19 = (bf16[128,1536]{1,0:T(8,128)(2,1)S(1)}, bf16[128,1536]{1,0:T(8,128)(2,1)S(1)}, u32[]{:S(2)}, u32[]{:S(2)}) collective-permute-start(bf16[128,1536]{1,0:T(8,128)(2,1)S(1)} %fusion.35), channel_id=1, source_target_pairs={{0,8},{28,20},{4,4},{12,12},{16,16},{24,24},{1,9},{29,21},{5,5},{1... | collective-permute-start | bytes 1179656 | tf_op jit(solution)/shard_map/ppermute | solution.py:201
  78.8 13.6 %collective-permute-start.18 = (f16[2,128,1024]{2,1,0:T(8,128)(2,1)S(1)}, f16[2,128,1024]{2,1,0:T(8,128)(2,1)S(1)}, u32[]{:S(2)}, u32[]{:S(2)}) collective-permute-start(f16[2,128,1024]{2,1,0:T(8,128)(2,1)S(1)} %multiply_convert_fusion.11), channel_id=1, source_target_pairs={{8,0},{20,28},{4,4},{12,12},{16,16},{24,24},{9,1},{21,29},{5,5},{1... | collective-permute-start | bytes 1572872 | tf_op jit(solution)/shard_map/ppermute | solution.py:201
  83.3 10.8 %collective-permute-start.17 = (f16[2,128,1024]{2,1,0:T(8,128)(2,1)S(1)}, f16[2,128,1024]{2,1,0:T(8,128)(2,1)S(1)}, u32[]{:S(2)}, u32[]{:S(2)}) collective-permute-start(f16[2,128,1024]{2,1,0:T(8,128)(2,1)S(1)} %multiply_convert_fusion.10), channel_id=1, source_target_pairs={{16,8},{12,20},{0,0},{4,4},{24,24},{28,28},{17,9},{13,21},{1,1},{5... | collective-permute-start | bytes 1572872 | tf_op jit(solution)/shard_map/ppermute | solution.py:201
  85.1 13.5 %collective-permute-start.26 = (bf16[128,1536]{1,0:T(8,128)(2,1)S(1)}, bf16[128,1536]{1,0:T(8,128)(2,1)S(1)}, u32[]{:S(2)}, u32[]{:S(2)}) collective-permute-start(bf16[128,1536]{1,0:T(8,128)(2,1)S(1)} %fusion.33), channel_id=1, source_target_pairs={{0,8},{28,20},{4,4},{12,12},{16,16},{24,24},{1,9},{29,21},{5,5},{1... | collective-permute-start | bytes 1179656 | tf_op jit(solution)/shard_map/ppermute | solution.py:201
  88.6 11.3 %collective-permute-start.25 = (f16[2,128,1536]{2,1,0:T(8,128)(2,1)S(1)}, f16[2,128,1536]{2,1,0:T(8,128)(2,1)S(1)}, u32[]{:S(2)}, u32[]{:S(2)}) collective-permute-start(f16[2,128,1536]{2,1,0:T(8,128)(2,1)S(1)} %multiply_convert_fusion), channel_id=1, source_target_pairs={{8,0},{20,28},{4,4},{12,12},{16,16},{24,24},{9,1},{21,29},{5,5},{1... | collective-permute-start | bytes 2359304 | tf_op jit(solution)/shard_map/ppermute | solution.py:201
  91.1 10.7 %collective-permute-start.24 = (bf16[128,1536]{1,0:T(8,128)(2,1)S(1)}, bf16[128,1536]{1,0:T(8,128)(2,1)S(1)}, u32[]{:S(2)}, u32[]{:S(2)}) collective-permute-start(bf16[128,1536]{1,0:T(8,128)(2,1)S(1)} %collective-permute-done.19), channel_id=1, source_target_pairs={{8,16},{20,12},{0,0},{4,4},{24,24},{28,28},{9,17},{21,13},{1,1},{5... | collective-permute-start | bytes 1179656 | tf_op jit(solution)/shard_map/ppermute | solution.py:201
  92.8 9.7 %collective-permute-start.23 = (bf16[128,1024]{1,0:T(8,128)(2,1)S(1)}, bf16[128,1024]{1,0:T(8,128)(2,1)S(1)}, u32[]{:S(2)}, u32[]{:S(2)}) collective-permute-start(bf16[128,1024]{1,0:T(8,128)(2,1)S(1)} %fusion.39), channel_id=1, source_target_pairs={{0,8},{28,20},{4,4},{12,12},{16,16},{24,24},{1,9},{29,21},{5,5},{1... | collective-permute-start | bytes 786440 | tf_op jit(solution)/shard_map/ppermute | solution.py:201
  94.5 13.1 %collective-permute-start.22 = (f16[2,128,1024]{2,1,0:T(8,128)(2,1)S(1)}, f16[2,128,1024]{2,1,0:T(8,128)(2,1)S(1)}, u32[]{:S(2)}, u32[]{:S(2)}) collective-permute-start(f16[2,128,1024]{2,1,0:T(8,128)(2,1)S(1)} %multiply_convert_fusion.9), channel_id=1, source_target_pairs={{8,0},{20,28},{4,4},{12,12},{16,16},{24,24},{9,1},{21,29},{5,5},{1... | collective-permute-start | bytes 1572872 | tf_op jit(solution)/shard_map/ppermute | solution.py:201
  98.5 11.0 %collective-permute-start.31 = (bf16[128,1536]{1,0:T(8,128)(2,1)S(1)}, bf16[128,1536]{1,0:T(8,128)(2,1)S(1)}, u32[]{:S(2)}, u32[]{:S(2)}) collective-permute-start(bf16[128,1536]{1,0:T(8,128)(2,1)S(1)} %collective-permute-done.26), channel_id=1, source_target_pairs={{8,16},{20,12},{0,0},{4,4},{24,24},{28,28},{9,17},{21,13},{1,1},{5... | collective-permute-start | bytes 1179656 | tf_op jit(solution)/shard_map/ppermute | solution.py:201
  100.5 9.8 %collective-permute-start.30 = (bf16[128,1536]{1,0:T(8,128)(2,1)S(1)}, bf16[128,1536]{1,0:T(8,128)(2,1)S(1)}, u32[]{:S(2)}, u32[]{:S(2)}) collective-permute-start(bf16[128,1536]{1,0:T(8,128)(2,1)S(1)} %fusion.31), channel_id=1, source_target_pairs={{0,8},{28,20},{4,4},{12,12},{16,16},{24,24},{1,9},{29,21},{5,5},{1... | collective-permute-start | bytes 1179656 | tf_op jit(solution)/shard_map/ppermute | solution.py:201
  101.8 9.8 %collective-permute-start.29 = (bf16[128,1536]{1,0:T(8,128)(2,1)S(1)}, bf16[128,1536]{1,0:T(8,128)(2,1)S(1)}, u32[]{:S(2)}, u32[]{:S(2)}) collective-permute-start(bf16[128,1536]{1,0:T(8,128)(2,1)S(1)} %collective-permute-done.24), channel_id=1, source_target_pairs={{16,24},{12,4},{0,0},{8,8},{20,20},{28,28},{17,25},{13,5},{1,1},{9... | collective-permute-start | bytes 1179656 | tf_op jit(solution)/shard_map/ppermute | solution.py:201
  102.5 10.1 %collective-permute-start.28 = (bf16[128,1024]{1,0:T(8,128)(2,1)S(1)}, bf16[128,1024]{1,0:T(8,128)(2,1)S(1)}, u32[]{:S(2)}, u32[]{:S(2)}) collective-permute-start(bf16[128,1024]{1,0:T(8,128)(2,1)S(1)} %collective-permute-done.23), channel_id=1, source_target_pairs={{8,16},{20,12},{0,0},{4,4},{24,24},{28,28},{9,17},{21,13},{1,1},{5... | collective-permute-start | bytes 786440 | tf_op jit(solution)/shard_map/ppermute | solution.py:201
  108.0 7.2 %collective-permute-start.27 = (bf16[128,1024]{1,0:T(8,128)(2,1)S(1)}, bf16[128,1024]{1,0:T(8,128)(2,1)S(1)}, u32[]{:S(2)}, u32[]{:S(2)}) collective-permute-start(bf16[128,1024]{1,0:T(8,128)(2,1)S(1)} %fusion.37), channel_id=1, source_target_pairs={{0,8},{28,20},{4,4},{12,12},{16,16},{24,24},{1,9},{29,21},{5,5},{1... | collective-permute-start | bytes 786440 | tf_op jit(solution)/shard_map/ppermute | solution.py:201
  109.5 16.2 %collective-permute-start.36 = (bf16[128,1536]{1,0:T(8,128)(2,1)S(1)}, bf16[128,1536]{1,0:T(8,128)(2,1)S(1)}, u32[]{:S(2)}, u32[]{:S(2)}) collective-permute-start(bf16[128,1536]{1,0:T(8,128)(2,1)S(1)} %collective-permute-done.31), channel_id=1, source_target_pairs={{16,24},{12,4},{0,0},{8,8},{20,20},{28,28},{17,25},{13,5},{1,1},{9... | collective-permute-start | bytes 1179656 | tf_op jit(solution)/shard_map/ppermute | solution.py:201
  110.3 15.9 %collective-permute-start.35 = (bf16[128,1536]{1,0:T(8,128)(2,1)S(1)}, bf16[128,1536]{1,0:T(8,128)(2,1)S(1)}, u32[]{:S(2)}, u32[]{:S(2)}) collective-permute-start(bf16[128,1536]{1,0:T(8,128)(2,1)S(1)} %collective-permute-done.30), channel_id=1, source_target_pairs={{8,16},{20,12},{0,0},{4,4},{24,24},{28,28},{9,17},{21,13},{1,1},{5... | collective-permute-start | bytes 1179656 | tf_op jit(solution)/shard_map/ppermute | solution.py:201
  112.0 14.9 %collective-permute-start.34 = (bf16[128,1536]{1,0:T(8,128)(2,1)S(1)}, bf16[128,1536]{1,0:T(8,128)(2,1)S(1)}, u32[]{:S(2)}, u32[]{:S(2)}) collective-permute-start(bf16[128,1536]{1,0:T(8,128)(2,1)S(1)} %select_select_fusion.2.refs_0_), channel_id=1, source_target_pairs={{0,4},{4,0},{8,12},{12,8},{16,20},{20,16},{24,28},{28,24},{1,5},{5... | collective-permute-start | bytes 1179656 | tf_op jit(solution)/shard_map/ppermute | solution.py:197
  112.5 18.2 %collective-permute-start.33 = (bf16[128,1024]{1,0:T(8,128)(2,1)S(1)}, bf16[128,1024]{1,0:T(8,128)(2,1)S(1)}, u32[]{:S(2)}, u32[]{:S(2)}) collective-permute-start(bf16[128,1024]{1,0:T(8,128)(2,1)S(1)} %collective-permute-done.28), channel_id=1, source_target_pairs={{16,24},{12,4},{0,0},{8,8},{20,20},{28,28},{17,25},{13,5},{1,1},{9... | collective-permute-start | bytes 786440 | tf_op jit(solution)/shard_map/ppermute | solution.py:201
  115.3 17.0 %collective-permute-start.32 = (bf16[128,1024]{1,0:T(8,128)(2,1)S(1)}, bf16[128,1024]{1,0:T(8,128)(2,1)S(1)}, u32[]{:S(2)}, u32[]{:S(2)}) collective-permute-start(bf16[128,1024]{1,0:T(8,128)(2,1)S(1)} %collective-permute-done.27), channel_id=1, source_target_pairs={{8,16},{20,12},{0,0},{4,4},{24,24},{28,28},{9,17},{21,13},{1,1},{5... | collective-permute-start | bytes 786440 | tf_op jit(solution)/shard_map/ppermute | solution.py:201
  126.1 6.8 %collective-permute-start.40 = (bf16[128,1536]{1,0:T(8,128)(2,1)S(1)}, bf16[128,1536]{1,0:T(8,128)(2,1)S(1)}, u32[]{:S(2)}, u32[]{:S(2)}) collective-permute-start(bf16[128,1536]{1,0:T(8,128)(2,1)S(1)} %select_select_fusion.1.refs_0_), channel_id=1, source_target_pairs={{0,4},{4,0},{8,12},{12,8},{16,20},{20,16},{24,28},{28,24},{1,5},{5... | collective-permute-start | bytes 1179656 | tf_op jit(solution)/shard_map/ppermute | solution.py:197
  126.2 10.6 %collective-permute-start.39 = (bf16[128,1536]{1,0:T(8,128)(2,1)S(1)}, bf16[128,1536]{1,0:T(8,128)(2,1)S(1)}, u32[]{:S(2)}, u32[]{:S(2)}) collective-permute-start(bf16[128,1536]{1,0:T(8,128)(2,1)S(1)} %collective-permute-done.35), channel_id=1, source_target_pairs={{16,24},{12,4},{0,0},{8,8},{20,20},{28,28},{17,25},{13,5},{1,1},{9... | collective-permute-start | bytes 1179656 | tf_op jit(solution)/shard_map/ppermute | solution.py:201
  131.1 6.8 %collective-permute-start.38 = (bf16[128,1024]{1,0:T(8,128)(2,1)S(1)}, bf16[128,1024]{1,0:T(8,128)(2,1)S(1)}, u32[]{:S(2)}, u32[]{:S(2)}) collective-permute-start(bf16[128,1024]{1,0:T(8,128)(2,1)S(1)} %select_select_fusion.4.refs_0_), channel_id=1, source_target_pairs={{0,4},{4,0},{8,12},{12,8},{16,20},{20,16},{24,28},{28,24},{1,5},{5... | collective-permute-start | bytes 786440 | tf_op jit(solution)/shard_map/ppermute | solution.py:197
  132.3 8.9 %collective-permute-start.37 = (bf16[128,1024]{1,0:T(8,128)(2,1)S(1)}, bf16[128,1024]{1,0:T(8,128)(2,1)S(1)}, u32[]{:S(2)}, u32[]{:S(2)}) collective-permute-start(bf16[128,1024]{1,0:T(8,128)(2,1)S(1)} %collective-permute-done.32), channel_id=1, source_target_pairs={{16,24},{12,4},{0,0},{8,8},{20,20},{28,28},{17,25},{13,5},{1,1},{9... | collective-permute-start | bytes 786440 | tf_op jit(solution)/shard_map/ppermute | solution.py:201
  137.2 4.4 %collective-permute-start.42 = (bf16[128,1536]{1,0:T(8,128)(2,1)S(1)}, bf16[128,1536]{1,0:T(8,128)(2,1)S(1)}, u32[]{:S(2)}, u32[]{:S(2)}) collective-permute-start(bf16[128,1536]{1,0:T(8,128)(2,1)S(1)} %select_select_fusion.refs_0_), channel_id=1, source_target_pairs={{0,4},{4,0},{8,12},{12,8},{16,20},{20,16},{24,28},{28,24},{1,5},{5... | collective-permute-start | bytes 1179656 | tf_op jit(solution)/shard_map/ppermute | solution.py:197
  141.5 4.1 %collective-permute-start.41 = (bf16[128,1024]{1,0:T(8,128)(2,1)S(1)}, bf16[128,1024]{1,0:T(8,128)(2,1)S(1)}, u32[]{:S(2)}, u32[]{:S(2)}) collective-permute-start(bf16[128,1024]{1,0:T(8,128)(2,1)S(1)} %select_select_fusion.3.refs_0_), channel_id=1, source_target_pairs={{0,4},{4,0},{8,12},{12,8},{16,20},{20,16},{24,28},{28,24},{1,5},{5... | collective-permute-start | bytes 786440 | tf_op jit(solution)/shard_map/ppermute | solution.py:197
  148.9 8.5 %collective-permute-start.45 = (bf16[64,2048]{1,0:T(8,128)(2,1)S(1)}, bf16[64,2048]{1,0:T(8,128)(2,1)S(1)}, u32[]{:S(2)}, u32[]{:S(2)}) collective-permute-start(bf16[64,2048]{1,0:T(8,128)(2,1)S(1)} %get-tuple-element.176), channel_id=1, source_target_pairs={{0,3},{1,2},{2,1},{3,0},{4,7},{5,6},{6,5},{7,4},{8,11},{9,10},{10,... | collective-permute-start | bytes 786440 | tf_op jit(solution)/shard_map/ppermute | solution.py:222
  150.3 13.5 %collective-permute-start.44 = (bf16[64,2048]{1,0:T(8,128)(2,1)S(1)}, bf16[64,2048]{1,0:T(8,128)(2,1)S(1)}, u32[]{:S(2)}, u32[]{:S(2)}) collective-permute-start(bf16[64,2048]{1,0:T(8,128)(2,1)S(1)} %get-tuple-element.177), channel_id=1, source_target_pairs={{0,2},{1,3},{2,0},{3,1},{4,6},{5,7},{6,4},{7,5},{8,10},{9,11},{10,... | collective-permute-start | bytes 786440 | tf_op jit(solution)/shard_map/ppermute | solution.py:222
  151.4 12.5 %collective-permute-start.43 = (bf16[64,2048]{1,0:T(8,128)(2,1)S(1)}, bf16[64,2048]{1,0:T(8,128)(2,1)}, u32[]{:S(2)}, u32[]{:S(2)}) collective-permute-start(bf16[64,2048]{1,0:T(8,128)(2,1)S(1)} %get-tuple-element.175), channel_id=1, source_target_pairs={{0,1},{1,0},{2,3},{3,2},{4,5},{5,4},{6,7},{7,6},{8,9},{9,8},{10,11... | collective-permute-start | bytes 786440 | tf_op jit(solution)/shard_map/ppermute | solution.py:222

commit v4 on v3

--- a/solution.py
+++ b/solution.py
@@ -13,7 +13,7 @@
 WEIGHT_MAX = 0.046875
 VMEM = 14 * 1024 * 1024
 PIECES = 2
-SIZES = [3, 3, 2, 3, 2]
+SIZES = [2, 2, 3, 3, 3]
 GAPS = [0, 1, 1, 2]
 
 

time: 167 us -> 170 us (1.018)
    convert_element_type x15, other arithmetic: 10.4 us -> 7.12 us  [encode(): return (v * root * scale).astype(jnp.float16)]
    select_n x5, other arithmetic: 1.65 us -> 4.65 us  [gather(): rows_here = jnp.where(away == step, stage, rows_here)]
    pallas_call x5, Pallas kernels: 29.2 us -> 26.9 us  [first(): pl.pallas_call(kernel, in_specs=[vmem, hbm, hbm], out_specs=[vmem, vmem],...]
    convert_element_type x5, other arithmetic: 0.97 us -> 2.79 us  [finish(): hidden = (jax.nn.silu(value[0]) * value[1]).astype(jnp.bfloat16)]
  transfers between devices with their start and end apart: 46 -> 46, of which waited for: 9 -> 10; matrix products, arithmetic and copies ran while one was open for 9% -> 9% of each run, Pallas kernels for 22% -> 22%
where the time goes in v4:
time: 170 us; the launch traced here: 167 us
  starting transfers between devices  63.5 us (37%)
  Pallas kernels  46 us (27%)
  waiting for transfers between devices  36.5 us (21%)
  other arithmetic  18.8 us (11%)
    ppermute x30, starting transfers between devices, hop(): return lax.ppermute(v, 'gx', pairs + [(i, i) for i in sorted(idle)])  49.4 us
    pallas_call x5, Pallas kernels, first(): pl.pallas_call(kernel, in_specs=[vmem, hbm, hbm], out_specs=[vmem, vmem],...  26.9 us
    ppermute x6, waiting for transfers between devices, across(): return lax.ppermute(v, 'gy', [(i, i ^ shift) for i in range(n_gy)])  24.5 us
    pallas_call x5, Pallas kernels, second(): pl.pallas_call(kernel, in_specs=[vmem, vmem, hbm] + ([vmem] if carried el...  19.1 us
    ppermute x30, waiting for transfers between devices, hop(): return lax.ppermute(v, 'gx', pairs + [(i, i) for i in sorted(idle)])  12 us
    ppermute x10, starting transfers between devices, swap(): return lax.ppermute(v, 'gx', [(i, i ^ 1) for i in range(n_gx)])  8.79 us
    convert_element_type x15, other arithmetic, encode(): return (v * root * scale).astype(jnp.float16)  7.12 us
    ppermute x6, starting transfers between devices, across(): return lax.ppermute(v, 'gy', [(i, i ^ shift) for i in range(n_gy)])  5.36 us
  transfers between devices with their start and end apart: 46, of which 10 were waited for; matrix products, arithmetic and copies ran while one was open for 9% of the time, Pallas kernels for 22%

profile of v4, /device:TPU:17, one launch (start us, length us, event | category | flops | bytes accessed | tf_op | source)
XLA Modules:
  0.0 167.1 jit_solution(6143895700144601431)
XLA Ops:
  0.0 2.2 %collective-permute-start.2 = (bf16[64,2048]{1,0:T(8,128)(2,1)}, bf16[64,2048]{1,0:T(8,128)(2,1)S(1)}, u32[]{:S(2)}, u32[]{:S(2)}) collective-permute-start(bf16[64,2048]{1,0:T(8,128)(2,1)} %param.4), channel_id=1, source_target_pairs={{0,3},{1,2},{2,1},{3,0},{4,7},{5,6},{6,5},{7,4},{8,11},{9,10},{10,... | collective-permute-start | bytes 786440 | tf_op jit(solution)/shard_map/ppermute | solution.py:222
  2.7 5.7 %collective-permute-done.2 = bf16[64,2048]{1,0:T(8,128)(2,1)S(1)} collective-permute-done((bf16[64,2048]{1,0:T(8,128)(2,1)}, bf16[64,2048]{1,0:T(8,128)(2,1)S(1)}, u32[]{:S(2)}, u32[]{:S(2)}) %collective-permute-start.2) | collective-permute-done | bytes 262176 | tf_op jit(solution)/shard_map/ppermute | solution.py:222
  8.3 6.6 %collective-permute-done.1 = bf16[64,2048]{1,0:T(8,128)(2,1)S(1)} collective-permute-done((bf16[64,2048]{1,0:T(8,128)(2,1)}, bf16[64,2048]{1,0:T(8,128)(2,1)S(1)}, u32[]{:S(2)}, u32[]{:S(2)}) %collective-permute-start.1) | collective-permute-done | bytes 262176 | tf_op jit(solution)/shard_map/ppermute | solution.py:222
  16.2 4.5 %shard_map.46 = (f32[2,128,1024]{2,1,0:T(8,128)S(1)}, f32[2,128,1024]{2,1,0:T(8,128)S(1)}) custom-call(bf16[256,2048]{1,0:T(8,128)(2,1)S(1)} %pad_maximum_fusion.1.rows_ref, bf16[2048,6656]{1,0:T(8,128)(2,1)} %gate_ref.9, bf16[2048,6656]{1,0:T(8,128)(2,1)} %up_ref.9), custom_call_target="tpu_custom_call" | custom-call | flops 2147483648 | bytes 10485760 | tf_op jit(solution)/shard_map/pallas_call | solution.py:67
  21.4 4.5 %shard_map.47 = (f32[2,128,1024]{2,1,0:T(8,128)S(1)}, f32[2,128,1024]{2,1,0:T(8,128)S(1)}) custom-call(bf16[256,2048]{1,0:T(8,128)(2,1)S(1)} %pad_maximum_fusion.1.rows_ref, bf16[2048,6656]{1,0:T(8,128)(2,1)} %gate_ref.9, bf16[2048,6656]{1,0:T(8,128)(2,1)} %up_ref.9), custom_call_target="tpu_custom_call" | custom-call | flops 2147483648 | bytes 10485760 | tf_op jit(solution)/shard_map/pallas_call | solution.py:67
  26.4 6.0 %shard_map.48 = (f32[2,128,1536]{2,1,0:T(8,128)S(1)}, f32[2,128,1536]{2,1,0:T(8,128)S(1)}) custom-call(bf16[256,2048]{1,0:T(8,128)(2,1)S(1)} %pad_maximum_fusion.1.rows_ref, bf16[2048,6656]{1,0:T(8,128)(2,1)} %gate_ref.9, bf16[2048,6656]{1,0:T(8,128)(2,1)} %up_ref.9), custom_call_target="tpu_custom_call" | custom-call | flops 3221225472 | bytes 15728640 | tf_op jit(solution)/shard_map/pallas_call | solution.py:67
  34.0 6.0 %shard_map.49 = (f32[2,128,1536]{2,1,0:T(8,128)S(1)}, f32[2,128,1536]{2,1,0:T(8,128)S(1)}) custom-call(bf16[256,2048]{1,0:T(8,128)(2,1)S(1)} %pad_maximum_fusion.1.rows_ref, bf16[2048,6656]{1,0:T(8,128)(2,1)} %gate_ref.9, bf16[2048,6656]{1,0:T(8,128)(2,1)} %up_ref.9), custom_call_target="tpu_custom_call" | custom-call | flops 3221225472 | bytes 15728640 | tf_op jit(solution)/shard_map/pallas_call | solution.py:67
  41.7 1.3 collective-permute-start.9
  44.4 6.0 %shard_map.50 = (f32[2,128,1536]{2,1,0:T(8,128)S(1)}, f32[2,128,1536]{2,1,0:T(8,128)S(1)}) custom-call(bf16[256,2048]{1,0:T(8,128)(2,1)S(1)} %pad_maximum_fusion.1.rows_ref, bf16[2048,6656]{1,0:T(8,128)(2,1)} %gate_ref.9, bf16[2048,6656]{1,0:T(8,128)(2,1)} %up_ref.9), custom_call_target="tpu_custom_call" | custom-call | flops 3221225472 | bytes 15728640 | tf_op jit(solution)/shard_map/pallas_call | solution.py:67
  50.3 3.3 %collective-permute-start.7 = (f32[2,128,1536]{2,1,0:T(8,128)S(1)}, f32[2,128,1536]{2,1,0:T(8,128)S(1)}, u32[]{:S(2)}, u32[]{:S(2)}) collective-permute-start(f32[2,128,1536]{2,1,0:T(8,128)S(1)} %get-tuple-element.106), channel_id=1, source_target_pairs={{0,4},{4,0},{8,12},{12,8},{16,20},{20,16},{24,28},{28,24},{1,5},{5... | collective-permute-start | bytes 4718600 | tf_op jit(solution)/shard_map/ppermute | solution.py:197
  54.1 1.3 collective-permute-start.16
  57.0 3.7 %collective-permute-start.14 = (f16[2,128,1024]{2,1,0:T(8,128)(2,1)S(1)}, f16[2,128,1024]{2,1,0:T(8,128)(2,1)S(1)}, u32[]{:S(2)}, u32[]{:S(2)}) collective-permute-start(f16[2,128,1024]{2,1,0:T(8,128)(2,1)S(1)} %multiply_convert_fusion.10), channel_id=1, source_target_pairs={{8,0},{20,28},{4,4},{12,12},{16,16},{24,24},{9,1},{21,29},{5,5},{1... | collective-permute-start | bytes 1572872 | tf_op jit(solution)/shard_map/ppermute | solution.py:201
  61.3 1.3 collective-permute-start.13
  64.7 1.3 collective-permute-start.21
  66.7 1.3 collective-permute-start.20
  68.3 1.3 collective-permute-start.19
  69.6 4.7 %collective-permute-done.13 = f16[2,128,1536]{2,1,0:T(8,128)(2,1)S(1)} collective-permute-done((f16[2,128,1536]{2,1,0:T(8,128)(2,1)S(1)}, f16[2,128,1536]{2,1,0:T(8,128)(2,1)S(1)}, u32[]{:S(2)}, u32[]{:S(2)}) %collective-permute-start.13) | collective-permute-done | bytes 786464 | tf_op jit(solution)/shard_map/ppermute | solution.py:201
  74.9 1.3 collective-permute-start.18
  76.9 1.3 collective-permute-start.17
  79.5 1.3 collective-permute-start.26
  80.8 1.6 collective-permute-done.20
  83.1 3.1 %collective-permute-start.25 = (f16[2,128,1536]{2,1,0:T(8,128)(2,1)S(1)}, f16[2,128,1536]{2,1,0:T(8,128)(2,1)S(1)}, u32[]{:S(2)}, u32[]{:S(2)}) collective-permute-start(f16[2,128,1536]{2,1,0:T(8,128)(2,1)S(1)} %multiply_convert_fusion.1), channel_id=1, source_target_pairs={{8,0},{20,28},{4,4},{12,12},{16,16},{24,24},{9,1},{21,29},{5,5},{1... | collective-permute-start | bytes 2359304 | tf_op jit(solution)/shard_map/ppermute | solution.py:201
  86.2 4.6 %collective-permute-start.24 = (bf16[128,1024]{1,0:T(8,128)(2,1)S(1)}, bf16[128,1024]{1,0:T(8,128)(2,1)}, u32[]{:S(2)}, u32[]{:S(2)}) collective-permute-start(bf16[128,1024]{1,0:T(8,128)(2,1)S(1)} %collective-permute-done.19), channel_id=1, source_target_pairs={{8,16},{20,12},{0,0},{4,4},{24,24},{28,28},{9,17},{21,13},{1,1},{5... | collective-permute-start | bytes 786440 | tf_op jit(solution)/shard_map/ppermute | solution.py:201
  91.3 1.3 collective-permute-start.23
  92.6 2.1 %collective-permute-done.17 = f16[2,128,1536]{2,1,0:T(8,128)(2,1)S(1)} collective-permute-done((f16[2,128,1536]{2,1,0:T(8,128)(2,1)S(1)}, f16[2,128,1536]{2,1,0:T(8,128)(2,1)S(1)}, u32[]{:S(2)}, u32[]{:S(2)}) %collective-permute-start.17) | collective-permute-done | bytes 786464 | tf_op jit(solution)/shard_map/ppermute | solution.py:201
  95.3 2.0 %collective-permute-start.22 = (f16[2,128,1536]{2,1,0:T(8,128)(2,1)S(1)}, f16[2,128,1536]{2,1,0:T(8,128)(2,1)S(1)}, u32[]{:S(2)}, u32[]{:S(2)}) collective-permute-start(f16[2,128,1536]{2,1,0:T(8,128)(2,1)S(1)} %multiply_convert_fusion), channel_id=1, source_target_pairs={{8,0},{20,28},{4,4},{12,12},{16,16},{24,24},{9,1},{21,29},{5,5},{1... | collective-permute-start | bytes 2359304 | tf_op jit(solution)/shard_map/ppermute | solution.py:201
  97.3 2.0 %collective-permute-start.31 = (bf16[128,1024]{1,0:T(8,128)(2,1)}, bf16[128,1024]{1,0:T(8,128)(2,1)}, u32[]{:S(2)}, u32[]{:S(2)}) collective-permute-start(bf16[128,1024]{1,0:T(8,128)(2,1)} %collective-permute-done.26), channel_id=1, source_target_pairs={{8,16},{20,12},{0,0},{4,4},{24,24},{28,28},{9,17},{21,13},{1,1},{5... | collective-permute-start | bytes 786440 | tf_op jit(solution)/shard_map/ppermute | solution.py:201
  100.8 1.3 collective-permute-start.30
  102.1 3.6 %collective-permute-start.29 = (bf16[128,1024]{1,0:T(8,128)(2,1)}, bf16[128,1024]{1,0:T(8,128)(2,1)}, u32[]{:S(2)}, u32[]{:S(2)}) collective-permute-start(bf16[128,1024]{1,0:T(8,128)(2,1)} %collective-permute-done.24), channel_id=1, source_target_pairs={{16,24},{12,4},{0,0},{8,8},{20,20},{28,28},{17,25},{13,5},{1,1},{9... | collective-permute-start | bytes 786440 | tf_op jit(solution)/shard_map/ppermute | solution.py:201
  105.7 2.0 %collective-permute-start.28 = (bf16[128,1536]{1,0:T(8,128)(2,1)S(1)}, bf16[128,1536]{1,0:T(8,128)(2,1)}, u32[]{:S(2)}, u32[]{:S(2)}) collective-permute-start(bf16[128,1536]{1,0:T(8,128)(2,1)S(1)} %collective-permute-done.23), channel_id=1, source_target_pairs={{8,16},{20,12},{0,0},{4,4},{24,24},{28,28},{9,17},{21,13},{1,1},{5... | collective-permute-start | bytes 1179656 | tf_op jit(solution)/shard_map/ppermute | solution.py:201
  110.4 1.3 collective-permute-start.27
  111.7 1.7 %collective-permute-start.36 = (bf16[128,1024]{1,0:T(8,128)(2,1)}, bf16[128,1024]{1,0:T(8,128)(2,1)S(1)}, u32[]{:S(2)}, u32[]{:S(2)}) collective-permute-start(bf16[128,1024]{1,0:T(8,128)(2,1)} %collective-permute-done.31), channel_id=1, source_target_pairs={{16,24},{12,4},{0,0},{8,8},{20,20},{28,28},{17,25},{13,5},{1,1},{9... | collective-permute-start | bytes 786440 | tf_op jit(solution)/shard_map/ppermute | solution.py:201
  113.5 1.3 collective-permute-start.35
  114.8 1.3 select_select_fusion.4.refs_0_
  116.1 1.7 collective-permute-start.33
  117.8 1.9 %collective-permute-done.27 = bf16[128,1536]{1,0:T(8,128)(2,1)} collective-permute-done((bf16[128,1536]{1,0:T(8,128)(2,1)}, bf16[128,1536]{1,0:T(8,128)(2,1)}, u32[]{:S(2)}, u32[]{:S(2)}) %collective-permute-start.27) | collective-permute-done | bytes 393248 | tf_op jit(solution)/shard_map/ppermute | solution.py:201
  119.6 3.0 %collective-permute-start.32 = (bf16[128,1536]{1,0:T(8,128)(2,1)}, bf16[128,1536]{1,0:T(8,128)(2,1)S(1)}, u32[]{:S(2)}, u32[]{:S(2)}) collective-permute-start(bf16[128,1536]{1,0:T(8,128)(2,1)} %collective-permute-done.27), channel_id=1, source_target_pairs={{8,16},{20,12},{0,0},{4,4},{24,24},{28,28},{9,17},{21,13},{1,1},{5... | collective-permute-start | bytes 1179656 | tf_op jit(solution)/shard_map/ppermute | solution.py:201
  124.7 3.2 %shard_map.51.refs_3_ = f32[256,2048]{1,0:T(8,128)S(1)} custom-call(bf16[128,1024]{1,0:T(8,128)(2,1)S(1)} %select_select_fusion.4.refs_0_, bf16[128,1024]{1,0:T(8,128)(2,1)S(1)} %collective-permute-done.34.refs_1_, bf16[6656,2048]{1,0:T(8,128)(2,1)} %refs_2_.9), custom_call_target="tpu_custom_call" | custom-call | flops 1073741824 | bytes 8388608 | tf_op jit(solution)/shard_map/pallas_call | solution.py:126
  128.3 2.2 %collective-permute-start.38 = (bf16[128,1536]{1,0:T(8,128)(2,1)S(1)}, bf16[128,1536]{1,0:T(8,128)(2,1)S(1)}, u32[]{:S(2)}, u32[]{:S(2)}) collective-permute-start(bf16[128,1536]{1,0:T(8,128)(2,1)S(1)} %select_select_fusion.2.refs_0_), channel_id=1, source_target_pairs={{0,4},{4,0},{8,12},{12,8},{16,20},{20,16},{24,28},{28,24},{1,5},{5... | collective-permute-start | bytes 1179656 | tf_op jit(solution)/shard_map/ppermute | solution.py:197
  131.2 3.2 %shard_map.52.refs_3_ = f32[256,2048]{1,0:T(8,128)S(1)} custom-call(bf16[128,1024]{1,0:T(8,128)(2,1)S(1)} %select_select_fusion.3.refs_0_, bf16[128,1024]{1,0:T(8,128)(2,1)S(1)} %collective-permute-done.40.refs_1_, bf16[6656,2048]{1,0:T(8,128)(2,1)} %refs_2_.9, f32[256,2048]{1,0:T(8,128)S(1)} %shard_map.51.refs_3_), custom_call_target="tpu_custom_call" | custom-call | flops 1073741824 | bytes 8388608 | tf_op jit(solution)/shard_map/pallas_call | solution.py:126
  136.0 3.9 %shard_map.53.refs_3_ = f32[256,2048]{1,0:T(8,128)S(1)} custom-call(bf16[128,1536]{1,0:T(8,128)(2,1)S(1)} %select_select_fusion.2.refs_0_, bf16[128,1536]{1,0:T(8,128)(2,1)S(1)} %collective-permute-done.38.refs_1_, bf16[6656,2048]{1,0:T(8,128)(2,1)} %refs_2_.9, f32[256,2048]{1,0:T(8,128)S(1)} %shard_map.52.refs_3_), custom_call_target="tpu_custom_call" | custom-call | flops 1610612736 | bytes 10485760 | tf_op jit(solution)/shard_map/pallas_call | solution.py:126
  139.9 1.4 select_select_fusion.refs_0_
  141.4 3.9 %shard_map.54.refs_3_ = f32[256,2048]{1,0:T(8,128)S(1)} custom-call(bf16[128,1536]{1,0:T(8,128)(2,1)S(1)} %select_select_fusion.1.refs_0_, bf16[128,1536]{1,0:T(8,128)(2,1)S(1)} %collective-permute-done.42.refs_1_, bf16[6656,2048]{1,0:T(8,128)(2,1)} %refs_2_.9, f32[256,2048]{1,0:T(8,128)S(1)} %shard_map.53.refs_3_), custom_call_target="tpu_custom_call" | custom-call | flops 1610612736 | bytes 10485760 | tf_op jit(solution)/shard_map/pallas_call | solution.py:126
  145.3 4.9 %shard_map.55 = f32[256,2048]{1,0:T(8,128)S(1)} custom-call(bf16[128,1536]{1,0:T(8,128)(2,1)S(1)} %select_select_fusion.refs_0_, bf16[128,1536]{1,0:T(8,128)(2,1)} %collective-permute-done.41.refs_1_, bf16[6656,2048]{1,0:T(8,128)(2,1)} %refs_2_.9, f32[256,2048]{1,0:T(8,128)S(1)} %shard_map.54.refs_3_), custom_call_target="tpu_custom_call" | custom-call | flops 1610612736 | bytes 10485760 | tf_op jit(solution)/shard_map/pallas_call | solution.py:126
  150.4 1.4 collective-permute-start.45
  153.1 5.8 %collective-permute-done.45 = bf16[64,2048]{1,0:T(8,128)(2,1)S(1)} collective-permute-done((bf16[64,2048]{1,0:T(8,128)(2,1)S(1)}, bf16[64,2048]{1,0:T(8,128)(2,1)S(1)}, u32[]{:S(2)}, u32[]{:S(2)}) %collective-permute-start.45) | collective-permute-done | bytes 262176 | tf_op jit(solution)/shard_map/ppermute | solution.py:222
  158.9 6.4 %collective-permute-done.44 = bf16[64,2048]{1,0:T(8,128)(2,1)S(1)} collective-permute-done((bf16[64,2048]{1,0:T(8,128)(2,1)S(1)}, bf16[64,2048]{1,0:T(8,128)(2,1)S(1)}, u32[]{:S(2)}, u32[]{:S(2)}) %collective-permute-start.44) | collective-permute-done | bytes 262176 | tf_op jit(solution)/shard_map/ppermute | solution.py:222
  165.3 1.9 %convert_add_fusion = f32[64,2048]{1,0:T(8,128)} fusion(bf16[64,2048]{1,0:T(8,128)(2,1)S(1)} %collective-permute-done.45, bf16[64,2048]{1,0:T(8,128)(2,1)S(1)} %collective-permute-done.44, bf16[64,2048]{1,0:T(8,128)(2,1)} %collective-permute-done.43, f32[256,2048]{1,0:T(8,128)S(1)} %shard_map.55, s32[]{:T(128)S(6)} %select_n.173), kind=kLoop, calls=%fused_computation.82 | loop fusion | flops 786432 | bytes 1835012 | tf_op jit(solution)/shard_map/add | solution.py:313
  (103 shorter events, 27.4 us)
Async XLA Ops:
  0.0 8.3 %collective-permute-start.2 = (bf16[64,2048]{1,0:T(8,128)(2,1)}, bf16[64,2048]{1,0:T(8,128)(2,1)S(1)}, u32[]{:S(2)}, u32[]{:S(2)}) collective-permute-start(bf16[64,2048]{1,0:T(8,128)(2,1)} %param.4), channel_id=1, source_target_pairs={{0,3},{1,2},{2,1},{3,0},{4,7},{5,6},{6,5},{7,4},{8,11},{9,10},{10,... | collective-permute-start | bytes 786440 | tf_op jit(solution)/shard_map/ppermute | solution.py:222
  2.2 12.8 %collective-permute-start.1 = (bf16[64,2048]{1,0:T(8,128)(2,1)}, bf16[64,2048]{1,0:T(8,128)(2,1)S(1)}, u32[]{:S(2)}, u32[]{:S(2)}) collective-permute-start(bf16[64,2048]{1,0:T(8,128)(2,1)} %param.4), channel_id=1, source_target_pairs={{0,2},{1,3},{2,0},{3,1},{4,6},{5,7},{6,4},{7,5},{8,10},{9,11},{10,... | collective-permute-start | bytes 786440 | tf_op jit(solution)/shard_map/ppermute | solution.py:222
  2.4 12.6 %collective-permute-start = (bf16[64,2048]{1,0:T(8,128)(2,1)}, bf16[64,2048]{1,0:T(8,128)(2,1)S(1)}, u32[]{:S(2)}, u32[]{:S(2)}) collective-permute-start(bf16[64,2048]{1,0:T(8,128)(2,1)} %param.4), channel_id=1, source_target_pairs={{0,1},{1,0},{2,3},{3,2},{4,5},{5,4},{6,7},{7,6},{8,9},{9,8},{10,11... | collective-permute-start | bytes 786440 | tf_op jit(solution)/shard_map/ppermute | solution.py:222
  20.8 5.3 %collective-permute-start.3 = (f32[2,128,1024]{2,1,0:T(8,128)S(1)}, f32[2,128,1024]{2,1,0:T(8,128)S(1)}, u32[]{:S(2)}, u32[]{:S(2)}) collective-permute-start(f32[2,128,1024]{2,1,0:T(8,128)S(1)} %get-tuple-element.87), channel_id=1, source_target_pairs={{0,4},{4,0},{8,12},{12,8},{16,20},{20,16},{24,28},{28,24},{1,5},{5... | collective-permute-start | bytes 3145736 | tf_op jit(solution)/shard_map/ppermute | solution.py:197
  25.9 7.7 %collective-permute-start.6 = (f32[2,128,1024]{2,1,0:T(8,128)S(1)}, f32[2,128,1024]{2,1,0:T(8,128)S(1)}, u32[]{:S(2)}, u32[]{:S(2)}) collective-permute-start(f32[2,128,1024]{2,1,0:T(8,128)S(1)} %get-tuple-element.95), channel_id=1, source_target_pairs={{0,4},{4,0},{8,12},{12,8},{16,20},{20,16},{24,28},{28,24},{1,5},{5... | collective-permute-start | bytes 3145736 | tf_op jit(solution)/shard_map/ppermute | solution.py:197
  32.4 10.7 %collective-permute-start.4 = (f32[2,128,1536]{2,1,0:T(8,128)S(1)}, f32[2,128,1536]{2,1,0:T(8,128)S(1)}, u32[]{:S(2)}, u32[]{:S(2)}) collective-permute-start(f32[2,128,1536]{2,1,0:T(8,128)S(1)} %get-tuple-element.94), channel_id=1, source_target_pairs={{0,4},{4,0},{8,12},{12,8},{16,20},{20,16},{24,28},{28,24},{1,5},{5... | collective-permute-start | bytes 4718600 | tf_op jit(solution)/shard_map/ppermute | solution.py:197
  32.9 8.4 %collective-permute-start.5 = (f16[2,128,1024]{2,1,0:T(8,128)(2,1)S(1)}, f16[2,128,1024]{2,1,0:T(8,128)(2,1)S(1)}, u32[]{:S(2)}, u32[]{:S(2)}) collective-permute-start(f16[2,128,1024]{2,1,0:T(8,128)(2,1)S(1)} %get-tuple-element.173), channel_id=1, source_target_pairs={{24,16},{4,12},{0,0},{8,8},{20,20},{28,28},{25,17},{5,13},{1,1},{9... | collective-permute-start | bytes 1572872 | tf_op jit(solution)/shard_map/ppermute | solution.py:201
  39.9 15.4 %collective-permute-start.10 = (f32[2,128,1536]{2,1,0:T(8,128)S(1)}, f32[2,128,1536]{2,1,0:T(8,128)S(1)}, u32[]{:S(2)}, u32[]{:S(2)}) collective-permute-start(f32[2,128,1536]{2,1,0:T(8,128)S(1)} %get-tuple-element.107), channel_id=1, source_target_pairs={{0,4},{4,0},{8,12},{12,8},{16,20},{20,16},{24,28},{28,24},{1,5},{5... | collective-permute-start | bytes 4718600 | tf_op jit(solution)/shard_map/ppermute | solution.py:197
  40.6 13.1 %collective-permute-start.11 = (f16[2,128,1024]{2,1,0:T(8,128)(2,1)S(1)}, f16[2,128,1024]{2,1,0:T(8,128)(2,1)S(1)}, u32[]{:S(2)}, u32[]{:S(2)}) collective-permute-start(f16[2,128,1024]{2,1,0:T(8,128)(2,1)S(1)} %get-tuple-element.171), channel_id=1, source_target_pairs={{24,16},{4,12},{0,0},{8,8},{20,20},{28,28},{25,17},{5,13},{1,1},{9... | collective-permute-start | bytes 1572872 | tf_op jit(solution)/shard_map/ppermute | solution.py:201
  41.7 14.8 %collective-permute-start.9 = (f16[2,128,1024]{2,1,0:T(8,128)(2,1)S(1)}, f16[2,128,1024]{2,1,0:T(8,128)(2,1)S(1)}, u32[]{:S(2)}, u32[]{:S(2)}) collective-permute-start(f16[2,128,1024]{2,1,0:T(8,128)(2,1)S(1)} %multiply_convert_fusion.12), channel_id=1, source_target_pairs={{16,8},{12,20},{0,0},{4,4},{24,24},{28,28},{17,9},{13,21},{1,1},{5... | collective-permute-start | bytes 1572872 | tf_op jit(solution)/shard_map/ppermute | solution.py:201
  43.5 17.2 %collective-permute-start.8 = (f16[2,128,1536]{2,1,0:T(8,128)(2,1)S(1)}, f16[2,128,1536]{2,1,0:T(8,128)(2,1)S(1)}, u32[]{:S(2)}, u32[]{:S(2)}) collective-permute-start(f16[2,128,1536]{2,1,0:T(8,128)(2,1)S(1)} %get-tuple-element.169), channel_id=1, source_target_pairs={{24,16},{4,12},{0,0},{8,8},{20,20},{28,28},{25,17},{5,13},{1,1},{9... | collective-permute-start | bytes 2359304 | tf_op jit(solution)/shard_map/ppermute | solution.py:201
  50.3 12.3 %collective-permute-start.7 = (f32[2,128,1536]{2,1,0:T(8,128)S(1)}, f32[2,128,1536]{2,1,0:T(8,128)S(1)}, u32[]{:S(2)}, u32[]{:S(2)}) collective-permute-start(f32[2,128,1536]{2,1,0:T(8,128)S(1)} %get-tuple-element.106), channel_id=1, source_target_pairs={{0,4},{4,0},{8,12},{12,8},{16,20},{20,16},{24,28},{28,24},{1,5},{5... | collective-permute-start | bytes 4718600 | tf_op jit(solution)/shard_map/ppermute | solution.py:197
  54.1 10.2 %collective-permute-start.16 = (f16[2,128,1024]{2,1,0:T(8,128)(2,1)S(1)}, f16[2,128,1024]{2,1,0:T(8,128)(2,1)S(1)}, u32[]{:S(2)}, u32[]{:S(2)}) collective-permute-start(f16[2,128,1024]{2,1,0:T(8,128)(2,1)S(1)} %multiply_convert_fusion.11), channel_id=1, source_target_pairs={{16,8},{12,20},{0,0},{4,4},{24,24},{28,28},{17,9},{13,21},{1,1},{5... | collective-permute-start | bytes 1572872 | tf_op jit(solution)/shard_map/ppermute | solution.py:201
  55.8 10.2 %collective-permute-start.15 = (f16[2,128,1536]{2,1,0:T(8,128)(2,1)S(1)}, f16[2,128,1536]{2,1,0:T(8,128)(2,1)S(1)}, u32[]{:S(2)}, u32[]{:S(2)}) collective-permute-start(f16[2,128,1536]{2,1,0:T(8,128)(2,1)S(1)} %get-tuple-element.167), channel_id=1, source_target_pairs={{24,16},{4,12},{0,0},{8,8},{20,20},{28,28},{25,17},{5,13},{1,1},{9... | collective-permute-start | bytes 2359304 | tf_op jit(solution)/shard_map/ppermute | solution.py:201
  57.0 11.0 %collective-permute-start.14 = (f16[2,128,1024]{2,1,0:T(8,128)(2,1)S(1)}, f16[2,128,1024]{2,1,0:T(8,128)(2,1)S(1)}, u32[]{:S(2)}, u32[]{:S(2)}) collective-permute-start(f16[2,128,1024]{2,1,0:T(8,128)(2,1)S(1)} %multiply_convert_fusion.10), channel_id=1, source_target_pairs={{8,0},{20,28},{4,4},{12,12},{16,16},{24,24},{9,1},{21,29},{5,5},{1... | collective-permute-start | bytes 1572872 | tf_op jit(solution)/shard_map/ppermute | solution.py:201
  61.3 13.0 %collective-permute-start.13 = (f16[2,128,1536]{2,1,0:T(8,128)(2,1)S(1)}, f16[2,128,1536]{2,1,0:T(8,128)(2,1)S(1)}, u32[]{:S(2)}, u32[]{:S(2)}) collective-permute-start(f16[2,128,1536]{2,1,0:T(8,128)(2,1)S(1)} %multiply_convert_fusion.6), channel_id=1, source_target_pairs={{16,8},{12,20},{0,0},{4,4},{24,24},{28,28},{17,9},{13,21},{1,1},{5... | collective-permute-start | bytes 2359304 | tf_op jit(solution)/shard_map/ppermute | solution.py:201
  63.1 13.2 %collective-permute-start.12 = (f16[2,128,1536]{2,1,0:T(8,128)(2,1)S(1)}, f16[2,128,1536]{2,1,0:T(8,128)(2,1)S(1)}, u32[]{:S(2)}, u32[]{:S(2)}) collective-permute-start(f16[2,128,1536]{2,1,0:T(8,128)(2,1)S(1)} %get-tuple-element.165), channel_id=1, source_target_pairs={{24,16},{4,12},{0,0},{8,8},{20,20},{28,28},{25,17},{5,13},{1,1},{9... | collective-permute-start | bytes 2359304 | tf_op jit(solution)/shard_map/ppermute | solution.py:201
  64.7 13.5 %collective-permute-start.21 = (f16[2,128,1024]{2,1,0:T(8,128)(2,1)S(1)}, f16[2,128,1024]{2,1,0:T(8,128)(2,1)S(1)}, u32[]{:S(2)}, u32[]{:S(2)}) collective-permute-start(f16[2,128,1024]{2,1,0:T(8,128)(2,1)S(1)} %multiply_convert_fusion.9), channel_id=1, source_target_pairs={{8,0},{20,28},{4,4},{12,12},{16,16},{24,24},{9,1},{21,29},{5,5},{1... | collective-permute-start | bytes 1572872 | tf_op jit(solution)/shard_map/ppermute | solution.py:201
  66.7 15.8 %collective-permute-start.20 = (f16[2,128,1536]{2,1,0:T(8,128)(2,1)S(1)}, f16[2,128,1536]{2,1,0:T(8,128)(2,1)S(1)}, u32[]{:S(2)}, u32[]{:S(2)}) collective-permute-start(f16[2,128,1536]{2,1,0:T(8,128)(2,1)S(1)} %multiply_convert_fusion.4), channel_id=1, source_target_pairs={{16,8},{12,20},{0,0},{4,4},{24,24},{28,28},{17,9},{13,21},{1,1},{5... | collective-permute-start | bytes 2359304 | tf_op jit(solution)/shard_map/ppermute | solution.py:201
  68.3 17.9 %collective-permute-start.19 = (bf16[128,1024]{1,0:T(8,128)(2,1)S(1)}, bf16[128,1024]{1,0:T(8,128)(2,1)S(1)}, u32[]{:S(2)}, u32[]{:S(2)}) collective-permute-start(bf16[128,1024]{1,0:T(8,128)(2,1)S(1)} %fusion.39), channel_id=1, source_target_pairs={{0,8},{28,20},{4,4},{12,12},{16,16},{24,24},{1,9},{29,21},{5,5},{1... | collective-permute-start | bytes 786440 | tf_op jit(solution)/shard_map/ppermute | solution.py:201
  74.9 15.9 %collective-permute-start.18 = (f16[2,128,1536]{2,1,0:T(8,128)(2,1)S(1)}, f16[2,128,1536]{2,1,0:T(8,128)(2,1)S(1)}, u32[]{:S(2)}, u32[]{:S(2)}) collective-permute-start(f16[2,128,1536]{2,1,0:T(8,128)(2,1)S(1)} %multiply_convert_fusion.3), channel_id=1, source_target_pairs={{8,0},{20,28},{4,4},{12,12},{16,16},{24,24},{9,1},{21,29},{5,5},{1... | collective-permute-start | bytes 2359304 | tf_op jit(solution)/shard_map/ppermute | solution.py:201
  76.9 17.8 %collective-permute-start.17 = (f16[2,128,1536]{2,1,0:T(8,128)(2,1)S(1)}, f16[2,128,1536]{2,1,0:T(8,128)(2,1)S(1)}, u32[]{:S(2)}, u32[]{:S(2)}) collective-permute-start(f16[2,128,1536]{2,1,0:T(8,128)(2,1)S(1)} %multiply_convert_fusion.2), channel_id=1, source_target_pairs={{16,8},{12,20},{0,0},{4,4},{24,24},{28,28},{17,9},{13,21},{1,1},{5... | collective-permute-start | bytes 2359304 | tf_op jit(solution)/shard_map/ppermute | solution.py:201
  79.5 17.8 %collective-permute-start.26 = (bf16[128,1024]{1,0:T(8,128)(2,1)S(1)}, bf16[128,1024]{1,0:T(8,128)(2,1)}, u32[]{:S(2)}, u32[]{:S(2)}) collective-permute-start(bf16[128,1024]{1,0:T(8,128)(2,1)S(1)} %fusion.37), channel_id=1, source_target_pairs={{0,8},{28,20},{4,4},{12,12},{16,16},{24,24},{1,9},{29,21},{5,5},{1... | collective-permute-start | bytes 786440 | tf_op jit(solution)/shard_map/ppermute | solution.py:201
  83.1 16.2 %collective-permute-start.25 = (f16[2,128,1536]{2,1,0:T(8,128)(2,1)S(1)}, f16[2,128,1536]{2,1,0:T(8,128)(2,1)S(1)}, u32[]{:S(2)}, u32[]{:S(2)}) collective-permute-start(f16[2,128,1536]{2,1,0:T(8,128)(2,1)S(1)} %multiply_convert_fusion.1), channel_id=1, source_target_pairs={{8,0},{20,28},{4,4},{12,12},{16,16},{24,24},{9,1},{21,29},{5,5},{1... | collective-permute-start | bytes 2359304 | tf_op jit(solution)/shard_map/ppermute | solution.py:201
  86.2 15.9 %collective-permute-start.24 = (bf16[128,1024]{1,0:T(8,128)(2,1)S(1)}, bf16[128,1024]{1,0:T(8,128)(2,1)}, u32[]{:S(2)}, u32[]{:S(2)}) collective-permute-start(bf16[128,1024]{1,0:T(8,128)(2,1)S(1)} %collective-permute-done.19), channel_id=1, source_target_pairs={{8,16},{20,12},{0,0},{4,4},{24,24},{28,28},{9,17},{21,13},{1,1},{5... | collective-permute-start | bytes 786440 | tf_op jit(solution)/shard_map/ppermute | solution.py:201
  91.3 14.4 %collective-permute-start.23 = (bf16[128,1536]{1,0:T(8,128)(2,1)S(1)}, bf16[128,1536]{1,0:T(8,128)(2,1)S(1)}, u32[]{:S(2)}, u32[]{:S(2)}) collective-permute-start(bf16[128,1536]{1,0:T(8,128)(2,1)S(1)} %fusion.35), channel_id=1, source_target_pairs={{0,8},{28,20},{4,4},{12,12},{16,16},{24,24},{1,9},{29,21},{5,5},{1... | collective-permute-start | bytes 1179656 | tf_op jit(solution)/shard_map/ppermute | solution.py:201
  95.3 13.5 %collective-permute-start.22 = (f16[2,128,1536]{2,1,0:T(8,128)(2,1)S(1)}, f16[2,128,1536]{2,1,0:T(8,128)(2,1)S(1)}, u32[]{:S(2)}, u32[]{:S(2)}) collective-permute-start(f16[2,128,1536]{2,1,0:T(8,128)(2,1)S(1)} %multiply_convert_fusion), channel_id=1, source_target_pairs={{8,0},{20,28},{4,4},{12,12},{16,16},{24,24},{9,1},{21,29},{5,5},{1... | collective-permute-start | bytes 2359304 | tf_op jit(solution)/shard_map/ppermute | solution.py:201
  97.3 14.4 %collective-permute-start.31 = (bf16[128,1024]{1,0:T(8,128)(2,1)}, bf16[128,1024]{1,0:T(8,128)(2,1)}, u32[]{:S(2)}, u32[]{:S(2)}) collective-permute-start(bf16[128,1024]{1,0:T(8,128)(2,1)} %collective-permute-done.26), channel_id=1, source_target_pairs={{8,16},{20,12},{0,0},{4,4},{24,24},{28,28},{9,17},{21,13},{1,1},{5... | collective-permute-start | bytes 786440 | tf_op jit(solution)/shard_map/ppermute | solution.py:201
  99.6 9.5 %copy-start = (f32[2,128,1536]{2,1,0:T(8,128)}, f32[2,128,1536]{2,1,0:T(8,128)S(1)}, u32[]{:S(2)}) copy-start(f32[2,128,1536]{2,1,0:T(8,128)S(1)} %fusion.15) | copy-start | bytes 4718596
  100.8 12.7 %collective-permute-start.30 = (bf16[128,1536]{1,0:T(8,128)(2,1)}, bf16[128,1536]{1,0:T(8,128)(2,1)S(1)}, u32[]{:S(2)}, u32[]{:S(2)}) collective-permute-start(bf16[128,1536]{1,0:T(8,128)(2,1)} %fusion.33), channel_id=1, source_target_pairs={{0,8},{28,20},{4,4},{12,12},{16,16},{24,24},{1,9},{29,21},{5,5},{1... | collective-permute-start | bytes 1179656 | tf_op jit(solution)/shard_map/ppermute | solution.py:201
  102.1 12.7 %collective-permute-start.29 = (bf16[128,1024]{1,0:T(8,128)(2,1)}, bf16[128,1024]{1,0:T(8,128)(2,1)}, u32[]{:S(2)}, u32[]{:S(2)}) collective-permute-start(bf16[128,1024]{1,0:T(8,128)(2,1)} %collective-permute-done.24), channel_id=1, source_target_pairs={{16,24},{12,4},{0,0},{8,8},{20,20},{28,28},{17,25},{13,5},{1,1},{9... | collective-permute-start | bytes 786440 | tf_op jit(solution)/shard_map/ppermute | solution.py:201
  105.7 10.4 %collective-permute-start.28 = (bf16[128,1536]{1,0:T(8,128)(2,1)S(1)}, bf16[128,1536]{1,0:T(8,128)(2,1)}, u32[]{:S(2)}, u32[]{:S(2)}) collective-permute-start(bf16[128,1536]{1,0:T(8,128)(2,1)S(1)} %collective-permute-done.23), channel_id=1, source_target_pairs={{8,16},{20,12},{0,0},{4,4},{24,24},{28,28},{9,17},{21,13},{1,1},{5... | collective-permute-start | bytes 1179656 | tf_op jit(solution)/shard_map/ppermute | solution.py:201
  110.4 9.2 %collective-permute-start.27 = (bf16[128,1536]{1,0:T(8,128)(2,1)}, bf16[128,1536]{1,0:T(8,128)(2,1)}, u32[]{:S(2)}, u32[]{:S(2)}) collective-permute-start(bf16[128,1536]{1,0:T(8,128)(2,1)} %fusion.31), channel_id=1, source_target_pairs={{0,8},{28,20},{4,4},{12,12},{16,16},{24,24},{1,9},{29,21},{5,5},{1... | collective-permute-start | bytes 1179656 | tf_op jit(solution)/shard_map/ppermute | solution.py:201
  111.7 10.9 %copy-start.5 = (f32[2,128,1024]{2,1,0:T(8,128)S(1)}, f32[2,128,1024]{2,1,0:T(8,128)}, u32[]{:S(2)}) copy-start(f32[2,128,1024]{2,1,0:T(8,128)} %copy-done.4) | copy-start | bytes 3145732
  111.7 10.9 %collective-permute-start.36 = (bf16[128,1024]{1,0:T(8,128)(2,1)}, bf16[128,1024]{1,0:T(8,128)(2,1)S(1)}, u32[]{:S(2)}, u32[]{:S(2)}) collective-permute-start(bf16[128,1024]{1,0:T(8,128)(2,1)} %collective-permute-done.31), channel_id=1, source_target_pairs={{16,24},{12,4},{0,0},{8,8},{20,20},{28,28},{17,25},{13,5},{1,1},{9... | collective-permute-start | bytes 786440 | tf_op jit(solution)/shard_map/ppermute | solution.py:201
  113.5 10.5 %collective-permute-start.35 = (bf16[128,1536]{1,0:T(8,128)(2,1)S(1)}, bf16[128,1536]{1,0:T(8,128)(2,1)S(1)}, u32[]{:S(2)}, u32[]{:S(2)}) collective-permute-start(bf16[128,1536]{1,0:T(8,128)(2,1)S(1)} %collective-permute-done.30), channel_id=1, source_target_pairs={{8,16},{20,12},{0,0},{4,4},{24,24},{28,28},{9,17},{21,13},{1,1},{5... | collective-permute-start | bytes 1179656 | tf_op jit(solution)/shard_map/ppermute | solution.py:201
  116.1 11.8 %collective-permute-start.33 = (bf16[128,1536]{1,0:T(8,128)(2,1)}, bf16[128,1536]{1,0:T(8,128)(2,1)S(1)}, u32[]{:S(2)}, u32[]{:S(2)}) collective-permute-start(bf16[128,1536]{1,0:T(8,128)(2,1)} %collective-permute-done.28), channel_id=1, source_target_pairs={{16,24},{12,4},{0,0},{8,8},{20,20},{28,28},{17,25},{13,5},{1,1},{9... | collective-permute-start | bytes 1179656 | tf_op jit(solution)/shard_map/ppermute | solution.py:201
  117.8 6.9 %collective-permute-start.34 = (bf16[128,1024]{1,0:T(8,128)(2,1)S(1)}, bf16[128,1024]{1,0:T(8,128)(2,1)S(1)}, u32[]{:S(2)}, u32[]{:S(2)}) collective-permute-start(bf16[128,1024]{1,0:T(8,128)(2,1)S(1)} %select_select_fusion.4.refs_0_), channel_id=1, source_target_pairs={{0,4},{4,0},{8,12},{12,8},{16,20},{20,16},{24,28},{28,24},{1,5},{5... | collective-permute-start | bytes 786440 | tf_op jit(solution)/shard_map/ppermute | solution.py:197
  119.6 10.8 %collective-permute-start.32 = (bf16[128,1536]{1,0:T(8,128)(2,1)}, bf16[128,1536]{1,0:T(8,128)(2,1)S(1)}, u32[]{:S(2)}, u32[]{:S(2)}) collective-permute-start(bf16[128,1536]{1,0:T(8,128)(2,1)} %collective-permute-done.27), channel_id=1, source_target_pairs={{8,16},{20,12},{0,0},{4,4},{24,24},{28,28},{9,17},{21,13},{1,1},{5... | collective-permute-start | bytes 1179656 | tf_op jit(solution)/shard_map/ppermute | solution.py:201
  123.9 7.3 %collective-permute-start.40 = (bf16[128,1024]{1,0:T(8,128)(2,1)S(1)}, bf16[128,1024]{1,0:T(8,128)(2,1)S(1)}, u32[]{:S(2)}, u32[]{:S(2)}) collective-permute-start(bf16[128,1024]{1,0:T(8,128)(2,1)S(1)} %select_select_fusion.3.refs_0_), channel_id=1, source_target_pairs={{0,4},{4,0},{8,12},{12,8},{16,20},{20,16},{24,28},{28,24},{1,5},{5... | collective-permute-start | bytes 786440 | tf_op jit(solution)/shard_map/ppermute | solution.py:197
  124.0 10.4 %collective-permute-start.39 = (bf16[128,1536]{1,0:T(8,128)(2,1)S(1)}, bf16[128,1536]{1,0:T(8,128)(2,1)S(1)}, u32[]{:S(2)}, u32[]{:S(2)}) collective-permute-start(bf16[128,1536]{1,0:T(8,128)(2,1)S(1)} %collective-permute-done.35), channel_id=1, source_target_pairs={{16,24},{12,4},{0,0},{8,8},{20,20},{28,28},{17,25},{13,5},{1,1},{9... | collective-permute-start | bytes 1179656 | tf_op jit(solution)/shard_map/ppermute | solution.py:201
  128.3 7.7 %collective-permute-start.38 = (bf16[128,1536]{1,0:T(8,128)(2,1)S(1)}, bf16[128,1536]{1,0:T(8,128)(2,1)S(1)}, u32[]{:S(2)}, u32[]{:S(2)}) collective-permute-start(bf16[128,1536]{1,0:T(8,128)(2,1)S(1)} %select_select_fusion.2.refs_0_), channel_id=1, source_target_pairs={{0,4},{4,0},{8,12},{12,8},{16,20},{20,16},{24,28},{28,24},{1,5},{5... | collective-permute-start | bytes 1179656 | tf_op jit(solution)/shard_map/ppermute | solution.py:197
  130.5 9.4 %collective-permute-start.37 = (bf16[128,1536]{1,0:T(8,128)(2,1)S(1)}, bf16[128,1536]{1,0:T(8,128)(2,1)S(1)}, u32[]{:S(2)}, u32[]{:S(2)}) collective-permute-start(bf16[128,1536]{1,0:T(8,128)(2,1)S(1)} %collective-permute-done.32), channel_id=1, source_target_pairs={{16,24},{12,4},{0,0},{8,8},{20,20},{28,28},{17,25},{13,5},{1,1},{9... | collective-permute-start | bytes 1179656 | tf_op jit(solution)/shard_map/ppermute | solution.py:201
  134.8 6.6 %collective-permute-start.42 = (bf16[128,1536]{1,0:T(8,128)(2,1)S(1)}, bf16[128,1536]{1,0:T(8,128)(2,1)S(1)}, u32[]{:S(2)}, u32[]{:S(2)}) collective-permute-start(bf16[128,1536]{1,0:T(8,128)(2,1)S(1)} %select_select_fusion.1.refs_0_), channel_id=1, source_target_pairs={{0,4},{4,0},{8,12},{12,8},{16,20},{20,16},{24,28},{28,24},{1,5},{5... | collective-permute-start | bytes 1179656 | tf_op jit(solution)/shard_map/ppermute | solution.py:197
  141.2 4.1 %collective-permute-start.41 = (bf16[128,1536]{1,0:T(8,128)(2,1)S(1)}, bf16[128,1536]{1,0:T(8,128)(2,1)}, u32[]{:S(2)}, u32[]{:S(2)}) collective-permute-start(bf16[128,1536]{1,0:T(8,128)(2,1)S(1)} %select_select_fusion.refs_0_), channel_id=1, source_target_pairs={{0,4},{4,0},{8,12},{12,8},{16,20},{20,16},{24,28},{28,24},{1,5},{5... | collective-permute-start | bytes 1179656 | tf_op jit(solution)/shard_map/ppermute | solution.py:197
  150.4 8.5 %collective-permute-start.45 = (bf16[64,2048]{1,0:T(8,128)(2,1)S(1)}, bf16[64,2048]{1,0:T(8,128)(2,1)S(1)}, u32[]{:S(2)}, u32[]{:S(2)}) collective-permute-start(bf16[64,2048]{1,0:T(8,128)(2,1)S(1)} %get-tuple-element.176), channel_id=1, source_target_pairs={{0,3},{1,2},{2,1},{3,0},{4,7},{5,6},{6,5},{7,4},{8,11},{9,10},{10,... | collective-permute-start | bytes 786440 | tf_op jit(solution)/shard_map/ppermute | solution.py:222
  151.8 13.5 %collective-permute-start.44 = (bf16[64,2048]{1,0:T(8,128)(2,1)S(1)}, bf16[64,2048]{1,0:T(8,128)(2,1)S(1)}, u32[]{:S(2)}, u32[]{:S(2)}) collective-permute-start(bf16[64,2048]{1,0:T(8,128)(2,1)S(1)} %get-tuple-element.177), channel_id=1, source_target_pairs={{0,2},{1,3},{2,0},{3,1},{4,6},{5,7},{6,4},{7,5},{8,10},{9,11},{10,... | collective-permute-start | bytes 786440 | tf_op jit(solution)/shard_map/ppermute | solution.py:222
  152.8 12.4 %collective-permute-start.43 = (bf16[64,2048]{1,0:T(8,128)(2,1)S(1)}, bf16[64,2048]{1,0:T(8,128)(2,1)}, u32[]{:S(2)}, u32[]{:S(2)}) collective-permute-start(bf16[64,2048]{1,0:T(8,128)(2,1)S(1)} %get-tuple-element.175), channel_id=1, source_target_pairs={{0,1},{1,0},{2,3},{3,2},{4,5},{5,4},{6,7},{7,6},{8,9},{9,8},{10,11... | collective-permute-start | bytes 786440 | tf_op jit(solution)/shard_map/ppermute | solution.py:222
  (5 other events, 18.3 us)
